TPU v7x, 32 devices: a whole 2x2x4 slice. The times are simulated.
32 devices in a mesh: dp: 16 (over z, y, x), seq: 2 (over core).
Axes of the slice: x: 2, y: 2, z: 4, core: 2. Of those that a mesh axis runs over, the one named last changes fastest.
Arguments:
- labels: int32 [32], P('dp'), may hold values from 0 to 1000
- targets: int32 [32, 256], P('dp', 'seq'), may hold values from 0 to 16383
- heights: int32 [32], P('dp'), may hold values from 8 to 16, as said below
- loss_mask: int32 [32, 256], P('dp', 'seq'), may hold values from 0 to 1
- class_table: float32 [1001, 768], P(None, ('dp', 'seq')), may hold values from -1.8 to 1.8
- code_table: float32 [16384, 768], P(('dp', 'seq')), may hold values from -1.8 to 1.8
- attend_in: float32 [768, 2304], P(('dp', 'seq')), may hold values from -0.21875 to 0.21875
- attend_mix: float32 [768, 768], P(('dp', 'seq')), may hold values from -0.625 to 0.625
- expand_in: float32 [768, 4096], P(('dp', 'seq')), may hold values from -0.21875 to 0.21875
- shrink_out: float32 [2048, 768], P(('dp', 'seq')), may hold values from -0.125 to 0.125
- head_weight: float32 [768, 16384], P(None, ('dp', 'seq')), may hold values from -0.21875 to 0.21875
- norm_gains: float32 [3, 768], P(None, ('dp', 'seq')), may hold values from 0.34 to 2.3
- drift_class: float32 [1001, 768], P(None, ('dp', 'seq')), may hold values from -1.1920929e-07 to 1.1920929e-07
- drift_code: float32 [16384, 768], P(('dp', 'seq')), may hold values from -2.9802322e-07 to 2.9802322e-07
- drift_attend: float32 [768, 2304], P(('dp', 'seq')), may hold values from -2.861023e-06 to 2.861023e-06
- drift_mix: float32 [768, 768], P(('dp', 'seq')), may hold values from -2.861023e-06 to 2.861023e-06
- drift_expand: float32 [768, 4096], P(('dp', 'seq')), may hold values from -2.861023e-06 to 2.861023e-06
- drift_shrink: float32 [2048, 768], P(('dp', 'seq')), may hold values from -2.861023e-06 to 2.861023e-06
- drift_head: float32 [768, 16384], P(None, ('dp', 'seq')), may hold values from -2.861023e-06 to 2.861023e-06
- drift_gains: float32 [3, 768], P(None, ('dp', 'seq')), may hold values from -1.1444092e-05 to 1.1444092e-05
- square_class: float32 [1001, 768], P(None, ('dp', 'seq')), may hold values from 1.4031683e-16 to 1.1204005e-15
- square_code: float32 [16384, 768], P(('dp', 'seq')), may hold values from 7.942518e-16 to 6.3419343e-15
- square_attend: float32 [768, 2304], P(('dp', 'seq')), may hold values from 7.966128e-14 to 1.2721573e-12
- square_mix: float32 [768, 768], P(('dp', 'seq')), may hold values from 7.966128e-14 to 1.2721573e-12
- square_expand: float32 [768, 4096], P(('dp', 'seq')), may hold values from 7.966128e-14 to 1.2721573e-12
- square_shrink: float32 [2048, 768], P(('dp', 'seq')), may hold values from 7.966128e-14 to 1.2721573e-12
- square_head: float32 [768, 16384], P(None, ('dp', 'seq')), may hold values from 7.966128e-14 to 1.2721573e-12
- square_gains: float32 [3, 768], P(None, ('dp', 'seq')), may hold values from 1.2721573e-12 to 2.0293938e-11
Outputs:
- class_new: float32 [1001, 768], P(None, ('dp', 'seq'))
- code_new: float32 [16384, 768], P(('dp', 'seq'))
- attend_new: float32 [768, 2304], P(('dp', 'seq'))
- mix_new: float32 [768, 768], P(('dp', 'seq'))
- expand_new: float32 [768, 4096], P(('dp', 'seq'))
- shrink_new: float32 [2048, 768], P(('dp', 'seq'))
- head_new: float32 [768, 16384], P(None, ('dp', 'seq'))
- gains_new: float32 [3, 768], P(None, ('dp', 'seq'))
- momentum_class: float32 [1001, 768], P(None, ('dp', 'seq'))
- momentum_code: float32 [16384, 768], P(('dp', 'seq'))
- momentum_attend: float32 [768, 2304], P(('dp', 'seq'))
- momentum_mix: float32 [768, 768], P(('dp', 'seq'))
- momentum_expand: float32 [768, 4096], P(('dp', 'seq'))
- momentum_shrink: float32 [2048, 768], P(('dp', 'seq'))
- momentum_head: float32 [768, 16384], P(None, ('dp', 'seq'))
- momentum_gains: float32 [3, 768], P(None, ('dp', 'seq'))
- variance_class: float32 [1001, 768], P(None, ('dp', 'seq'))
- variance_code: float32 [16384, 768], P(('dp', 'seq'))
- variance_attend: float32 [768, 2304], P(('dp', 'seq'))
- variance_mix: float32 [768, 768], P(('dp', 'seq'))
- variance_expand: float32 [768, 4096], P(('dp', 'seq'))
- variance_shrink: float32 [2048, 768], P(('dp', 'seq'))
- variance_head: float32 [768, 16384], P(None, ('dp', 'seq'))
- variance_gains: float32 [3, 768], P(None, ('dp', 'seq'))
- grad_norm: float32 [], replicated
- loss_sum: float32 [], replicated
- loss_count: float32 [], replicated
Inputs may be any that keep to these rules, and one draw needn't show every extreme that they name: `heights`: in each aligned block of 2 images (those of one index of dp) at least one image has 16 rows.
All inputs are finite; a program needn't handle non-finite values.
Results may differ from a plain program's by a relative error of at most 0.02.
The roundings to bfloat16 on the way count: a program that leaves them out, or rounds other values in their place, can miss the bound.
Values may be sent and summed in bfloat16 or wider, within the bound.
A program may use at most 320 MiB of HBM per device.

v0:
```python
import jax
import jax.numpy as jnp
from jax import lax
from jax.sharding import PartitionSpec as P

HD = 64
GRID = 16
STEP = 10


EPS_NORM = 1e-05
BETA_ONE = 0.9
BETA_TWO = 0.95
ADAM_EPS = 1e-08
CLIP_NORM = 0.01
NEGATIVE_FILL = -1000000000.0
RATES = (0.8, 0.8, 0.08, 0.08, 0.08, 0.08, 0.08, 0.8)
DECAYS = (0.1, 0.1, 0.1, 0.1, 0.1, 0.1, 0.1, 0.0)


def from_behind(value, axis, steps):
    count = lax.axis_size(axis)
    first, last = (max(0, -steps), min(count, count - steps))
    return lax.ppermute(value, axis, [(source, source + steps) for source in range(first, last)])


def matmul(left, right):
    return jnp.dot(left, right, preferred_element_type=jnp.float32)


def norm_forward(values, gain):
    inverse = lax.rsqrt(jnp.mean(values * values, axis=-1, keepdims=True) + EPS_NORM)
    normed = values * inverse
    return (normed * gain, normed, inverse)


def norm_backward(grad, normed, inverse, gain):
    scaled = grad * gain
    inner = jnp.mean(scaled * normed, axis=-1, keepdims=True)
    return (inverse * (scaled - normed * inner), jnp.sum(grad * normed, axis=0))


def turn_half(tensor):
    quarter = tensor.shape[-1] // 4
    return jnp.concatenate(
        [
            -tensor[..., quarter : 2 * quarter],
            tensor[..., :quarter],
            -tensor[..., 3 * quarter :],
            tensor[..., 2 * quarter : 3 * quarter],
        ],
        axis=-1,
    )


def rope_tables(positions, width):
    quarter = width // 4
    freq = 10000.0 ** (-jnp.arange(quarter, dtype=jnp.float32) / quarter)
    row_angle = (positions // GRID).astype(jnp.float32)[:, None] * freq
    col_angle = (positions % GRID).astype(jnp.float32)[:, None] * freq
    angles = jnp.concatenate([row_angle, row_angle, col_angle, col_angle], axis=-1)
    return (jnp.cos(angles), jnp.sin(angles))


def rotate(tensor, cosine, sine):
    return tensor * cosine[None, :, None, :] + turn_half(tensor) * sine[None, :, None, :]


def rotate_back(grad, cosine, sine):
    return grad * cosine[None, :, None, :] - turn_half(grad * sine[None, :, None, :])


def split_heads(heads):
    parts = heads.reshape(heads.shape[0], heads.shape[1], 3, -1, HD)
    return (parts[:, :, 0], parts[:, :, 1], parts[:, :, 2])


def masked_scores(query, keys, lengths):
    length = query.shape[1]
    scores = jnp.einsum(
        "bqhd,bkhd->bhqk", query, keys, preferred_element_type=jnp.float32
    ) * HD ** (-0.5)
    places = jnp.arange(length)
    allowed = (places[None, :] <= places[:, None])[None, None] & (
        places[None, :] < lengths[:, None]
    )[:, None, None, :]
    return jnp.where(allowed, scores, NEGATIVE_FILL)


def attend(heads, lengths):
    query, keys, values = split_heads(heads)
    scores = masked_scores(query, keys, lengths)
    score_peak = jnp.max(scores, axis=-1, keepdims=True)
    exponent = jnp.exp(scores - score_peak)
    score_total = jnp.sum(exponent, axis=-1, keepdims=True)
    probs = (exponent / score_total).astype(jnp.bfloat16)
    output = jnp.einsum("bhqk,bkhd->bqhd", probs, values, preferred_element_type=jnp.float32)
    output = output.astype(jnp.bfloat16).reshape(heads.shape[0], heads.shape[1], 1, -1)
    return (output, score_peak[..., 0] + jnp.log(score_total[..., 0]))


def attend_back(heads, log_total, grad_out, lengths):
    query, keys, values = split_heads(heads)
    grad_heads = grad_out.reshape(heads.shape[0], heads.shape[1], -1, HD)
    probs = jnp.exp(masked_scores(query, keys, lengths) - log_total[..., None])
    grad_probs = jnp.einsum(
        "bqhd,bkhd->bhqk", grad_heads, values, preferred_element_type=jnp.float32
    )
    grad_scores = probs * (grad_probs - jnp.sum(probs * grad_probs, axis=-1, keepdims=True))
    grad_scores = grad_scores.astype(jnp.bfloat16)
    grad_query = jnp.einsum(
        "bhqk,bkhd->bqhd", grad_scores, keys, preferred_element_type=jnp.float32
    ) * HD ** (-0.5)
    grad_keys = jnp.einsum(
        "bhqk,bqhd->bkhd", grad_scores, query, preferred_element_type=jnp.float32
    ) * HD ** (-0.5)
    grad_values = jnp.einsum(
        "bhqk,bqhd->bkhd",
        probs.astype(jnp.bfloat16),
        grad_heads,
        preferred_element_type=jnp.float32,
    )
    stacked = jnp.stack([grad_query, grad_keys, grad_values], axis=2).astype(jnp.bfloat16)
    return stacked.reshape(heads.shape[0], heads.shape[1], 3, 1, -1)


def layer_forward(start, gain, weights, lengths, turning):
    qkv_w, mix_w, expand_w, shrink_w = weights
    cosine, sine = turning
    images, local_len = (lengths.shape[0], cosine.shape[0])
    groups = lax.axis_size("seq")
    normed_one, norm_one, inverse_one = norm_forward(start, gain[0])
    normed_one = normed_one.astype(jnp.bfloat16)
    mixed = matmul(normed_one, qkv_w).reshape(images, local_len, 3, -1, HD)
    query = rotate(mixed[:, :, 0], cosine, sine)
    keys = rotate(mixed[:, :, 1], cosine, sine)
    packed = jnp.stack([query, keys, mixed[:, :, 2]], axis=2).astype(jnp.bfloat16)
    packed = packed.reshape(images, local_len, 3, groups, -1)
    heads = lax.all_to_all(packed, "seq", split_axis=3, concat_axis=1, tiled=True)
    output, log_total = attend(heads, lengths)
    attended = lax.all_to_all(output, "seq", split_axis=1, concat_axis=2, tiled=True).reshape(
        images * local_len, -1
    )
    middle = start + matmul(attended, mix_w)
    normed_two, norm_two, inverse_two = norm_forward(middle, gain[1])
    normed_two = normed_two.astype(jnp.bfloat16)
    both = matmul(normed_two, expand_w)
    width = both.shape[1] // 2
    gate_part, up_part = (both[:, :width], both[:, width:])
    hidden = (jax.nn.silu(gate_part) * up_part).astype(jnp.bfloat16)
    final = middle + matmul(hidden, shrink_w)
    saved = (
        norm_one,
        inverse_one,
        normed_one,
        heads,
        log_total,
        attended,
        norm_two,
        inverse_two,
        normed_two,
        gate_part,
        up_part,
        hidden,
    )
    return (final, saved)


def layer_backward(grad_final, saved, gain, weights, lengths, turning):
    qkv_w, mix_w, expand_w, shrink_w = weights
    cosine, sine = turning
    (
        norm_one,
        inverse_one,
        normed_one,
        heads,
        log_total,
        attended,
        norm_two,
        inverse_two,
        normed_two,
        gate_part,
        up_part,
        hidden,
    ) = saved
    images, local_len = (lengths.shape[0], cosine.shape[0])
    groups = lax.axis_size("seq")
    back_down = grad_final.astype(jnp.bfloat16)
    grad_shrink = matmul(hidden.T, back_down)
    grad_hidden = matmul(back_down, shrink_w.T)
    sigma = jax.nn.sigmoid(gate_part)
    grad_gate = grad_hidden * up_part * sigma * (1.0 + gate_part * (1.0 - sigma))
    grad_up = grad_hidden * gate_part * sigma
    grad_both = jnp.concatenate([grad_gate, grad_up], axis=1).astype(jnp.bfloat16)
    grad_expand = matmul(normed_two.T, grad_both)
    grad_norm_two, gain_two = norm_backward(
        matmul(grad_both, expand_w.T), norm_two, inverse_two, gain[1]
    )
    grad_middle = grad_final + grad_norm_two
    back_mix = grad_middle.astype(jnp.bfloat16)
    grad_mix = matmul(attended.T, back_mix)
    grad_attended = (
        matmul(back_mix, mix_w.T).astype(jnp.bfloat16).reshape(images, local_len, groups, -1)
    )
    grad_output = lax.all_to_all(grad_attended, "seq", split_axis=2, concat_axis=1, tiled=True)
    grad_heads = attend_back(heads, log_total, grad_output, lengths)
    grad_parts = lax.all_to_all(grad_heads, "seq", split_axis=1, concat_axis=3, tiled=True).reshape(
        images, local_len, 3, -1, HD
    )
    grad_query = rotate_back(grad_parts[:, :, 0].astype(jnp.float32), cosine, sine)
    grad_keys = rotate_back(grad_parts[:, :, 1].astype(jnp.float32), cosine, sine)
    grad_mixed = jnp.stack([grad_query, grad_keys, grad_parts[:, :, 2].astype(jnp.float32)], axis=2)
    grad_mixed = grad_mixed.astype(jnp.bfloat16).reshape(images * local_len, -1)
    grad_qkv = matmul(normed_one.T, grad_mixed)
    grad_norm_one, gain_one = norm_backward(
        matmul(grad_mixed, qkv_w.T), norm_one, inverse_one, gain[0]
    )
    grad_start = grad_middle + grad_norm_one
    return (grad_start, (grad_qkv, grad_mix, grad_expand, grad_shrink), (gain_one, gain_two))


def adam_update(master, drift, square, grad, rate, decay):
    moment = BETA_ONE * drift + (1.0 - BETA_ONE) * grad
    second = BETA_TWO * square + (1.0 - BETA_TWO) * grad * grad
    stride = (
        moment / (1.0 - BETA_ONE**STEP) / (jnp.sqrt(second / (1.0 - BETA_TWO**STEP)) + ADAM_EPS)
    )
    return (master - rate * (stride + decay * master), moment, second)


def on_device(
    labels,
    targets,
    heights,
    loss_mask,
    class_table,
    code_table,
    attend_in,
    attend_mix,
    expand_in,
    shrink_out,
    head_weight,
    norm_gains,
    drift_class,
    drift_code,
    drift_attend,
    drift_mix,
    drift_expand,
    drift_shrink,
    drift_head,
    drift_gains,
    square_class,
    square_code,
    square_attend,
    square_mix,
    square_expand,
    square_shrink,
    square_head,
    square_gains,
):
    masters = (
        class_table,
        code_table,
        attend_in,
        attend_mix,
        expand_in,
        shrink_out,
        head_weight,
        norm_gains,
    )
    drifts = (
        drift_class,
        drift_code,
        drift_attend,
        drift_mix,
        drift_expand,
        drift_shrink,
        drift_head,
        drift_gains,
    )
    squares = (
        square_class,
        square_code,
        square_attend,
        square_mix,
        square_expand,
        square_shrink,
        square_head,
        square_gains,
    )
    gathered = (
        lax.all_gather(class_table.astype(jnp.bfloat16), ("dp", "seq"), axis=1, tiled=True),
        lax.all_gather(code_table.astype(jnp.bfloat16), ("dp", "seq"), axis=0, tiled=True),
        lax.all_gather(attend_in.astype(jnp.bfloat16), ("dp", "seq"), axis=0, tiled=True),
        lax.all_gather(attend_mix.astype(jnp.bfloat16), ("dp", "seq"), axis=0, tiled=True),
        lax.all_gather(expand_in.astype(jnp.bfloat16), ("dp", "seq"), axis=0, tiled=True),
        lax.all_gather(shrink_out.astype(jnp.bfloat16), ("dp", "seq"), axis=0, tiled=True),
        lax.all_gather(head_weight.astype(jnp.bfloat16), ("dp", "seq"), axis=1, tiled=True),
        lax.all_gather(norm_gains.astype(jnp.bfloat16), ("dp", "seq"), axis=1, tiled=True),
    )
    class_full, code_full, qkv_full, mix_full, expand_full, shrink_full, head_full, gains_full = (
        gathered
    )
    weights = (qkv_full, mix_full, expand_full, shrink_full)
    gain = gains_full.astype(jnp.float32)
    images, local_len = targets.shape
    positions = lax.axis_index("seq") * local_len + jnp.arange(local_len)
    previous = from_behind(targets[:, local_len - 1 :], "seq", 1)
    codes = jnp.concatenate([previous, targets[:, : local_len - 1]], axis=1)
    opening = (positions == 0)[None, :, None]
    code_rows = jnp.take(code_full, codes, axis=0)
    class_rows = jnp.take(class_full, labels, axis=0)[:, None, :]
    start = (
        jnp.where(opening, class_rows, code_rows)
        .astype(jnp.float32)
        .reshape(images * local_len, -1)
    )
    lengths = GRID * heights
    counted = (loss_mask * (positions[None, :] < lengths[:, None])).astype(jnp.float32).reshape(-1)
    turning = rope_tables(positions, HD)
    final, saved = layer_forward(start, gain, weights, lengths, turning)
    normed_top, norm_top, inverse_top = norm_forward(final, gain[2])
    normed_top = normed_top.astype(jnp.bfloat16)
    logits = matmul(normed_top, head_full)
    logit_peak = jnp.max(logits, axis=1, keepdims=True)
    exponent = jnp.exp(logits - logit_peak)
    logit_total = jnp.sum(exponent, axis=1, keepdims=True)
    log_total = logit_peak + jnp.log(logit_total)
    flat_targets = targets.reshape(-1, 1)
    picked = jnp.take_along_axis(logits, flat_targets, axis=1)
    loss_local = jnp.sum((log_total - picked)[:, 0] * counted)
    count_local = jnp.sum(counted)
    onehot = (jnp.arange(logits.shape[1])[None, :] == flat_targets).astype(jnp.float32)
    grad_logits = ((exponent / logit_total - onehot) * counted[:, None]).astype(jnp.bfloat16)
    grad_head = matmul(normed_top.T, grad_logits)
    grad_final, gain_top = norm_backward(
        matmul(grad_logits, head_full.T), norm_top, inverse_top, gain[2]
    )
    saved = layer_forward(start, gain, weights, lengths, turning)[1]
    grad_start, grad_layer, gain_layer = layer_backward(
        grad_final, saved, gain, weights, lengths, turning
    )
    grad_rows = grad_start.reshape(images, local_len, -1)
    code_part = jnp.where(opening, 0.0, grad_rows).reshape(images * local_len, -1)
    grad_code = jnp.zeros(code_full.shape, jnp.float32).at[codes.reshape(-1)].add(code_part)
    class_part = jnp.where(positions[0] == 0, grad_rows[:, 0, :], 0.0)
    grad_class = jnp.zeros(class_full.shape, jnp.float32).at[labels].add(class_part)
    grad_gains = jnp.stack([gain_layer[0], gain_layer[1], gain_top])
    shares = (
        lax.psum_scatter(grad_class, ("dp", "seq"), scatter_dimension=1, tiled=True),
        lax.psum_scatter(grad_code, ("dp", "seq"), scatter_dimension=0, tiled=True),
        lax.psum_scatter(grad_layer[0], ("dp", "seq"), scatter_dimension=0, tiled=True),
        lax.psum_scatter(grad_layer[1], ("dp", "seq"), scatter_dimension=0, tiled=True),
        lax.psum_scatter(grad_layer[2], ("dp", "seq"), scatter_dimension=0, tiled=True),
        lax.psum_scatter(grad_layer[3], ("dp", "seq"), scatter_dimension=0, tiled=True),
        lax.psum_scatter(grad_head, ("dp", "seq"), scatter_dimension=1, tiled=True),
        lax.psum_scatter(grad_gains, ("dp", "seq"), scatter_dimension=1, tiled=True),
    )
    square_local = sum((jnp.sum(member * member) for member in shares))
    total_square, loss_sum, loss_count = lax.psum(
        (square_local, loss_local, count_local), ("dp", "seq")
    )
    grad_norm = jnp.sqrt(total_square) / loss_count
    factor = CLIP_NORM / jnp.maximum(grad_norm, CLIP_NORM) / loss_count
    news, firsts, seconds = ([], [], [])
    for member in range(8):
        fresh, moment, second = adam_update(
            masters[member],
            drifts[member],
            squares[member],
            shares[member] * factor,
            RATES[member],
            DECAYS[member],
        )
        news.append(fresh)
        firsts.append(moment)
        seconds.append(second)
    return tuple(news) + tuple(firsts) + tuple(seconds) + (grad_norm, loss_sum, loss_count)


def solution(mesh):
    placed = (
        P("dp"),
        P("dp", "seq"),
        P("dp"),
        P("dp", "seq"),
        P(None, ("dp", "seq")),
        P(("dp", "seq"), None),
        P(("dp", "seq"), None),
        P(("dp", "seq"), None),
        P(("dp", "seq"), None),
        P(("dp", "seq"), None),
        P(None, ("dp", "seq")),
        P(None, ("dp", "seq")),
        P(None, ("dp", "seq")),
        P(("dp", "seq"), None),
        P(("dp", "seq"), None),
        P(("dp", "seq"), None),
        P(("dp", "seq"), None),
        P(("dp", "seq"), None),
        P(None, ("dp", "seq")),
        P(None, ("dp", "seq")),
        P(None, ("dp", "seq")),
        P(("dp", "seq"), None),
        P(("dp", "seq"), None),
        P(("dp", "seq"), None),
        P(("dp", "seq"), None),
        P(("dp", "seq"), None),
        P(None, ("dp", "seq")),
        P(None, ("dp", "seq")),
    )
    return jax.shard_map(
        on_device,
        mesh=mesh,
        in_specs=placed,
        out_specs=(
            P(None, ("dp", "seq")),
            P(("dp", "seq"), None),
            P(("dp", "seq"), None),
            P(("dp", "seq"), None),
            P(("dp", "seq"), None),
            P(("dp", "seq"), None),
            P(None, ("dp", "seq")),
            P(None, ("dp", "seq")),
            P(None, ("dp", "seq")),
            P(("dp", "seq"), None),
            P(("dp", "seq"), None),
            P(("dp", "seq"), None),
            P(("dp", "seq"), None),
            P(("dp", "seq"), None),
            P(None, ("dp", "seq")),
            P(None, ("dp", "seq")),
            P(None, ("dp", "seq")),
            P(("dp", "seq"), None),
            P(("dp", "seq"), None),
            P(("dp", "seq"), None),
            P(("dp", "seq"), None),
            P(("dp", "seq"), None),
            P(None, ("dp", "seq")),
            P(None, ("dp", "seq")),
            P(),
            P(),
            P(),
        ),
        check_vma=False,
    )
```

profile of v0, /device:TPU:0, one launch (start us, length us, event | category | flops | bytes accessed | tf_op | source)
XLA Modules:
  0.0 2281.2 jit_solution(8389376737609976683)
XLA Ops:
  18.9 42.7 %all-gather = bf16[32,24,3]{1,2,0:T(4,128)(2,1)S(1)} all-gather(bf16[1,24,3]{1,2,0:T(4,128)(2,1)S(1)} %convert_bitcast_fusion.2), channel_id=1, replica_groups=mesh['dp'=16,'seq'=2] {'dp','seq'}, dimensions={0}, use_global_device_ids=true | all-gather | bytes 4752 | tf_op jit(solution)/shard_map/all_gather | solution.py:299
  71.8 59.8 %all-gather.13.cloned.1.call-done = bf16[768,2304]{1,0:T(8,128)(2,1)} async-done(((bf16[24,2304]{1,0:T(8,128)(2,1)}), bf16[768,2304]{1,0:T(8,128)(2,1)}) %all-gather.13.cloned.1.call-update) | async-done | bytes 3538960 | tf_op jit(solution)/shard_map/all_gather | solution.py:294
  131.6 4.5 copy.189
  136.1 152.4 %all-gather.11.cloned.1.call-done = bf16[16384,768]{1,0:T(8,128)(2,1)} async-done(((bf16[512,768]{1,0:T(8,128)(2,1)}), bf16[16384,768]{1,0:T(8,128)(2,1)}) %all-gather.11.cloned.1.call-update) | async-done | bytes 25165840 | tf_op jit(solution)/shard_map/all_gather | solution.py:293
  288.5 13.7 gather_fusion.1
  308.0 4.9 all_to_all.70
  323.1 5.1 all_to_all.71
  331.0 13.0 all-gather.15.cloned.1.call-done
  346.9 68.9 %all-gather.17.cloned.1.call-done = bf16[768,4096]{1,0:T(8,128)(2,1)} async-done(((bf16[24,4096]{1,0:T(8,128)(2,1)}), bf16[768,4096]{1,0:T(8,128)(2,1)}) %all-gather.17.cloned.1.call-update) | async-done | bytes 6291472 | tf_op jit(solution)/shard_map/all_gather | solution.py:296
  415.8 4.9 fusion.92
  424.4 52.2 %all-gather.19.cloned.1.call-done = bf16[2048,768]{1,0:T(8,128)(2,1)} async-done(((bf16[64,768]{1,0:T(8,128)(2,1)}), bf16[2048,768]{1,0:T(8,128)(2,1)}) %all-gather.19.cloned.1.call-update) | async-done | bytes 3145744 | tf_op jit(solution)/shard_map/all_gather | solution.py:297
  476.6 4.3 multiply_reduce_fusion.7
  481.5 169.0 %all-gather.21.cloned.1.call-done = bf16[768,16384]{1,0:T(8,128)(2,1)} async-done(((bf16[768,512]{1,0:T(8,128)(2,1)}), bf16[768,16384]{1,0:T(8,128)(2,1)}) %all-gather.21.cloned.1.call-update) | async-done | bytes 25165840 | tf_op jit(solution)/shard_map/all_gather | solution.py:298
  650.5 15.1 fusion.106
  669.1 8.2 fusion.2
  678.0 11.0 multiply_convert_fusion
  689.0 16.5 multiply_reduce_fusion.3
  707.2 4.9 multiply_convert_fusion.3
  721.7 4.0 all_to_all.72
  741.3 4.7 all_to_all.73
  763.3 4.0 fusion.21
  769.1 6.4 fusion.13
  776.7 22.5 scatter_custom_fusion.1
  800.3 23.0 %fusion.93 = f32[768,16384]{1,0:T(8,128)} fusion(bf16[256,16384]{1,0:T(8,128)(2,1)} %multiply_convert_fusion, f32[256,768]{1,0:T(8,128)S(1)} %copy-done.6, f32[768]{0:T(1024)S(1)} %get-tuple-element.141, f32[256]{0:T(256)S(1)} %add_rsqrt_fusion), kind=kOutput, calls=%fused_computation.243 | convolution fusion | flops 6443040768 | bytes 59510784 | tf_op jit(solution)/shard_map/dot_general | solution.py:28
  824.0 38.6 %all-reduce = f32[3,768]{1,0:T(4,128)S(1)} all-reduce(f32[3,768]{1,0:T(4,128)S(1)} %pad_maximum_fusion.6), channel_id=9, replica_groups=mesh['dp'=16,'seq'=2] {'dp','seq'}, use_global_device_ids=true, to_apply=%region_30.31.clone | all-reduce | flops 2304 | bytes 18432
  864.9 67.5 %reduce-scatter.23.cloned.1.call-done = f32[24,1001]{1,0:T(8,128)} async-done(((f32[768,1001]{1,0:T(8,128)}), f32[24,1001]{1,0:T(8,128)}) %reduce-scatter.23.cloned.1.call-update) | async-done | bytes 96112
  934.3 118.2 %reduce-scatter.19.cloned.1.call-done = f32[64,768]{1,0:T(8,128)} async-done(((f32[2048,768]{1,0:T(8,128)}), f32[64,768]{1,0:T(8,128)}) %reduce-scatter.19.cloned.1.call-update) | async-done | bytes 196624 | tf_op jit(solution)/shard_map/reduce_scatter | solution.py:355
  1054.0 122.5 %reduce-scatter.13.cloned.1.call-done = f32[24,2304]{1,0:T(8,128)} async-done(((f32[768,2304]{1,0:T(8,128)}), f32[24,2304]{1,0:T(8,128)}) %reduce-scatter.13.cloned.1.call-update) | async-done | bytes 221200 | tf_op jit(solution)/shard_map/reduce_scatter | solution.py:352
  1178.1 160.0 %reduce-scatter.17.cloned.1.call-done = f32[24,4096]{1,0:T(8,128)} async-done(((f32[768,4096]{1,0:T(8,128)}), f32[24,4096]{1,0:T(8,128)}) %reduce-scatter.17.cloned.1.call-update) | async-done | bytes 393232 | tf_op jit(solution)/shard_map/reduce_scatter | solution.py:354
  1339.8 435.4 %reduce-scatter.11.cloned.1.call-done = f32[512,768]{1,0:T(8,128)} async-done(((f32[16384,768]{1,0:T(8,128)}), f32[512,768]{1,0:T(8,128)}) %reduce-scatter.11.cloned.1.call-update) | async-done | bytes 1572880 | tf_op jit(solution)/shard_map/reduce_scatter | solution.py:351
  1781.7 429.4 %reduce-scatter.21.cloned.1.call-done = f32[768,512]{1,0:T(8,128)} async-done(((f32[768,16384]{1,0:T(8,128)}), f32[768,512]{1,0:T(8,128)}) %reduce-scatter.21.cloned.1.call-update) | async-done | bytes 1572880 | tf_op jit(solution)/shard_map/reduce_scatter | solution.py:356
  2214.8 39.4 %all-reduce.1 = (f32[]{:T(128)}, f32[]{:T(128)}, f32[]{:T(128)}) all-reduce(f32[]{:T(128)S(6)} %add.385, f32[]{:T(128)} %get-tuple-element.145, f32[]{:T(128)} %get-tuple-element.144), channel_id=1, replica_groups=mesh['dp'=16,'seq'=2] {'dp','seq'}, use_global_device_ids=true, to_apply=%region_32.33 | all-reduce | flops 3 | bytes 24 | tf_op jit(solution)/shard_map/psum | solution.py:360
  (324 shorter events, 130.4 us)
Async XLA Ops:
  7.2 62.0 %all-gather.9.cloned.1.call-start = ((), (), s32[]{:S(2)}) async-start(), calls=%async_computation.11 | async-start | bytes 1622016 | tf_op jit(solution)/shard_map/all_gather | solution.py:292
  8.9 122.7 %all-gather.13.cloned.1.call-start = ((), (), s32[]{:S(2)}) async-start(), calls=%async_computation.13 | async-start | bytes 3649536 | tf_op jit(solution)/shard_map/all_gather | solution.py:294
  10.6 278.0 %all-gather.11.cloned.1.call-start = ((), (), s32[]{:S(2)}) async-start(), calls=%async_computation.12 | async-start | bytes 25952256 | tf_op jit(solution)/shard_map/all_gather | solution.py:293
  13.1 331.0 %all-gather.15.cloned.1.call-start = ((), (), s32[]{:S(2)}) async-start(), calls=%async_computation.14 | async-start | bytes 1216512 | tf_op jit(solution)/shard_map/all_gather | solution.py:295
  13.8 402.0 %all-gather.17.cloned.1.call-start = ((), (), s32[]{:S(2)}) async-start(), calls=%async_computation.15 | async-start | bytes 6488064 | tf_op jit(solution)/shard_map/all_gather | solution.py:296
  14.6 49.8 %copy-start.81 = (s32[2]{0:T(128)S(1)}, s32[2]{0:T(128)}, u32[]{:S(2)}) copy-start(s32[2]{0:T(128)} %param.30) | copy-start | bytes 28
  14.6 462.0 %all-gather.19.cloned.1.call-start = ((), (), s32[]{:S(2)}) async-start(), calls=%async_computation.16 | async-start | bytes 3244032 | tf_op jit(solution)/shard_map/all_gather | solution.py:297
  15.4 635.2 %all-gather.21.cloned.1.call-start = ((), (), s32[]{:S(2)}) async-start(), calls=%async_computation.17 | async-start | bytes 25952256 | tf_op jit(solution)/shard_map/all_gather | solution.py:298
  16.4 846.9 %reduce-scatter.15.cloned.1.call-start = ((), (), s32[]{:S(2)}) async-start(), calls=%async_computation.20 | async-start | bytes 2433024 | tf_op jit(solution)/shard_map/reduce_scatter | solution.py:353
  16.6 48.8 %collective-permute-start = (s32[2,1]{1,0:T(2,128)S(1)}, s32[2,1]{1,0:T(2,128)S(1)}, u32[]{:S(2)}, u32[]{:S(2)}) collective-permute-start(s32[2,1]{1,0:T(2,128)S(1)} %slice.128), channel_id=1, source_target_pairs={{0,1},{2,3},{4,5},{6,7},{8,9},{10,11},{12,13},{14,15},{16,17},{18,... | collective-permute-start | bytes 32 | tf_op jit(solution)/shard_map/ppermute | solution.py:24
  64.5 67.2 %copy-start.78 = (s32[2]{0:T(128)}, s32[2]{0:T(128)S(1)}, u32[]{:S(2)}) copy-start(s32[2]{0:T(128)S(1)} %broadcast_multiply_fusion.5) | copy-start | bytes 28
  346.9 367.8 %copy-start.60 = (f32[256]{0:T(256)}, f32[256]{0:T(256)S(1)}, u32[]{:S(2)}) copy-start(f32[256]{0:T(256)S(1)} %add_rsqrt_fusion.1) | copy-start | bytes 3076
  424.4 56.5 %copy-start.57 = (f32[2,6,256]{2,1,0:T(8,128)S(1)}, f32[2,6,256]{2,1,0:T(8,128)}, u32[]{:S(2)}) copy-start(f32[2,6,256]{2,1,0:T(8,128)} %copy-done.56) | copy-start | bytes 36868
  424.4 56.5 %copy-start.59 = (f32[2,6,256]{2,1,0:T(8,128)S(1)}, f32[2,6,256]{2,1,0:T(8,128)}, u32[]{:S(2)}) copy-start(f32[2,6,256]{2,1,0:T(8,128)} %copy-done.58) | copy-start | bytes 36868
  728.1 204.3 %reduce-scatter.23.cloned.1.call-start = ((), (), s32[]{:S(2)}) async-start(), calls=%async_computation.24 | async-start | bytes 3244032
  756.8 295.6 %reduce-scatter.19.cloned.1.call-start = ((), (), s32[]{:S(2)}) async-start(), calls=%async_computation.22 | async-start | bytes 6488064 | tf_op jit(solution)/shard_map/reduce_scatter | solution.py:355
  761.9 414.5 %reduce-scatter.13.cloned.1.call-start = ((), (), s32[]{:S(2)}) async-start(), calls=%async_computation.19 | async-start | bytes 7299072 | tf_op jit(solution)/shard_map/reduce_scatter | solution.py:352
  767.3 570.7 %reduce-scatter.17.cloned.1.call-start = ((), (), s32[]{:S(2)}) async-start(), calls=%async_computation.21 | async-start | bytes 12976128 | tf_op jit(solution)/shard_map/reduce_scatter | solution.py:354
  775.5 999.7 %reduce-scatter.11.cloned.1.call-start = ((), (), s32[]{:S(2)}) async-start(), calls=%async_computation.18 | async-start | bytes 51904512 | tf_op jit(solution)/shard_map/reduce_scatter | solution.py:351
  799.2 1411.9 %reduce-scatter.21.cloned.1.call-start = ((), (), s32[]{:S(2)}) async-start(), calls=%async_computation.23 | async-start | bytes 51904512 | tf_op jit(solution)/shard_map/reduce_scatter | solution.py:356
  934.2 1322.1 %copy-start.66 = (f32[3,24]{1,0:T(4,128)S(1)}, f32[3,24]{1,0:T(4,128)}, u32[]{:S(2)}) copy-start(f32[3,24]{1,0:T(4,128)} %param.39) | copy-start | bytes 868
  934.2 1323.6 %copy-start.50 = (f32[24,768]{1,0:T(8,128)S(1)}, f32[24,768]{1,0:T(8,128)}, u32[]{:S(2)}) copy-start(f32[24,768]{1,0:T(8,128)} %param.35) | copy-start | bytes 221188
  934.2 1323.6 %copy-start.51 = (f32[24,768]{1,0:T(8,128)S(1)}, f32[24,768]{1,0:T(8,128)}, u32[]{:S(2)}) copy-start(f32[24,768]{1,0:T(8,128)} %reduce-scatter.15.cloned.1.call-done) | copy-start | bytes 221188
  1178.1 1081.4 %copy-start.41 = (f32[24,1001]{1,0:T(8,128)S(1)}, f32[24,1001]{1,0:T(8,128)}, u32[]{:S(2)}) copy-start(f32[24,1001]{1,0:T(8,128)} %reduce-scatter.23.cloned.1.call-done) | copy-start | bytes 288292
  1178.1 1081.4 %copy-start.42 = (f32[1001,24]{0,1:T(8,128)S(1)}, f32[1001,24]{0,1:T(8,128)}, u32[]{:S(2)}) copy-start(f32[1001,24]{0,1:T(8,128)} %param.32) | copy-start | bytes 288292
  1339.8 921.4 %copy-start.39 = (f32[64,768]{1,0:T(8,128)S(1)}, f32[64,768]{1,0:T(8,128)}, u32[]{:S(2)}) copy-start(f32[64,768]{1,0:T(8,128)} %param.37) | copy-start | bytes 589828
  1339.8 921.4 %copy-start.40 = (f32[64,768]{1,0:T(8,128)S(1)}, f32[64,768]{1,0:T(8,128)}, u32[]{:S(2)}) copy-start(f32[64,768]{1,0:T(8,128)} %reduce-scatter.19.cloned.1.call-done) | copy-start | bytes 589828
  1775.2 490.3 %copy-start.29 = (f32[768,512]{1,0:T(8,128)S(1)}, f32[768,512]{1,0:T(8,128)}, u32[]{:S(2)}) copy-start(f32[768,512]{1,0:T(8,128)} %param.54) | copy-start | bytes 4718596
  1781.6 481.6 %copy-start.36 = (f32[24,2304]{1,0:T(8,128)S(1)}, f32[24,2304]{1,0:T(8,128)}, u32[]{:S(2)}) copy-start(f32[24,2304]{1,0:T(8,128)} %reduce-scatter.13.cloned.1.call-done) | copy-start | bytes 663556
  1781.6 481.6 %copy-start.37 = (f32[24,2304]{1,0:T(8,128)S(1)}, f32[24,2304]{1,0:T(8,128)}, u32[]{:S(2)}) copy-start(f32[24,2304]{1,0:T(8,128)} %param.34) | copy-start | bytes 663556
  2213.5 50.8 %copy-start.26 = (f32[24,4096]{1,0:T(8,128)S(1)}, f32[24,4096]{1,0:T(8,128)}, u32[]{:S(2)}) copy-start(f32[24,4096]{1,0:T(8,128)} %param.36) | copy-start | bytes 1179652
  2213.5 50.8 %copy-start.27 = (f32[24,4096]{1,0:T(8,128)S(1)}, f32[24,4096]{1,0:T(8,128)}, u32[]{:S(2)}) copy-start(f32[24,4096]{1,0:T(8,128)} %reduce-scatter.17.cloned.1.call-done) | copy-start | bytes 1179652
  (67 other events, 254.4 us)
Sparse Core Ops, SparseCore 0:
  11.5 57.6 all-gather.8
  72.6 58.9 all-gather.12
  135.1 153.4 all-gather.10
  291.8 52.2 all-gather.14
  347.4 68.4 all-gather.16
  419.1 57.4 all-gather.18
  480.1 170.4 all-gather.20
  728.2 97.2 reduce-scatter.14
  831.8 100.5 reduce-scatter.22
  938.8 113.5 reduce-scatter.18
  1058.1 118.3 reduce-scatter.12
  1183.4 154.6 reduce-scatter.16
  1344.5 430.6 reduce-scatter.10
  1781.5 429.5 reduce-scatter.20
where the time goes:
time: 2290 us; the launch traced here: 2280 us
  waiting for transfers between devices  1850 us (81%)
  blocking collectives  139 us (6%)
  matrix products  106 us (5%)
  other arithmetic  98.4 us (4%)
  local copies, waits for them, and re-layouts  59.7 us (3%)
  between operations  23.9 us (1%)
    reduce_scatter x1, waiting for transfers between devices, on_device(): lax.psum_scatter(grad_code, ('dp', 'seq'), scatter_dimension=0, tiled=True)  435 us
    reduce_scatter x1, waiting for transfers between devices, on_device(): lax.psum_scatter(grad_head, ('dp', 'seq'), scatter_dimension=1, tiled=True)  429 us
    all_gather x1, waiting for transfers between devices, on_device(): lax.all_gather(head_weight.astype(jnp.bfloat16), ('dp', 'seq'), axis=1, t...  169 us
    reduce_scatter x1, waiting for transfers between devices, on_device(): lax.psum_scatter(grad_layer[2], ('dp', 'seq'), scatter_dimension=0, tiled...  160 us
    all_gather x1, waiting for transfers between devices, on_device(): lax.all_gather(code_table.astype(jnp.bfloat16), ('dp', 'seq'), axis=0, ti...  152 us
    reduce_scatter x1, waiting for transfers between devices, on_device(): lax.psum_scatter(grad_layer[0], ('dp', 'seq'), scatter_dimension=0, tiled...  122 us
    reduce_scatter x1, waiting for transfers between devices, on_device(): lax.psum_scatter(grad_layer[3], ('dp', 'seq'), scatter_dimension=0, tiled...  118 us
    dot_general x15, matrix products, matmul(): return jnp.dot(left, right, preferred_element_type=jnp.float32)  94.5 us
  transfers between devices with their start and end apart: 15, of which 13 were waited for; matrix products, arithmetic and copies ran while one was open for 7% of the time, Pallas kernels for 0%

commit v1 on v0

v1 whole, which is shorter than its diff:
```python
import functools

import jax
import jax.numpy as jnp
from jax import lax
from jax.experimental import pallas as pl
from jax.experimental.pallas import tpu as pltpu
from jax.sharding import PartitionSpec as P

HD = 64
GRID = 16
STEP = 10

EPS_NORM = 1e-05
BETA_ONE = 0.9
BETA_TWO = 0.95
ADAM_EPS = 1e-08
CLIP_NORM = 0.01
NEGATIVE_FILL = -1000000000.0
RATES = (0.8, 0.8, 0.08, 0.08, 0.08, 0.08, 0.08, 0.8)
DECAYS = (0.1, 0.1, 0.1, 0.1, 0.1, 0.1, 0.1, 0.0)

MESH = pl.DeviceIdType.MESH
ANY = pl.BlockSpec(memory_space=pl.ANY)
VMEM = pl.BlockSpec(memory_space=pltpu.VMEM)
BF = jnp.bfloat16
F32 = jnp.float32


def dims_of(dp):
    bits = dp.bit_length() - 1
    nz = 1 << (bits // 2)
    rest = dp // nz
    ny = 1 << ((rest.bit_length() - 1) // 2)
    return (nz, ny, rest // ny)


class Place:
    def __init__(self, dims):
        self.dims = dims
        nz, ny, nx = dims
        chip = lax.axis_index("dp")
        self.c = lax.axis_index("seq")
        self.z = chip // (ny * nx)
        self.y = (chip // nx) % ny
        self.x = chip % nx

    def zs(self, back):
        return (self.z + self.dims[0] - back) % self.dims[0]

    def ys(self, back):
        return (self.y + self.dims[1] - back) % self.dims[1]

    def xs(self, back):
        return (self.x + self.dims[2] - back) % self.dims[2]

    def dev(self, z=0, y=0, x=0, c=0):
        nz, ny, nx = self.dims
        z, y, x = ((self.z + z) % nz, (self.y + y) % ny, (self.x + x) % nx)
        return ((z * ny + y) * nx + x, (self.c + c) % 2)


def line_offsets(dims):
    nz, ny, nx = dims
    return (
        [(s, 0, 0, 0) for s in range(1, nz)]
        + [(0, s, 0, 0) for s in range(1, ny)]
        + [(0, 0, s, 0) for s in range(1, nx)]
        + [(0, 0, 0, 1)]
    )


def plane_offsets(dims):
    return [(0, v, u, 0) for v in range(dims[1]) for u in range(dims[2]) if v or u]


def greet(place, offsets):
    offsets = sorted(set(offsets))
    sem = pltpu.get_barrier_semaphore()
    for off in offsets:
        pl.semaphore_signal(sem, inc=1, device_id=place.dev(*off), device_id_type=MESH)
    pl.semaphore_wait(sem, len(offsets))


class Comm:
    def __init__(self, send_sems, recv_sems, local_sems):
        self.send_sems, self.recv_sems, self.local_sems = (send_sems, recv_sems, local_sems)
        self.sent, self.held, self.count, self.locals = ([], [], 0, 0)

    def send(self, src, dst, device):
        k = self.count
        self.count += 1
        copy = pltpu.make_async_remote_copy(
            src_ref=src,
            dst_ref=dst,
            send_sem=self.send_sems.at[k],
            recv_sem=self.recv_sems.at[k],
            device_id=device,
            device_id_type=MESH,
        )
        copy.start()
        self.sent.append(copy)
        return copy

    def keep(self, src, dst):
        copy = pltpu.make_async_copy(src, dst, self.local_sems.at[self.locals])
        self.locals += 1
        copy.start()
        self.held.append(copy)
        return copy

    def finish(self, but=()):
        for copy in self.sent:
            copy.wait_send()
        for copy in self.held:
            if copy not in but:
                copy.wait()


def small_gather(comm, place, src, out):
    nz, ny, nx = place.dims
    z, y, x, c = (place.z, place.y, place.x, place.c)
    mine = comm.keep(src, out.at[z, y, x, c])
    comm.held.remove(mine)
    got = [comm.send(src, out.at[z, y, x, c], place.dev(c=1))]
    yield
    for copy in got:
        copy.wait_recv()
    mine.wait()
    got = [comm.send(out.at[z, y, x], out.at[z, y, x], place.dev(x=t)) for t in range(1, nx)]
    yield
    for copy in got:
        copy.wait_recv()
    got = [comm.send(out.at[z, y], out.at[z, y], place.dev(y=t)) for t in range(1, ny)]
    yield
    for copy in got:
        copy.wait_recv()
    got = [comm.send(out.at[z], out.at[z], place.dev(z=t)) for t in range(1, nz)]
    yield
    for copy in got:
        copy.wait_recv()


def drain(stages):
    for _ in stages:
        pass


def sems(count):
    return pltpu.SemaphoreType.DMA((count,))


def shape(dims, dtype):
    return jax.ShapeDtypeStruct(tuple(dims), dtype)


def call(kernel, outs, in_specs, out_specs, scratch, cid, name, args, vmem=None):
    return pl.pallas_call(
        kernel,
        out_shape=outs,
        in_specs=in_specs,
        out_specs=out_specs,
        scratch_shapes=scratch,
        compiler_params=pltpu.CompilerParams(
            collective_id=cid, has_side_effects=True, vmem_limit_bytes=vmem
        ),
        name=name,
    )(*args)


def small_sends(dims):
    return sum(dims) - 2


def gather_first(dims, layers, table, meta, cid):
    nz, ny, nx = dims
    n = len(layers)

    def kernel(*refs):
        ins, rest = (refs[: n + 2], refs[n + 2 :])
        outs, (ssem, rsem, lsem) = (rest[: n + 2], rest[n + 2 :])
        place = Place(dims)
        z, y, x, c = (place.z, place.y, place.x, place.c)
        greet(place, line_offsets(dims) + plane_offsets(dims))
        comm = Comm(ssem, rsem, lsem)
        small = small_gather(comm, place, ins[n + 1], outs[n + 1])
        next(small)
        tab, whole = (ins[n], outs[n])
        slot = whole.at[y, x, c]
        near = [
            (off, comm.send(tab, slot, place.dev(*off))) for off in plane_offsets(dims)
        ]
        waits = []
        for a in range(n):
            comm.keep(ins[a], outs[a].at[z])
            for s in range(1, nz):
                waits.append(comm.send(ins[a], outs[a].at[z], place.dev(z=s)))
        comm.keep(tab, slot)
        waits.append(comm.send(tab, slot, place.dev(c=1)))
        next(small)
        next(small)
        next(small)
        for off, copy in near:
            copy.wait_recv()
            block = whole.at[place.ys(off[1]), place.xs(off[2]), c]
            waits.append(comm.send(block, block, place.dev(c=1)))
        drain(small)
        for copy in waits:
            copy.wait_recv()
        comm.finish()

    count = n * (nz - 1) + 2 * ny * nx + small_sends(dims)
    outs = [shape((nz,) + v.shape, v.dtype) for v in layers]
    outs += [shape((ny, nx, 2) + table.shape, table.dtype), shape(dims + (2,) + meta.shape, meta.dtype)]
    return call(
        kernel, outs, [ANY] * (n + 2), [ANY] * (n + 2), [sems(count), sems(count), sems(n + 2)],
        cid, "gather_first", (*layers, table, meta),
    )


def gather_second(dims, lines, first_axes, rows, small, cid):
    nz, ny, nx = dims
    n = len(lines)
    parts = 2 if nz <= 4 else 1
    step = nz // parts

    def kernel(*refs):
        ins, rest = (refs[: n + 2], refs[n + 2 :])
        outs, (ssem, rsem, lsem) = (rest[: n + 2], rest[n + 2 :])
        place = Place(dims)
        z, y, x, c = (place.z, place.y, place.x, place.c)
        greet(place, line_offsets(dims))
        comm = Comm(ssem, rsem, lsem)
        gather = small_gather(comm, place, ins[n + 1], outs[n + 1])
        next(gather)
        waits = []
        for s in range(1, nz):
            waits.append(comm.send(ins[n].at[place.zs(nz - s)], outs[n].at[z], place.dev(z=s)))
        comm.keep(ins[n].at[z], outs[n].at[z])
        firsts, seconds = ([], [])
        for g in range(parts):
            span = pl.ds(g * step, step)
            for a in range(n):
                src, dst = (ins[a].at[span], outs[a].at[span, y, x, c])
                comm.keep(src, dst)
                waits.append(comm.send(src, dst, place.dev(c=1)))
                first = first_axes[a]
                second = "y" if first == "x" else "x"
                sizes = {"x": nx, "y": ny}
                for t in range(1, sizes[first]):
                    firsts.append((a, span, first, second, sizes[second], t, comm.send(src, dst, place.dev(**{first: t}))))
                for t in range(1, sizes[second]):
                    yy, xx = (place.ys(t), x) if second == "y" else (y, place.xs(t))
                    seconds.append((a, span, yy, xx, comm.send(src, dst, place.dev(**{second: t}))))
        next(gather)
        next(gather)
        next(gather)
        for a, span, first, second, size, t, copy in firsts:
            copy.wait_recv()
            yy, xx = (place.ys(t), x) if first == "y" else (y, place.xs(t))
            block = outs[a].at[span, yy, xx, c]
            for u in range(1, size):
                y2, x2 = (place.ys(u), xx) if second == "y" else (yy, place.xs(u))
                seconds.append((a, span, y2, x2, comm.send(block, block, place.dev(**{second: u}))))
            waits.append(comm.send(block, block, place.dev(c=1)))
        drain(gather)
        for a, span, yy, xx, copy in seconds:
            copy.wait_recv()
            block = outs[a].at[span, yy, xx, c]
            waits.append(comm.send(block, block, place.dev(c=1)))
        for copy in waits:
            copy.wait_recv()
        comm.finish()

    count = n * parts * (2 * ny * nx - 1) + nz + small_sends(dims)
    outs = [shape(dims + (2,) + v.shape[1:], v.dtype) for v in lines]
    outs += [shape(rows.shape, rows.dtype), shape(dims + (2,) + small.shape, small.dtype)]
    return call(
        kernel, outs, [ANY] * (n + 2), [ANY] * (n + 2),
        [sems(count), sems(count), sems(n * parts + 2)],
        cid, "gather_second", (*lines, rows, small),
    )


def line_gather(dims, block, cid, name):
    nz = dims[0]

    def kernel(src, out, ssem, rsem, lsem):
        place = Place(dims)
        greet(place, [(s, 0, 0, 0) for s in range(1, nz)])
        comm = Comm(ssem, rsem, lsem)
        waits = [comm.send(src, out.at[place.z], place.dev(z=s)) for s in range(1, nz)]
        comm.keep(src, out.at[place.z])
        for copy in waits:
            copy.wait_recv()
        comm.finish()

    return call(
        kernel, shape((nz,) + block.shape, block.dtype), [ANY], ANY,
        [sems(nz), sems(nz), sems(1)], cid, name, (block,),
    )


def all_small(dims, block, cid, name):
    def kernel(src, out, ssem, rsem, lsem):
        place = Place(dims)
        greet(place, line_offsets(dims))
        comm = Comm(ssem, rsem, lsem)
        drain(small_gather(comm, place, src, out))
        comm.finish()

    count = small_sends(dims)
    return call(
        kernel, shape(dims + (2,) + block.shape, block.dtype), [ANY], ANY,
        [sems(count), sems(count), sems(1)], cid, name, (block,),
    )


def add_blocks(out, terms):
    lead = out.shape[:-2]

    def visit(index):
        if len(index) < len(lead):

            @pl.loop(0, lead[len(index)])
            def _(i):
                visit(index + (i,))

        else:
            total = terms[0][index].astype(F32)
            for term in terms[1:]:
                total = total + term[index].astype(F32)
            out[index] = total.astype(out.dtype)

    visit(())


def scatter_first(dims, grads, first_axes, rows, small, cid):
    nz, ny, nx = dims
    n = len(grads)

    def kernel(*refs):
        ins, rest = (refs[: n + 2], refs[n + 2 :])
        outs, rest = (rest[: n + 2], rest[n + 2 :])
        halves, ones, twos, (ssem, rsem, lsem) = (
            rest[:n], rest[n : 2 * n], rest[2 * n : 3 * n], rest[3 * n :]
        )
        place = Place(dims)
        z, y, x, c = (place.z, place.y, place.x, place.c)
        greet(place, line_offsets(dims))
        comm = Comm(ssem, rsem, lsem)
        gather = small_gather(comm, place, ins[n + 1], outs[n + 1])
        pair = []
        for a in range(n):
            pair.append(comm.send(ins[a].at[:, :, :, 1 - c], halves[a], place.dev(c=1)))
        next(gather)
        waits = [comm.send(ins[n], outs[n].at[z], place.dev(z=s)) for s in range(1, nz)]
        comm.keep(ins[n], outs[n].at[z])
        got_one = []
        for a in range(n):
            pair[a].wait_recv()
            add_blocks(halves[a], [halves[a], ins[a].at[:, :, :, c]])
            if first_axes[a] == "y":
                got_one.append([
                    comm.send(halves[a].at[:, place.ys(ny - t)], ones[a].at[t - 1], place.dev(y=t))
                    for t in range(1, ny)
                ])
            else:
                got_one.append([
                    comm.send(halves[a].at[:, :, place.xs(nx - t)], ones[a].at[t - 1], place.dev(x=t))
                    for t in range(1, nx)
                ])
        next(gather)
        next(gather)
        next(gather)
        got_two = []
        for a in range(n):
            for copy in got_one[a]:
                copy.wait_recv()
            if first_axes[a] == "y":
                mine = halves[a].at[:, y]
                add_blocks(mine, [mine] + [ones[a].at[t] for t in range(ny - 1)])
                got_two.append([
                    comm.send(halves[a].at[:, y, place.xs(nx - t)], twos[a].at[t - 1], place.dev(x=t))
                    for t in range(1, nx)
                ])
            else:
                mine = halves[a].at[:, :, x]
                add_blocks(mine, [mine] + [ones[a].at[t] for t in range(nx - 1)])
                got_two.append([
                    comm.send(halves[a].at[:, place.ys(ny - t), x], twos[a].at[t - 1], place.dev(y=t))
                    for t in range(1, ny)
                ])
        drain(gather)
        for a in range(n):
            for copy in got_two[a]:
                copy.wait_recv()
            terms = [twos[a].at[t] for t in range(twos[a].shape[0])]
            add_blocks(outs[a], [halves[a].at[:, y, x]] + terms)
        for copy in waits:
            copy.wait_recv()
        comm.finish()

    count = n * (ny + nx - 1) + nz + small_sends(dims)
    scratch = [pltpu.VMEM((nz, ny, nx) + g.shape[4:], g.dtype) for g in grads]
    for g, axis in zip(grads, first_axes):
        near, far = (ny, nx) if axis == "y" else (nx, ny)
        scratch.append(pltpu.VMEM((near - 1, nz, far) + g.shape[4:], g.dtype))
    for g, axis in zip(grads, first_axes):
        scratch.append(pltpu.VMEM(((nx if axis == "y" else ny) - 1, nz) + g.shape[4:], g.dtype))
    outs = [shape((nz,) + g.shape[4:], g.dtype) for g in grads]
    outs += [shape((nz,) + rows.shape, rows.dtype), shape(dims + (2,) + small.shape, small.dtype)]
    return call(
        kernel, outs, [VMEM] * n + [ANY] * 2, [VMEM] * n + [ANY] * 2,
        scratch + [sems(count), sems(count), sems(2)],
        cid, "scatter_first", (*grads, rows, small), 60 * 2**20,
    )


def scatter_second(dims, lines, table, cid):
    nz, ny, nx = dims
    n = len(lines)
    block = table.shape[3:]

    def kernel(*refs):
        ins, rest = (refs[: n + 1], refs[n + 1 :])
        outs, rest = (rest[: n + 1], rest[n + 1 :])
        got, half, near, ssem, rsem, lsem = (rest[:n], *rest[n:])
        place = Place(dims)
        z, y, x, c = (place.z, place.y, place.x, place.c)
        offsets = plane_offsets(dims)
        greet(place, line_offsets(dims) + offsets)
        comm = Comm(ssem, rsem, lsem)
        pair = comm.send(ins[n].at[:, :, 1 - c], half, place.dev(c=1))
        lines_in = [
            [
                comm.send(ins[a].at[place.zs(nz - s)], got[a].at[s - 1], place.dev(z=s))
                for s in range(1, nz)
            ]
            for a in range(n)
        ]
        pair.wait_recv()
        add_blocks(half, [half, ins[n].at[:, :, c]])
        arriving = [
            comm.send(half.at[place.ys(ny - off[1]), place.xs(nx - off[2])], near.at[k], place.dev(*off))
            for k, off in enumerate(offsets)
        ]
        for a in range(n):
            for copy in lines_in[a]:
                copy.wait_recv()
            add_blocks(outs[a], [ins[a].at[z]] + [got[a].at[s] for s in range(nz - 1)])
        for copy in arriving:
            copy.wait_recv()
        add_blocks(outs[n], [half.at[y, x]] + [near.at[k] for k in range(len(offsets))])
        comm.finish()

    count = n * (nz - 1) + ny * nx
    scratch = [pltpu.VMEM((nz - 1,) + v.shape[1:], v.dtype) for v in lines]
    scratch += [pltpu.VMEM((ny, nx) + block, BF), pltpu.VMEM((ny * nx - 1,) + block, BF)]
    outs = [shape(v.shape[1:], F32) for v in lines] + [shape(block, F32)]
    return call(
        kernel, outs, [VMEM] * (n + 1), [VMEM] * (n + 1),
        scratch + [sems(count), sems(count), sems(1)],
        cid, "scatter_second", (*lines, table), 60 * 2**20,
    )


def matmul(left, right):
    return jnp.dot(left, right, preferred_element_type=F32)


def norm_forward(values, gain):
    inverse = lax.rsqrt(jnp.mean(values * values, axis=-1, keepdims=True) + EPS_NORM)
    normed = values * inverse
    return (normed * gain, normed, inverse)


def norm_backward(grad, normed, inverse, gain):
    scaled = grad * gain
    inner = jnp.mean(scaled * normed, axis=-1, keepdims=True)
    return (inverse * (scaled - normed * inner), jnp.sum(grad * normed, axis=0))


def turn_half(tensor):
    quarter = tensor.shape[-1] // 4
    return jnp.concatenate(
        [
            -tensor[..., quarter : 2 * quarter],
            tensor[..., :quarter],
            -tensor[..., 3 * quarter :],
            tensor[..., 2 * quarter : 3 * quarter],
        ],
        axis=-1,
    )


def rope_tables(positions, width):
    quarter = width // 4
    freq = 10000.0 ** (-jnp.arange(quarter, dtype=F32) / quarter)
    row_angle = (positions // GRID).astype(F32)[:, None] * freq
    col_angle = (positions % GRID).astype(F32)[:, None] * freq
    angles = jnp.concatenate([row_angle, row_angle, col_angle, col_angle], axis=-1)
    return (jnp.cos(angles)[:, None, :], jnp.sin(angles)[:, None, :])


def rotate(tensor, cosine, sine):
    return tensor * cosine + turn_half(tensor) * sine


def rotate_back(grad, cosine, sine):
    return grad * cosine - turn_half(grad * sine)


def masked_scores(query, keys, height):
    scores = jnp.einsum("qhd,khd->hqk", query, keys, preferred_element_type=F32) * HD ** (-0.5)
    places = jnp.arange(query.shape[0])
    allowed = (places[None, :] <= places[:, None]) & (places[None, :] < GRID * height)
    return jnp.where(allowed[None], scores, NEGATIVE_FILL)


def attend(query, keys, values, height):
    scores = masked_scores(query, keys, height)
    score_peak = jnp.max(scores, axis=-1, keepdims=True)
    exponent = jnp.exp(scores - score_peak)
    score_total = jnp.sum(exponent, axis=-1, keepdims=True)
    probs = exponent / score_total
    output = jnp.einsum("hqk,khd->qhd", probs.astype(BF), values, preferred_element_type=F32)
    return (output.astype(BF).reshape(query.shape[0], -1), probs)


def attend_back(query, keys, values, probs, grad_out):
    grad_heads = grad_out.reshape(query.shape)
    grad_probs = jnp.einsum("qhd,khd->hqk", grad_heads, values, preferred_element_type=F32)
    grad_scores = probs * (grad_probs - jnp.sum(probs * grad_probs, axis=-1, keepdims=True))
    grad_scores = grad_scores.astype(BF)
    scale = HD ** (-0.5)
    grad_query = jnp.einsum("hqk,khd->qhd", grad_scores, keys, preferred_element_type=F32) * scale
    grad_keys = jnp.einsum("hqk,qhd->khd", grad_scores, query, preferred_element_type=F32) * scale
    grad_values = jnp.einsum(
        "hqk,qhd->khd", probs.astype(BF), grad_heads, preferred_element_type=F32
    )
    return (grad_query.astype(BF), grad_keys.astype(BF), grad_values.astype(BF))


def adam_update(master, drift, square, grad, rate, decay):
    moment = BETA_ONE * drift + (1.0 - BETA_ONE) * grad
    second = BETA_TWO * square + (1.0 - BETA_TWO) * grad * grad
    stride = (
        moment / (1.0 - BETA_ONE**STEP) / (jnp.sqrt(second / (1.0 - BETA_TWO**STEP)) + ADAM_EPS)
    )
    return (master - rate * (stride + decay * master), moment, second)


def pad_rows(value, rows):
    flat = value.reshape(-1)
    return jnp.pad(flat, (0, rows * 128 - flat.shape[0])).reshape(rows, 128)


def block_form(rows, columns):
    return (rows, columns) if rows % 8 == 0 else (rows * columns // 128, 128)


FIRST_AXES = ("x", "x", "y", "x")


def on_device(dims, *args):
    labels, targets, heights, loss_mask = args[:4]
    masters, drifts, squares = (args[4:12], args[12:20], args[20:28])
    class_table, code_table, attend_in, attend_mix, expand_in, shrink_out, head_weight, norm_gains = masters
    nz, ny, nx = dims
    plane = ny * nx
    chips = nz * plane
    images, local_len = targets.shape
    length = local_len * 2
    width = code_table.shape[1]
    device_codes = code_table.shape[0]
    line_codes = device_codes * plane * 2
    gain_columns = norm_gains.shape[1]
    chip, core = (lax.axis_index("dp"), lax.axis_index("seq"))
    z, y, x = (chip // plane, (chip // nx) % ny, chip % nx)
    plane_groups = [[k * plane + i for i in range(plane)] for k in range(nz)]
    line_groups = [[k * plane + i for k in range(nz)] for i in range(plane)]

    head_near = lax.all_gather(head_weight.astype(BF), "dp", axis_index_groups=plane_groups)
    head_near = lax.all_gather(head_near, "seq")

    layers = [v.astype(BF) for v in (attend_in, attend_mix, expand_in, shrink_out)]
    tail = jnp.concatenate([labels, heights])
    meta = jnp.concatenate([targets, loss_mask, pad_rows(tail, 4)], axis=0)
    *lines, table, metas = gather_first(dims, layers, code_table.astype(BF), meta, 0)
    table = table.reshape(line_codes, width)

    own_tokens = lax.dynamic_slice_in_dim(metas, core, 1, axis=4)[:, :, :, :, 0]
    own_masks = lax.dynamic_slice_in_dim(metas, 2 + core, 1, axis=4)[:, :, :, :, 0]

    def of_line(value):
        value = lax.dynamic_slice_in_dim(value, y, 1, axis=1)
        return lax.dynamic_slice_in_dim(value, x, 1, axis=2).reshape(nz, -1)

    line_targets = of_line(own_tokens)
    line_heights = of_line(lax.dynamic_slice_in_dim(metas[:, :, :, 0, 4], images + core, 1, axis=3))
    places = jnp.arange(length)
    line_counted = (of_line(own_masks) * (places[None, :] < GRID * line_heights)).astype(F32)
    all_labels = metas[:, :, :, 0, 4, :images].reshape(-1)
    before = jnp.concatenate(
        [jnp.full((nz, 1), -1, jnp.int32), line_targets[:, :-1] - z * line_codes], axis=1
    ).reshape(-1)
    code_pick = (before[:, None] == jnp.arange(line_codes)[None, :]).astype(BF)
    rows = matmul(code_pick, table).astype(BF).reshape(nz, length, width)
    class_pick = all_labels[:, None] == jnp.arange(class_table.shape[0])[None, :]
    class_part = matmul(class_pick.astype(BF), class_table.astype(BF))
    gains_low = norm_gains.astype(BF).astype(F32)
    small = jnp.concatenate([pad_rows(class_part, 6), pad_rows(gains_low, 2)], axis=0)

    *weights, row_parts, smalls = gather_second(dims, lines, FIRST_AXES, rows, small, 1)
    qkv_w, mix_w, expand_w, shrink_w = (v.reshape(-1, v.shape[-1]) for v in weights)
    smalls = smalls.reshape(chips * 2, -1)
    class_rows = smalls[:, : 6 * 128].reshape(chips * 2, chips * images, -1)
    class_row = lax.dynamic_slice_in_dim(class_rows, chip * images + core, 1, axis=1).reshape(1, -1)
    gain = smalls[:, 6 * 128 : 6 * 128 + 3 * gain_columns].reshape(chips * 2, 3, gain_columns)
    gain = gain.transpose(1, 0, 2).reshape(3, -1)
    start = jnp.sum(row_parts.astype(F32), axis=0)
    start = jnp.where((places == 0)[:, None], class_row, start)
    height = lax.dynamic_slice_in_dim(line_heights, z, 1, axis=0).reshape(())

    cosine, sine = rope_tables(places, HD)
    normed_one, norm_one, inverse_one = norm_forward(start, gain[0])
    normed_one = normed_one.astype(BF)
    mixed = matmul(normed_one, qkv_w).reshape(length, 3, -1, HD)
    query = rotate(mixed[:, 0], cosine, sine).astype(BF)
    keys = rotate(mixed[:, 1], cosine, sine).astype(BF)
    values = mixed[:, 2].astype(BF)
    attended, probs = attend(query, keys, values, height)
    middle = start + matmul(attended, mix_w)
    normed_two, norm_two, inverse_two = norm_forward(middle, gain[1])
    normed_two = normed_two.astype(BF)
    both = matmul(normed_two, expand_w)
    inner = both.shape[1] // 2
    gate_part, up_part = (both[:, :inner], both[:, inner:])
    hidden = (jax.nn.silu(gate_part) * up_part).astype(BF)
    final = middle + matmul(hidden, shrink_w)
    normed_top, norm_top, inverse_top = norm_forward(final, gain[2])
    normed_top = normed_top.astype(BF)

    tops = line_gather(dims, normed_top, 2, "top_rows").reshape(nz * length, width)
    head_w = head_near.transpose(2, 1, 0, 3).reshape(width, line_codes)
    logits = matmul(tops, head_w)
    local_targets = (line_targets - z * line_codes).reshape(-1, 1)
    onehot = local_targets == jnp.arange(line_codes)[None, :]
    peak = jnp.max(logits, axis=1)
    total = jnp.sum(jnp.exp(logits - peak[:, None]), axis=1)
    picked = jnp.sum(jnp.where(onehot, logits, 0.0), axis=1)
    stats = jnp.concatenate([v.reshape(-1, 128) for v in (peak, total, picked)], axis=0)
    stats = line_gather(dims, stats, 3, "row_stats").reshape(nz, 3, -1)
    peaks = jnp.max(stats[:, 0], axis=0)
    totals = jnp.sum(stats[:, 1] * jnp.exp(stats[:, 0] - peaks[None, :]), axis=0)
    log_total = peaks + jnp.log(totals)
    counted = line_counted.reshape(-1)
    losses = (log_total - jnp.sum(stats[:, 2], axis=0)) * counted
    loss_local = jnp.sum(lax.dynamic_slice_in_dim(losses.reshape(nz, -1), z, 1, axis=0))
    count_local = jnp.sum(lax.dynamic_slice_in_dim(line_counted, z, 1, axis=0))
    softmax = jnp.exp(logits - peaks[:, None]) / totals[:, None]
    grad_logits = ((softmax - onehot.astype(F32)) * counted[:, None]).astype(BF)
    grad_tops = matmul(grad_logits, head_w.T).astype(BF).reshape(nz, length, width)
    grad_top = lax.psum_scatter(grad_tops, "dp", axis_index_groups=line_groups)
    grad_head = matmul(tops.T, grad_logits).astype(BF).reshape(width, plane, 2, -1)
    grad_head = lax.psum_scatter(grad_head, "seq", scatter_dimension=2)
    grad_head = lax.psum_scatter(
        grad_head, "dp", scatter_dimension=1, axis_index_groups=plane_groups
    ).astype(F32)

    grad_final, gain_top = norm_backward(grad_top.astype(F32), norm_top, inverse_top, gain[2])
    back_down = grad_final.astype(BF)
    grad_shrink = matmul(hidden.T, back_down)
    grad_hidden = matmul(back_down, shrink_w.T)
    sigma = jax.nn.sigmoid(gate_part)
    grad_gate = grad_hidden * up_part * sigma * (1.0 + gate_part * (1.0 - sigma))
    grad_up = grad_hidden * gate_part * sigma
    grad_both = jnp.concatenate([grad_gate, grad_up], axis=1).astype(BF)
    grad_expand = matmul(normed_two.T, grad_both)
    grad_norm_two, gain_two = norm_backward(
        matmul(grad_both, expand_w.T), norm_two, inverse_two, gain[1]
    )
    grad_middle = grad_final + grad_norm_two
    back_mix = grad_middle.astype(BF)
    grad_mix = matmul(attended.T, back_mix)
    grad_attended = matmul(back_mix, mix_w.T).astype(BF)
    grad_query, grad_keys, grad_values = attend_back(query, keys, values, probs, grad_attended)
    grad_mixed = jnp.stack(
        [
            rotate_back(grad_query.astype(F32), cosine, sine).astype(BF),
            rotate_back(grad_keys.astype(F32), cosine, sine).astype(BF),
            grad_values,
        ],
        axis=1,
    ).reshape(length, -1)
    grad_qkv = matmul(normed_one.T, grad_mixed)
    grad_norm_one, gain_one = norm_backward(
        matmul(grad_mixed, qkv_w.T), norm_one, inverse_one, gain[0]
    )
    grad_start = grad_middle + grad_norm_one

    grads_in = []
    for grad, shard in zip((grad_qkv, grad_mix, grad_expand, grad_shrink), layers):
        grads_in.append(grad.astype(BF).reshape(dims + (2,) + block_form(*shard.shape)))
    small = jnp.concatenate(
        [
            pad_rows(grad_start[0], width // 128),
            pad_rows(jnp.concatenate([gain_one, gain_two, gain_top]), 3 * width // 128),
        ],
        axis=0,
    )
    *line_grads, row_grads, smalls = scatter_first(
        dims, grads_in, FIRST_AXES, grad_start.astype(BF), small, 4
    )
    row_grads = row_grads.reshape(nz * length, width)
    table_grad = lax.dot_general(
        code_pick, row_grads, (((0,), (0,)), ((), ())), preferred_element_type=F32
    )
    table_grad = table_grad.astype(BF).reshape(ny, nx, 2, device_codes, width)
    *layer_shares, code_share = scatter_second(dims, line_grads, table_grad, 5)
    layer_shares = [g.reshape(v.shape) for g, v in zip(layer_shares, layers)]
    smalls = smalls.reshape(chips * 2, 4, -1)
    device = chip * 2 + core
    small_mine = lax.dynamic_slice_in_dim(smalls, device * gain_columns, gain_columns, axis=2)
    class_share = jnp.dot(
        class_pick.astype(F32).T,
        small_mine[:, 0],
        precision=lax.Precision.HIGHEST,
        preferred_element_type=F32,
    )
    gain_share = jnp.sum(small_mine[:, 1:], axis=0)
    shares = (class_share, code_share, *layer_shares, grad_head, gain_share)

    square_local = sum((jnp.sum(member * member) for member in shares))
    sums = pad_rows(jnp.stack([square_local, loss_local, count_local]), 8)
    sums = jnp.sum(all_small(dims, sums, 6, "last_sums").reshape(chips * 2, -1), axis=0)
    total_square, loss_sum, loss_count = (sums[0], sums[1], sums[2])
    grad_norm = jnp.sqrt(total_square) / loss_count
    factor = CLIP_NORM / jnp.maximum(grad_norm, CLIP_NORM) / loss_count
    news, firsts, seconds = ([], [], [])
    for member in range(8):
        fresh, moment, second = adam_update(
            masters[member],
            drifts[member],
            squares[member],
            shares[member] * factor,
            RATES[member],
            DECAYS[member],
        )
        news.append(fresh)
        firsts.append(moment)
        seconds.append(second)
    return tuple(news) + tuple(firsts) + tuple(seconds) + (grad_norm, loss_sum, loss_count)


def solution(mesh):
    rows, columns = (P(("dp", "seq"), None), P(None, ("dp", "seq")))
    eight = (columns, rows, rows, rows, rows, rows, columns, columns)
    return jax.shard_map(
        functools.partial(on_device, dims_of(mesh.shape["dp"])),
        mesh=mesh,
        in_specs=(P("dp"), P("dp", "seq"), P("dp"), P("dp", "seq")) + eight * 3,
        out_specs=eight * 3 + (P(), P(), P()),
        check_vma=False,
    )
```

time: 2290 us -> 605 us (0.26)
  waiting for transfers between devices: 1850 us -> 3.66 us
  Pallas kernels: 0 us -> 341 us
  blocking collectives: 139 us -> 0 us
  other arithmetic: 98.4 us -> 68.5 us
    reduce_scatter x6 -> x2, waiting for transfers between devices: 1270 us -> 3.55 us  [the longest x1 3.55 us: on_device(): grad_top = lax.psum_scatter(grad_tops, 'dp', axis_index_groups=line_groups)]
    all_gather x7 -> x2, waiting for transfers between devices: 517 us -> 0.02 us  [the longest x1 0.02 us: on_device(): head_near = lax.all_gather(head_near, 'seq')]
    pallas_call x0 -> x7, Pallas kernels: none -> 341 us  [call(): pl.pallas_call(kernel, out_shape=outs, in_specs=in_specs, out_specs=out_s...]
    unnamed x15 -> x6, waiting for transfers between devices: 67.8 us -> 0.09 us
    all_gather x1 -> x0, blocking collectives: 42.7 us -> none  [on_device(): lax.all_gather(norm_gains.astype(jnp.bfloat16), ('dp', 'seq'), axis=1, ti...]
    psum x1 -> x0, blocking collectives: 39.4 us -> none  [on_device(): lax.psum((square_local, loss_local, count_local), ('dp', 'seq'))]
    unnamed x1 -> x0, blocking collectives: 38.6 us -> none
    scatter-add x2 -> x0, other arithmetic: 24 us -> none  [the longest x1 22.5 us: on_device(): jnp.zeros(code_full.shape, jnp.float32).at[codes.reshape(-1)].add(code_part)]
  transfers between devices with their start and end apart: 15 -> 5, of which waited for: 13 -> 1; matrix products, arithmetic and copies ran while one was open for 7% -> 24% of each run, Pallas kernels for 0% -> 52%
where the time goes in v1:
time: 605 us; the launch traced here: 598 us
  Pallas kernels  341 us (56%)
  matrix products  106 us (18%)
  other arithmetic  68.5 us (11%)
  local copies, waits for them, and re-layouts  54.7 us (9%)
  between operations  23.7 us (4%)
    pallas_call x7, Pallas kernels, call(): pl.pallas_call(kernel, out_shape=outs, in_specs=in_specs, out_specs=out_s...  341 us
    dot_general x17, matrix products, matmul(): return jnp.dot(left, right, preferred_element_type=F32)  79.8 us
    reshape x2, local copies, waits for them, and re-layouts, on_device(): matmul(tops.T, grad_logits).astype(BF).reshape(width, plane, 2, -1)  18.9 us
    sub x8, other arithmetic, adam_update(): return (master - rate * (stride + decay * master), moment, second)  16.1 us
    unnamed x201, local copies, waits for them, and re-layouts  12.9 us
  transfers between devices with their start and end apart: 5, of which 1 were waited for; matrix products, arithmetic and copies ran while one was open for 24% of the time, Pallas kernels for 52%

profile of v1, /device:TPU:0, one launch (start us, length us, event | category | flops | bytes accessed | tf_op | source)
XLA Modules:
  0.0 598.3 jit_solution(11472211381014879004)
XLA Ops:
  7.3 2.5 convert_element_type.206
  14.5 74.5 %gather_first.1 = (bf16[4,24,2304]{2,1,0:T(8,128)(2,1)}, bf16[4,24,768]{2,1,0:T(8,128)(2,1)}, bf16[4,24,4096]{2,1,0:T(8,128)(2,1)}, bf16[4,64,768]{2,1,0:T(8,128...) custom-call(bf16[24,2304]{1,0:T(8,128)(2,1)} %convert_element_type.185.refs_0_, ...), custom_call_target="tpu_custom_call" | custom-call | tf_op jit(solution)/shard_map/gather_first/pallas_call | solution.py:158
  93.3 11.2 %fusion.7 = bf16[1024,768]{1,0:T(8,128)(2,1)} fusion(bf16[4096,768]{1,0:T(8,128)(2,1)} %bitcast.231, s32[1024]{0:T(1024)S(1)} %bitcast.229), kind=kOutput, calls=%fused_computation.30 | convolution fusion | flops 6447431680 | bytes 7868416 | tf_op jit(solution)/shard_map/dot_general | solution.py:469
  104.5 70.3 %gather_second.1 = (bf16[4,2,2,2,24,2304]{5,4,3,2,1,0:T(8,128)(2,1)}, bf16[4,2,2,2,24,768]{5,4,3,2,1,0:T(8,128)(2,1)}, bf16[4,2,2,2,24,4096]{5,4,3,2,1,0:T(8,128...) custom-call(bf16[4,24,2304]{2,1,0:T(8,128)(2,1)} %get-tuple-element., ...), custom_call_target="tpu_custom_call" | custom-call | tf_op jit(solution)/shard_map/gather_second/pallas_call | solution.py:158
  178.8 5.8 copy.95
  187.3 3.6 fusion.40
  192.3 4.8 fusion.103
  197.1 2.4 convolution_convert_fusion.8
  210.2 29.0 %top_rows.1 = bf16[4,256,768]{2,1,0:T(8,128)(2,1)} custom-call(bf16[256,768]{1,0:T(8,128)(2,1)} %multiply_convert_fusion.5.src), custom_call_target="tpu_custom_call" | custom-call | tf_op jit(solution)/shard_map/top_rows/pallas_call | solution.py:158
  239.3 8.8 %copy.99 = bf16[768,4,2,512]{0,3,2,1:T(8,128)(2,1)} copy(bf16[768,4,2,512]{3,0,1,2:T(8,128)(2,1)} %bitcast.189) | data formatting | bytes 12582912 | tf_op jit(solution)/shard_map/transpose | solution.py:646
  248.2 9.4 %fusion.104 = (f32[1024]{0:T(1024)S(1)}, f32[1024,4096]{1,0:T(8,128)S(1)}) fusion(bf16[1024,768]{1,0:T(8,128)(2,1)} %bitcast.206, bf16[768,4096]{0,1:T(8,128)(2,1)} %bitcast.190), kind=kOutput, calls=%fused_computation.236 | convolution fusion | flops 6446644224 | bytes 24645632 | tf_op jit(solution)/shard_map/dot_general | solution.py:469
  257.7 4.8 exponential_reduce_fusion
  264.0 13.6 %row_stats.1 = f32[4,24,128]{2,1,0:T(8,128)} custom-call(f32[24,128]{1,0:T(8,128)} %pad_maximum_fusion.5.src), custom_call_target="tpu_custom_call" | custom-call | tf_op jit(solution)/shard_map/row_stats/pallas_call | solution.py:158
  278.5 9.9 %multiply_convert_fusion = bf16[1024,4096]{1,0:T(8,128)(2,1)S(1)} fusion(f32[1024,4096]{1,0:T(8,128)} %copy-done, f32[1024]{0:T(1024)S(1)} %select_convert_fusion, f32[1024]{0:T(1024)S(1)} %fusion.69, f32[1024]{0:T(1024)S(1)} %get-tuple-element.82, s32[1024]{0:T(1024)S(1)} %bitcast.217), kind=kLoop, calls=%fused_computation.1 | loop fusion | flops 29360128 | bytes 25182208 | tf_op jit(solution)/shard_map/convert_element_type | solution.py:663
  288.5 13.6 %convolution_convert_fusion.4 = bf16[1024,768]{1,0:T(8,128)(2,1)} fusion(bf16[1024,4096]{1,0:T(8,128)(2,1)S(1)} %multiply_convert_fusion, bf16[768,4096]{0,1:T(8,128)(2,1)} %bitcast.191), kind=kOutput, calls=%fused_computation.31 | convolution fusion | flops 6443237376 | bytes 16252928 | tf_op jit(solution)/shard_map/dot_general | solution.py:469
  302.1 11.5 %convolution_convert_fusion = bf16[768,4096]{1,0:T(8,128)(2,1)} fusion(bf16[1024,768]{1,0:T(8,128)(2,1)} %bitcast.207, bf16[1024,4096]{1,0:T(8,128)(2,1)} %copy-done.10), kind=kOutput, calls=%fused_computation.10 | convolution fusion | flops 6445596672 | bytes 16252928 | tf_op jit(solution)/shard_map/dot_general | solution.py:469
  313.6 11.2 %reshape.501 = bf16[768,4,2,512]{3,2,1,0:T(2,128)(2,1)} reshape(bf16[768,4096]{1,0:T(8,128)(2,1)} %convolution_convert_fusion) | data formatting | bytes 12582912 | tf_op jit(solution)/shard_map/reshape | solution.py:666
  324.8 7.7 %copy.105 = bf16[768,4,2,512]{3,0,1,2:T(8,128)(2,1)} copy(bf16[768,4,2,512]{3,2,1,0:T(2,128)(2,1)} %reshape.501) | data formatting | bytes 12582912 | tf_op jit(solution)/shard_map/reshape | solution.py:666
  333.9 3.5 reduce-scatter.6.cloned.1.call-done
  339.6 5.0 multiply_convert_fusion.3
  344.7 7.0 %multiply_reduce_fusion.2 = (f32[768]{0:T(1024)}, f32[256]{0:T(256)S(1)}, f32[256,768]{1,0:T(8,128)S(1)}) fusion(f32[256,768]{1,0:T(8,128)S(1)} %copy-done.3, f32[256]{0:T(256)S(1)} %copy-done.64, f32[768]{0:T(1024)S(1)} %mul.708, bf16[768,4096]{1,0:T(8,128)(2,1)} %bitcast.185, bf16[256,2048]{1,0:T(8,128)(2,1)S(1)} %get-tuple-element.112, ...), kind=kOutput, calls=%fused_computation.83 | convolution fusion | flops 1615985664 | bytes 9969664 | tf_op jit(solution)/shard_map/dot_general | solution.py:469
  356.2 2.8 multiply_reduce_fusion
  373.6 3.0 convolution_convert_fusion.3
  376.6 3.1 convolution_convert_fusion.2
  379.7 4.7 convolution_convert_fusion.1
  384.4 92.1 %scatter_first.1 = (bf16[4,24,2304]{2,1,0:T(8,128)(2,1)}, bf16[4,24,768]{2,1,0:T(8,128)(2,1)}, bf16[4,24,4096]{2,1,0:T(8,128)(2,1)}, bf16[4,64,768]{2,1,0:T(8,12...) custom-call(bf16[4,2,2,2,24,2304]{5,4,3,2,1,0:T(8,128)(2,1)} %bitcast.182, ...), custom_call_target="tpu_custom_call" | custom-call | tf_op jit(solution)/shard_map/scatter_first/pallas_call | solution.py:158
  477.7 12.0 %fusion.5 = bf16[4096,768]{1,0:T(8,128)(2,1)} fusion(bf16[1024,768]{1,0:T(8,128)(2,1)} %bitcast.234, s32[1024]{0:T(1024)S(1)} %bitcast.230), kind=kOutput, calls=%fused_computation.12 | convolution fusion | flops 6449790976 | bytes 7868416 | tf_op jit(solution)/shard_map/dot_general | solution.py:717
  489.7 47.7 %scatter_second.1 = (f32[24,2304]{1,0:T(8,128)}, f32[24,768]{1,0:T(8,128)}, f32[24,4096]{1,0:T(8,128)}, f32[64,768]{1,0:T(8,128)}, f32[512,768]{1,0:T(8,128)}) custom-call(bf16[4,24,2304]{2,1,0:T(8,128)(2,1)} %get-tuple-element.63.refs_0_, bf16[4,24,768]{2,1,0:T(8,128)(2,1)} %get-tuple-element.64.refs_1_, bf16[4,24,4096]{2,1,0:T(8,128)(2,1)} %get-tuple-element.65.refs_2_, ...), custom_call_target="tpu_custom_call" | custom-call | tf_op jit(solution)/shard_map/scatter_second/pallas_call | solution.py:158
  537.6 2.5 multiply_reduce_fusion.1
  556.3 13.6 %last_sums.1 = f32[4,2,2,2,8,128]{5,4,3,2,1,0:T(8,128)} custom-call(f32[8,128]{1,0:T(8,128)} %fusion.71.src), custom_call_target="tpu_custom_call" | custom-call | tf_op jit(solution)/shard_map/last_sums/pallas_call | solution.py:158
  582.9 3.0 multiply_subtract_fusion.1
  587.4 3.1 multiply_subtract_fusion
  (319 shorter events, 76.9 us)
Async XLA Ops:
  7.3 177.3 %all-gather.5.cloned.1.call-start = ((), (), s32[]{:S(2)}) async-start(), calls=%async_computation.5 | async-start | bytes 3932160 | tf_op jit(solution)/shard_map/all_gather | solution.py:584
  9.9 229.4 %all-gather.7.cloned.1.call-start = ((), (), s32[]{:S(2)}) async-start(), calls=%async_computation.6 | async-start | bytes 9437184 | tf_op jit(solution)/shard_map/all_gather | solution.py:585
  12.1 80.3 %copy-start.52 = (f32[1001,24]{0,1:T(8,128)S(1)}, f32[1001,24]{0,1:T(8,128)}, u32[]{:S(2)}) copy-start(f32[1001,24]{0,1:T(8,128)} %param.32) | copy-start | bytes 288292
  92.4 12.1 %copy-start.84 = (s32[1,2,4,128]{3,1,2,0:T(2,128)}, s32[1,2,4,128]{3,1,2,0:T(2,128)S(1)}, u32[]{:S(2)}) copy-start(s32[1,2,4,128]{3,1,2,0:T(2,128)S(1)} %copy.117) | copy-start | bytes 12292
  184.6 152.8 %reduce-scatter.6.cloned.1.call-start = ((), (), s32[]{:S(2)}) async-start(), calls=%async_computation.3 | async-start | bytes 1966080 | tf_op jit(solution)/shard_map/reduce_scatter | solution.py:665
  208.5 30.8 %copy-start.62 = (s32[4,1,1,2,1,128]{5,4,3,2,1,0:T(1,128)S(1)}, s32[4,1,1,2,1,128]{5,4,3,2,1,0:T(1,128)}, u32[]{:S(2)}) copy-start(s32[4,1,1,2,1,128]{5,4,3,2,1,0:T(1,128)} %get-tuple-element.134) | copy-start | bytes 12292
  208.5 30.8 %copy-start.83 = (pred[1024]{0:T(1024)(128)(4,1)S(1)}, pred[1024]{0:T(1024)(128)(4,1)}, u32[]{:S(2)}) copy-start(pred[1024]{0:T(1024)(128)(4,1)} %lt.93) | copy-start | bytes 3076
  208.5 131.1 %copy-start.67 = (f32[256]{0:T(256)}, f32[256]{0:T(256)S(1)}, u32[]{:S(2)}) copy-start(f32[256]{0:T(256)S(1)} %add_rsqrt_fusion) | copy-start | bytes 3076
  248.2 9.5 %copy-start.66 = (s32[4,1,1,2,1,128]{5,4,3,2,1,0:T(1,128)S(1)}, s32[4,1,1,2,1,128]{5,4,3,2,1,0:T(1,128)}, u32[]{:S(2)}) copy-start(s32[4,1,1,2,1,128]{5,4,3,2,1,0:T(1,128)} %get-tuple-element.133) | copy-start | bytes 12292
  288.5 13.6 %copy-start.10 = (bf16[1024,4096]{1,0:T(8,128)(2,1)}, bf16[1024,4096]{1,0:T(8,128)(2,1)S(1)}, u32[]{:S(2)}) copy-start(bf16[1024,4096]{1,0:T(8,128)(2,1)S(1)} %multiply_convert_fusion) | copy-start | bytes 25165828
  302.0 62.3 %reduce-scatter.8.cloned.1.call-start = ((), (), s32[]{:S(2)}) async-start(), calls=%async_computation.4 | async-start | bytes 9437184 | tf_op jit(solution)/shard_map/reduce_scatter | solution.py:667
  332.5 218.3 %reduce-scatter.10.cloned.1.call-start = ((), (), s32[]{:S(2)}) async-start(), calls=%async_computation.7 | async-start | bytes 3932160
  339.6 12.1 %copy-start.78 = (f32[256]{0:T(256)}, f32[256]{0:T(256)S(1)}, u32[]{:S(2)}) copy-start(f32[256]{0:T(256)S(1)} %broadcast_multiply_fusion.6) | copy-start | bytes 3076
  344.6 7.1 %copy-start.38 = (bf16[256,2048]{1,0:T(8,128)(2,1)}, bf16[256,2048]{1,0:T(8,128)(2,1)S(1)}, u32[]{:S(2)}) copy-start(bf16[256,2048]{1,0:T(8,128)(2,1)S(1)} %get-tuple-element.111) | copy-start | bytes 3145732
  344.6 7.1 %copy-start.40 = (bf16[256,2048]{1,0:T(8,128)(2,1)}, bf16[256,2048]{1,0:T(8,128)(2,1)S(1)}, u32[]{:S(2)}) copy-start(bf16[256,2048]{1,0:T(8,128)(2,1)S(1)} %get-tuple-element.112) | copy-start | bytes 3145732
  344.6 7.1 %copy-start.6 = (f32[256,768]{1,0:T(8,128)S(1)}, f32[256,768]{1,0:T(8,128)}, u32[]{:S(2)}) copy-start(f32[256,768]{1,0:T(8,128)} %copy-done.5) | copy-start | bytes 2359300
  344.7 7.1 %copy-start.19 = (bf16[1,256,768]{2,1,0:T(8,128)(2,1)S(1)}, bf16[1,256,768]{2,1,0:T(8,128)(2,1)}, u32[]{:S(2)}) copy-start(bf16[1,256,768]{2,1,0:T(8,128)(2,1)} %reduce-scatter.6.cloned.1.call-done) | copy-start | bytes 1179652
  384.4 93.2 %copy-start.85 = (s32[1,2,4,128]{3,1,2,0:T(2,128)S(1)}, s32[1,2,4,128]{3,1,2,0:T(2,128)}, u32[]{:S(2)}) copy-start(s32[1,2,4,128]{3,1,2,0:T(2,128)} %copy-done.84) | copy-start | bytes 12292
  489.7 50.5 %copy-start.87 = (s32[32]{0:T(128)S(1)}, s32[32]{0:T(128)}, u32[]{:S(2)}) copy-start(s32[32]{0:T(128)} %copy-done.86) | copy-start | bytes 388
  537.4 9.9 %copy-start.32 = (f32[24,4096]{1,0:T(8,128)S(1)}, f32[24,4096]{1,0:T(8,128)}, u32[]{:S(2)}) copy-start(f32[24,4096]{1,0:T(8,128)} %get-tuple-element.71) | copy-start | bytes 1179652
  537.4 11.3 %copy-start.47 = (f32[64,768]{1,0:T(8,128)S(1)}, f32[64,768]{1,0:T(8,128)}, u32[]{:S(2)}) copy-start(f32[64,768]{1,0:T(8,128)} %get-tuple-element.72) | copy-start | bytes 589828
  537.4 36.0 %copy-start.81 = (f32[3,24]{1,0:T(4,128)S(1)}, f32[3,24]{1,0:T(4,128)}, u32[]{:S(2)}) copy-start(f32[3,24]{1,0:T(4,128)} %param.39) | copy-start | bytes 868
  537.4 36.0 %copy-start.90 = (f32[3,24]{1,0:T(4,128)S(1)}, f32[3,24]{1,0:T(4,128)}, u32[]{:S(2)}) copy-start(f32[3,24]{1,0:T(4,128)} %param.47) | copy-start | bytes 868
  537.4 37.4 %copy-start.56 = (f32[24,768]{1,0:T(8,128)S(1)}, f32[24,768]{1,0:T(8,128)}, u32[]{:S(2)}) copy-start(f32[24,768]{1,0:T(8,128)} %param.35) | copy-start | bytes 221188
  537.5 37.4 %copy-start.57 = (f32[24,768]{1,0:T(8,128)S(1)}, f32[24,768]{1,0:T(8,128)}, u32[]{:S(2)}) copy-start(f32[24,768]{1,0:T(8,128)} %get-tuple-element.70) | copy-start | bytes 221188
  537.6 38.9 %copy-start.46 = (f32[64,768]{1,0:T(8,128)S(1)}, f32[64,768]{1,0:T(8,128)}, u32[]{:S(2)}) copy-start(f32[64,768]{1,0:T(8,128)} %param.37) | copy-start | bytes 589828
  537.6 38.9 %copy-start.58 = (f32[64,768]{1,0:T(8,128)S(1)}, f32[64,768]{1,0:T(8,128)}, u32[]{:S(2)}) copy-start(f32[64,768]{1,0:T(8,128)} %param.45) | copy-start | bytes 589828
  540.1 38.3 %copy-start.42 = (f32[24,2304]{1,0:T(8,128)S(1)}, f32[24,2304]{1,0:T(8,128)}, u32[]{:S(2)}) copy-start(f32[24,2304]{1,0:T(8,128)} %get-tuple-element.69) | copy-start | bytes 663556
  540.1 38.3 %copy-start.44 = (f32[24,2304]{1,0:T(8,128)S(1)}, f32[24,2304]{1,0:T(8,128)}, u32[]{:S(2)}) copy-start(f32[24,2304]{1,0:T(8,128)} %param.34) | copy-start | bytes 663556
  550.8 29.8 %copy-start.31 = (f32[24,4096]{1,0:T(8,128)S(1)}, f32[24,4096]{1,0:T(8,128)}, u32[]{:S(2)}) copy-start(f32[24,4096]{1,0:T(8,128)} %param.36) | copy-start | bytes 1179652
  550.8 32.0 %copy-start.34 = (f32[512,768]{1,0:T(8,128)S(1)}, f32[512,768]{1,0:T(8,128)}, u32[]{:S(2)}) copy-start(f32[512,768]{1,0:T(8,128)} %param.49) | copy-start | bytes 4718596
  573.5 7.1 %copy-start.54 = (f32[24,4096]{1,0:T(8,128)S(1)}, f32[24,4096]{1,0:T(8,128)}, u32[]{:S(2)}) copy-start(f32[24,4096]{1,0:T(8,128)} %param.44) | copy-start | bytes 1179652
  (71 other events, 224.2 us)
Sparse Core Ops, SparseCore 0:
  10.5 71.3 all-gather.4
  184.7 14.7 all-gather.6
  302.2 35.1 reduce-scatter.5
  339.6 13.4 reduce-scatter.7
  364.5 51.3 reduce-scatter.9

commit v2 on v1

--- a/solution.py
+++ b/solution.py
@@ -298,21 +298,6 @@
     return call(
         kernel, shape((nz,) + block.shape, block.dtype), [ANY], ANY,
         [sems(nz), sems(nz), sems(1)], cid, name, (block,),
-    )
-
-
-def all_small(dims, block, cid, name):
-    def kernel(src, out, ssem, rsem, lsem):
-        place = Place(dims)
-        greet(place, line_offsets(dims))
-        comm = Comm(ssem, rsem, lsem)
-        drain(small_gather(comm, place, src, out))
-        comm.finish()
-
-    count = small_sends(dims)
-    return call(
-        kernel, shape(dims + (2,) + block.shape, block.dtype), [ANY], ANY,
-        [sems(count), sems(count), sems(1)], cid, name, (block,),
     )
 
 
@@ -417,15 +402,15 @@
     )
 
 
-def scatter_second(dims, lines, table, cid):
+def scatter_second(dims, lines, table, head, partial, cid):
     nz, ny, nx = dims
     n = len(lines)
     block = table.shape[3:]
 
     def kernel(*refs):
-        ins, rest = (refs[: n + 1], refs[n + 1 :])
-        outs, rest = (rest[: n + 1], rest[n + 1 :])
-        got, half, near, ssem, rsem, lsem = (rest[:n], *rest[n:])
+        ins, rest = (refs[: n + 3], refs[n + 3 :])
+        outs, rest = (rest[: n + 2], rest[n + 2 :])
+        got, (half, near, mine, every, ssem, rsem, lsem) = (rest[:n], rest[n:])
         place = Place(dims)
         z, y, x, c = (place.z, place.y, place.x, place.c)
         offsets = plane_offsets(dims)
@@ -445,28 +430,184 @@
             comm.send(half.at[place.ys(ny - off[1]), place.xs(nx - off[2])], near.at[k], place.dev(*off))
             for k, off in enumerate(offsets)
         ]
+        share = ins[n + 1][...].astype(F32)
+        square = jnp.sum(share * share)
         for a in range(n):
             for copy in lines_in[a]:
                 copy.wait_recv()
             add_blocks(outs[a], [ins[a].at[z]] + [got[a].at[s] for s in range(nz - 1)])
+            square = square + jnp.sum(outs[a][...] * outs[a][...])
         for copy in arriving:
             copy.wait_recv()
         add_blocks(outs[n], [half.at[y, x]] + [near.at[k] for k in range(len(offsets))])
+        square = square + jnp.sum(outs[n][...] * outs[n][...])
+        held = ins[n + 2][...]
+        first = (lax.broadcasted_iota(jnp.int32, held.shape, 0) == 0) & (
+            lax.broadcasted_iota(jnp.int32, held.shape, 1) == 0
+        )
+        mine[...] = held + jnp.where(first, square, 0.0)
+        drain(small_gather(comm, place, mine, every))
+        outs[n + 1][...] = jnp.zeros_like(held)
+        sums = outs[n + 1]
+
+        @pl.loop(0, nz)
+        def _(k):
+            for j in range(ny):
+                for i in range(nx):
+                    sums[...] += every[k, j, i, 0] + every[k, j, i, 1]
+
         comm.finish()
 
-    count = n * (nz - 1) + ny * nx
+    count = n * (nz - 1) + ny * nx + small_sends(dims)
     scratch = [pltpu.VMEM((nz - 1,) + v.shape[1:], v.dtype) for v in lines]
     scratch += [pltpu.VMEM((ny, nx) + block, BF), pltpu.VMEM((ny * nx - 1,) + block, BF)]
-    outs = [shape(v.shape[1:], F32) for v in lines] + [shape(block, F32)]
+    scratch += [pltpu.VMEM(partial.shape, F32), pltpu.VMEM(dims + (2,) + partial.shape, F32)]
+    outs = [shape(v.shape[1:], F32) for v in lines] + [shape(block, F32), shape(partial.shape, F32)]
     return call(
-        kernel, outs, [VMEM] * (n + 1), [VMEM] * (n + 1),
+        kernel, outs, [VMEM] * (n + 3), [VMEM] * (n + 2),
         scratch + [sems(count), sems(count), sems(1)],
-        cid, "scatter_second", (*lines, table), 60 * 2**20,
+        cid, "scatter_second", (*lines, table, head, partial), 60 * 2**20,
     )
 
 
 def matmul(left, right):
     return jnp.dot(left, right, preferred_element_type=F32)
+
+
+def head_forward(tops, weights, marks):
+    cores, plane, width, columns = weights.shape
+    rows = tops.shape[0]
+    blocks = cores * plane
+
+    def kernel(x_ref, w_ref, mark_ref, logit_ref, stat_ref, peak, total, picked):
+        k = pl.program_id(0)
+
+        @pl.when(k == 0)
+        def _():
+            peak[...] = jnp.full_like(peak, -jnp.inf)
+            total[...] = jnp.zeros_like(total)
+            picked[...] = jnp.zeros_like(picked)
+
+        logits = matmul(x_ref[...], w_ref[...])
+        logit_ref[...] = logits
+        lanes = lax.broadcasted_iota(jnp.int32, logits.shape, 1) + k * columns
+        chosen = jnp.where(lanes == mark_ref[...], logits, 0.0)
+        picked[...] += jnp.sum(chosen, axis=1, keepdims=True)
+        old = peak[...]
+        new = jnp.maximum(old, jnp.max(logits, axis=1, keepdims=True))
+        exponent = jnp.sum(jnp.exp(logits - new), axis=1, keepdims=True)
+        total[...] = total[...] * jnp.exp(old - new) + exponent
+        peak[...] = new
+
+        @pl.when(k == blocks - 1)
+        def _():
+            lane = lax.broadcasted_iota(jnp.int32, (rows, 128), 1)
+            table = jnp.where(lane == 0, peak[...], jnp.where(lane == 1, total[...], picked[...]))
+            stat_ref[...] = table.T[:8]
+
+    return pl.pallas_call(
+        kernel,
+        grid=(blocks,),
+        out_shape=[shape((blocks, rows, columns), F32), shape((8, rows), F32)],
+        in_specs=[
+            pl.BlockSpec((rows, width), lambda k: (0, 0)),
+            pl.BlockSpec((None, None, width, columns), lambda k: (k % 2, k // 2, 0, 0)),
+            pl.BlockSpec((rows, 1), lambda k: (0, 0)),
+        ],
+        out_specs=[
+            pl.BlockSpec((None, rows, columns), lambda k: (k, 0, 0)),
+            pl.BlockSpec((8, rows), lambda k: (0, 0)),
+        ],
+        scratch_shapes=[pltpu.VMEM((rows, 1), F32)] * 3,
+        compiler_params=pltpu.CompilerParams(vmem_limit_bytes=48 * 2**20),
+        cost_estimate=pl.CostEstimate(
+            flops=2 * rows * width * columns * blocks,
+            bytes_accessed=blocks * columns * (2 * width + 4 * rows),
+            transcendentals=rows * columns * blocks,
+        ),
+        name="head_forward",
+    )(tops, weights, marks)
+
+
+def head_backward(logits, weights, marks, stats):
+    blocks, rows, columns = logits.shape
+    width = weights.shape[2]
+
+    def kernel(l_ref, w_ref, mark_ref, stat_ref, grad_ref, top_ref, column, total):
+        k = pl.program_id(0)
+
+        @pl.when(k == 0)
+        def _():
+            column[...] = jnp.concatenate([stat_ref[...]] * 16, axis=0).T
+            total[...] = jnp.zeros_like(total)
+
+        held = column[...]
+        soft = jnp.exp(l_ref[...] - held[:, 0:1]) * held[:, 1:2]
+        lanes = lax.broadcasted_iota(jnp.int32, soft.shape, 1) + k * columns
+        grad = (soft - jnp.where(lanes == mark_ref[...], held[:, 2:3], 0.0)).astype(BF)
+        grad_ref[...] = grad
+        total[...] += lax.dot_general(
+            grad, w_ref[...], (((1,), (1,)), ((), ())), preferred_element_type=F32
+        )
+
+        @pl.when(k == blocks - 1)
+        def _():
+            top_ref[...] = total[...].astype(BF)
+
+    return pl.pallas_call(
+        kernel,
+        grid=(blocks,),
+        out_shape=[shape(logits.shape, BF), shape((rows, width), BF)],
+        in_specs=[
+            pl.BlockSpec((None, rows, columns), lambda k: (k, 0, 0)),
+            pl.BlockSpec((None, None, width, columns), lambda k: (k % 2, k // 2, 0, 0)),
+            pl.BlockSpec((rows, 1), lambda k: (0, 0)),
+            pl.BlockSpec((8, rows), lambda k: (0, 0)),
+        ],
+        out_specs=[
+            pl.BlockSpec((None, rows, columns), lambda k: (k, 0, 0)),
+            pl.BlockSpec((rows, width), lambda k: (0, 0)),
+        ],
+        scratch_shapes=[pltpu.VMEM((rows, 128), F32), pltpu.VMEM((rows, width), F32)],
+        compiler_params=pltpu.CompilerParams(vmem_limit_bytes=48 * 2**20),
+        cost_estimate=pl.CostEstimate(
+            flops=2 * rows * width * columns * blocks,
+            bytes_accessed=blocks * columns * (2 * width + 6 * rows),
+            transcendentals=rows * columns * blocks,
+        ),
+        name="head_backward",
+    )(logits, weights, marks, stats)
+
+
+def head_weights(tops, grads):
+    blocks, rows, columns = grads.shape
+    width = tops.shape[1]
+
+    def kernel(x_ref, g_ref, out_ref, turned):
+        @pl.when(pl.program_id(0) == 0)
+        def _():
+            turned[...] = x_ref[...].T
+
+        out_ref[...] = matmul(turned[...], g_ref[...]).astype(BF)
+
+    return pl.pallas_call(
+        kernel,
+        grid=(blocks,),
+        out_shape=shape((2, blocks // 2, width, columns), BF),
+        in_specs=[
+            pl.BlockSpec((rows, width), lambda k: (0, 0)),
+            pl.BlockSpec((None, rows, columns), lambda k: (k, 0, 0)),
+        ],
+        out_specs=pl.BlockSpec((None, None, width, columns), lambda k: (k % 2, k // 2, 0, 0)),
+        scratch_shapes=[pltpu.VMEM((width, rows), BF)],
+        compiler_params=pltpu.CompilerParams(vmem_limit_bytes=48 * 2**20),
+        cost_estimate=pl.CostEstimate(
+            flops=2 * rows * width * columns * blocks,
+            bytes_accessed=blocks * columns * 2 * (width + rows),
+            transcendentals=0,
+        ),
+        name="head_weights",
+    )(tops, grads)
 
 
 def norm_forward(values, gain):
@@ -581,9 +722,6 @@
     plane_groups = [[k * plane + i for i in range(plane)] for k in range(nz)]
     line_groups = [[k * plane + i for k in range(nz)] for i in range(plane)]
 
-    head_near = lax.all_gather(head_weight.astype(BF), "dp", axis_index_groups=plane_groups)
-    head_near = lax.all_gather(head_near, "seq")
-
     layers = [v.astype(BF) for v in (attend_in, attend_mix, expand_in, shrink_out)]
     tail = jnp.concatenate([labels, heights])
     meta = jnp.concatenate([targets, loss_mask, pad_rows(tail, 4)], axis=0)
@@ -614,6 +752,9 @@
 
     *weights, row_parts, smalls = gather_second(dims, lines, FIRST_AXES, rows, small, 1)
     qkv_w, mix_w, expand_w, shrink_w = (v.reshape(-1, v.shape[-1]) for v in weights)
+    head_low, smalls = lax.optimization_barrier((head_weight.astype(BF), smalls))
+    head_near = lax.all_gather(head_low, "dp", axis_index_groups=plane_groups)
+    head_near = lax.all_gather(head_near, "seq")
     smalls = smalls.reshape(chips * 2, -1)
     class_rows = smalls[:, : 6 * 128].reshape(chips * 2, chips * images, -1)
     class_row = lax.dynamic_slice_in_dim(class_rows, chip * images + core, 1, axis=1).reshape(1, -1)
@@ -643,15 +784,9 @@
     normed_top = normed_top.astype(BF)
 
     tops = line_gather(dims, normed_top, 2, "top_rows").reshape(nz * length, width)
-    head_w = head_near.transpose(2, 1, 0, 3).reshape(width, line_codes)
-    logits = matmul(tops, head_w)
-    local_targets = (line_targets - z * line_codes).reshape(-1, 1)
-    onehot = local_targets == jnp.arange(line_codes)[None, :]
-    peak = jnp.max(logits, axis=1)
-    total = jnp.sum(jnp.exp(logits - peak[:, None]), axis=1)
-    picked = jnp.sum(jnp.where(onehot, logits, 0.0), axis=1)
-    stats = jnp.concatenate([v.reshape(-1, 128) for v in (peak, total, picked)], axis=0)
-    stats = line_gather(dims, stats, 3, "row_stats").reshape(nz, 3, -1)
+    marks = (line_targets - z * line_codes).reshape(-1, 1)
+    logits, stats = head_forward(tops, head_near, marks)
+    stats = line_gather(dims, stats, 3, "row_stats")
     peaks = jnp.max(stats[:, 0], axis=0)
     totals = jnp.sum(stats[:, 1] * jnp.exp(stats[:, 0] - peaks[None, :]), axis=0)
     log_total = peaks + jnp.log(totals)
@@ -659,15 +794,14 @@
     losses = (log_total - jnp.sum(stats[:, 2], axis=0)) * counted
     loss_local = jnp.sum(lax.dynamic_slice_in_dim(losses.reshape(nz, -1), z, 1, axis=0))
     count_local = jnp.sum(lax.dynamic_slice_in_dim(line_counted, z, 1, axis=0))
-    softmax = jnp.exp(logits - peaks[:, None]) / totals[:, None]
-    grad_logits = ((softmax - onehot.astype(F32)) * counted[:, None]).astype(BF)
-    grad_tops = matmul(grad_logits, head_w.T).astype(BF).reshape(nz, length, width)
+    scales = jnp.stack([peaks, counted / totals, counted])
+    scales = jnp.pad(scales, ((0, 5), (0, 0)))
+    grad_logits, grad_tops = head_backward(logits, head_near, marks, scales)
+    grad_tops = grad_tops.reshape(nz, length, width)
     grad_top = lax.psum_scatter(grad_tops, "dp", axis_index_groups=line_groups)
-    grad_head = matmul(tops.T, grad_logits).astype(BF).reshape(width, plane, 2, -1)
-    grad_head = lax.psum_scatter(grad_head, "seq", scatter_dimension=2)
-    grad_head = lax.psum_scatter(
-        grad_head, "dp", scatter_dimension=1, axis_index_groups=plane_groups
-    ).astype(F32)
+    grad_head = head_weights(tops, grad_logits)
+    grad_head = lax.psum_scatter(grad_head, "seq", scatter_dimension=0)
+    grad_head = lax.psum_scatter(grad_head, "dp", axis_index_groups=plane_groups)
 
     grad_final, gain_top = norm_backward(grad_top.astype(F32), norm_top, inverse_top, gain[2])
     back_down = grad_final.astype(BF)
@@ -718,8 +852,6 @@
         code_pick, row_grads, (((0,), (0,)), ((), ())), preferred_element_type=F32
     )
     table_grad = table_grad.astype(BF).reshape(ny, nx, 2, device_codes, width)
-    *layer_shares, code_share = scatter_second(dims, line_grads, table_grad, 5)
-    layer_shares = [g.reshape(v.shape) for g, v in zip(layer_shares, layers)]
     smalls = smalls.reshape(chips * 2, 4, -1)
     device = chip * 2 + core
     small_mine = lax.dynamic_slice_in_dim(smalls, device * gain_columns, gain_columns, axis=2)
@@ -730,12 +862,14 @@
         preferred_element_type=F32,
     )
     gain_share = jnp.sum(small_mine[:, 1:], axis=0)
-    shares = (class_share, code_share, *layer_shares, grad_head, gain_share)
-
-    square_local = sum((jnp.sum(member * member) for member in shares))
-    sums = pad_rows(jnp.stack([square_local, loss_local, count_local]), 8)
-    sums = jnp.sum(all_small(dims, sums, 6, "last_sums").reshape(chips * 2, -1), axis=0)
-    total_square, loss_sum, loss_count = (sums[0], sums[1], sums[2])
+    square_local = jnp.sum(class_share * class_share) + jnp.sum(gain_share * gain_share)
+    partial = pad_rows(jnp.stack([square_local, loss_local, count_local]), 8)
+    *layer_shares, code_share, sums = scatter_second(
+        dims, line_grads, table_grad, grad_head, partial, 5
+    )
+    layer_shares = [g.reshape(v.shape) for g, v in zip(layer_shares, layers)]
+    shares = (class_share, code_share, *layer_shares, grad_head.astype(F32), gain_share)
+    total_square, loss_sum, loss_count = (sums[0, 0], sums[0, 1], sums[0, 2])
     grad_norm = jnp.sqrt(total_square) / loss_count
     factor = CLIP_NORM / jnp.maximum(grad_norm, CLIP_NORM) / loss_count
     news, firsts, seconds = ([], [], [])

time: 605 us -> 602 us (level)
  waiting for transfers between devices: 3.66 us -> 60.9 us
  matrix products: 106 us -> 69.5 us
  Pallas kernels: 341 us -> 374 us
  local copies, waits for them, and re-layouts: 54.7 us -> 27.8 us
  other arithmetic: 68.5 us -> 42.7 us
    pallas_call x0 -> x3, Pallas kernels: none -> 57.1 us  [the longest x1 26.3 us: head_forward(): pl.pallas_call(kernel, grid=(blocks,), out_shape=[shape((blocks, rows, co...]
    all_gather x1, waiting for transfers between devices: 0.01 us -> 39.1 us  [on_device(): head_near = lax.all_gather(head_low, 'dp', axis_index_groups=plane_groups)]
    dot_general x17 -> x14, matrix products: 79.8 us -> 44.4 us  [matmul(): return jnp.dot(left, right, preferred_element_type=F32)]
    pallas_call x7 -> x6, Pallas kernels: 341 us -> 317 us  [call(): pl.pallas_call(kernel, out_shape=outs, in_specs=in_specs, out_specs=out_s...]
    reshape x3 -> x0, local copies, waits for them, and re-layouts: 19.7 us -> none  [the longest x2 18.9 us: on_device(): matmul(tops.T, grad_logits).astype(BF).reshape(width, plane, 2, -1)]
    reduce_scatter x1, waiting for transfers between devices: 3.55 us -> 21.7 us  [on_device(): grad_top = lax.psum_scatter(grad_tops, 'dp', axis_index_groups=line_groups)]
    reduce_sum x9 -> x1, other arithmetic: 15.6 us -> 0.61 us  [on_device(): jnp.sum(gain_share * gain_share)]
    convert_element_type x1 -> x0, other arithmetic: 9.92 us -> none  [on_device(): grad_logits = ((softmax - onehot.astype(F32)) * counted[:, None]).astype(BF)]
  transfers between devices with their start and end apart: 5 -> 5, of which waited for: 1 -> 2; matrix products, arithmetic and copies ran while one was open for 24% -> 14% of each run, Pallas kernels for 52% -> 22%
where the time goes in v2:
time: 602 us; the launch traced here: 596 us
  Pallas kernels  374 us (62%)
  matrix products  69.5 us (12%)
  waiting for transfers between devices  60.9 us (10%)
  other arithmetic  42.7 us (7%)
  local copies, waits for them, and re-layouts  27.8 us (5%)
  between operations  19.8 us (3%)
    pallas_call x6, Pallas kernels, call(): pl.pallas_call(kernel, out_shape=outs, in_specs=in_specs, out_specs=out_s...  317 us
    dot_general x14, matrix products, matmul(): return jnp.dot(left, right, preferred_element_type=F32)  44.4 us
    all_gather x1, waiting for transfers between devices, on_device(): head_near = lax.all_gather(head_low, 'dp', axis_index_groups=plane_groups)  39.1 us
    pallas_call x1, Pallas kernels, head_forward(): pl.pallas_call(kernel, grid=(blocks,), out_shape=[shape((blocks, rows, co...  26.3 us
    reduce_scatter x1, waiting for transfers between devices, on_device(): grad_top = lax.psum_scatter(grad_tops, 'dp', axis_index_groups=line_groups)  21.7 us
    pallas_call x1, Pallas kernels, head_backward(): pl.pallas_call(kernel, grid=(blocks,), out_shape=[shape(logits.shape, BF)...  18.5 us
    unnamed x188, local copies, waits for them, and re-layouts  15.8 us
    sub x8, other arithmetic, adam_update(): return (master - rate * (stride + decay * master), moment, second)  15.2 us
  transfers between devices with their start and end apart: 5, of which 2 were waited for; matrix products, arithmetic and copies ran while one was open for 14% of the time, Pallas kernels for 22%

profile of v2, /device:TPU:0, one launch (start us, length us, event | category | flops | bytes accessed | tf_op | source)
XLA Modules:
  0.0 595.8 jit_solution(3311204233952966894)
XLA Ops:
  15.3 2.4 convert_element_type.185.refs_4_
  19.3 49.7 %gather_first.1 = (bf16[4,24,2304]{2,1,0:T(8,128)(2,1)}, bf16[4,24,768]{2,1,0:T(8,128)(2,1)}, bf16[4,24,4096]{2,1,0:T(8,128)(2,1)}, bf16[4,64,768]{2,1,0:T(8,128...) custom-call(bf16[24,2304]{1,0:T(8,128)(2,1)} %convert_element_type.181.refs_0_, ...), custom_call_target="tpu_custom_call" | custom-call | tf_op jit(solution)/shard_map/gather_first/pallas_call | solution.py:158
  71.3 11.2 %fusion.7 = bf16[1024,768]{1,0:T(8,128)(2,1)} fusion(bf16[4096,768]{1,0:T(8,128)(2,1)} %bitcast.214, s32[1024]{0:T(1024)S(1)} %bitcast.210), kind=kOutput, calls=%fused_computation.23 | convolution fusion | flops 6447431680 | bytes 7868416 | tf_op jit(solution)/shard_map/dot_general | solution.py:474
  83.1 70.3 %gather_second.1 = (bf16[4,2,2,2,24,2304]{5,4,3,2,1,0:T(8,128)(2,1)}, bf16[4,2,2,2,24,768]{5,4,3,2,1,0:T(8,128)(2,1)}, bf16[4,2,2,2,24,4096]{5,4,3,2,1,0:T(8,128...) custom-call(bf16[4,24,2304]{2,1,0:T(8,128)(2,1)} %get-tuple-element., ...), custom_call_target="tpu_custom_call" | custom-call | tf_op jit(solution)/shard_map/gather_second/pallas_call | solution.py:158
  156.6 39.1 %all-gather.5.cloned.1.call-done = bf16[3072,512]{1,0:T(8,128)(2,1)} async-done(((bf16[768,512]{1,0:T(8,128)(2,1)}), bf16[3072,512]{1,0:T(8,128)(2,1)}) %all-gather.5.cloned.1.call-update) | async-done | bytes 3145744 | tf_op jit(solution)/shard_map/all_gather | solution.py:756
  196.9 5.9 copy.81
  204.3 3.8 fusion.36
  210.0 2.8 fusion.100
  212.8 2.7 convolution_convert_fusion.6
  217.6 1.9 fusion.84
  226.1 30.0 %top_rows.1 = bf16[4,256,768]{2,1,0:T(8,128)(2,1)} custom-call(bf16[256,768]{1,0:T(8,128)(2,1)} %multiply_convert_fusion.4.src), custom_call_target="tpu_custom_call" | custom-call | tf_op jit(solution)/shard_map/top_rows/pallas_call | solution.py:158
  257.6 26.3 %head_forward.1 = (f32[8,1024,512]{2,1,0:T(8,128)}, f32[8,1024]{1,0:T(8,128)S(1)}) custom-call(bf16[1024,768]{1,0:T(8,128)(2,1)S(1)} %bitcast.167, bf16[2,4,768,512]{3,2,1,0:T(8,128)(2,1)} %bitcast.212, s32[1024,1]{1,0:T(8,128)S(1)} %copy.85.mark_ref), custom_call_target="tpu_custom_call" | custom-call | flops 6442450944 | bytes 23068672 | tf_op jit(solution)/shard_map/head_forward/pallas_call | solution.py:508
  284.5 14.3 %row_stats.1 = f32[4,8,1024]{2,1,0:T(8,128)} custom-call(f32[8,1024]{1,0:T(8,128)} %copy-done.2), custom_call_target="tpu_custom_call" | custom-call | tf_op jit(solution)/shard_map/row_stats/pallas_call | solution.py:158
  300.0 18.5 %head_backward.1 = (bf16[8,1024,512]{2,1,0:T(8,128)(2,1)}, bf16[1024,768]{1,0:T(8,128)(2,1)}) custom-call(f32[8,1024,512]{2,1,0:T(8,128)} %get-tuple-element.71.l_ref, bf16[2,4,768,512]{3,2,1,0:T(8,128)(2,1)} %bitcast.213, s32[1024,1]{1,0:T(8,128)S(1)} %copy.85.mark_ref, f32[8,1024]{1,0:T(8,128)S(1)} %select_maximum_fusion.stat_ref), custom_call_target="tpu_custom_call" | custom-call | flops 6442450944 | bytes 31457280 | tf_op jit(solution)/shard_map/head_backward/pallas_call | solution.py:557
  318.5 12.4 %head_weights.1 = bf16[2,4,768,512]{3,2,1,0:T(8,128)(2,1)} custom-call(bf16[1024,768]{1,0:T(8,128)(2,1)S(1)} %bitcast.168, bf16[8,1024,512]{2,1,0:T(8,128)(2,1)} %get-tuple-element.80.g_ref), custom_call_target="tpu_custom_call" | custom-call | flops 6442450944 | bytes 14680064 | tf_op jit(solution)/shard_map/head_weights/pallas_call | solution.py:593
  332.1 21.7 %reduce-scatter.6.cloned.1.call-done = bf16[1,256,768]{2,1,0:T(8,128)(2,1)} async-done(((bf16[4,256,768]{2,1,0:T(8,128)(2,1)}), bf16[1,256,768]{2,1,0:T(8,128)(2,1)}) %reduce-scatter.6.cloned.1.call-update) | async-done | bytes 393232 | tf_op jit(solution)/shard_map/reduce_scatter | solution.py:801
  353.9 1.9 fusion.25
  355.8 4.8 multiply_convert_fusion.2
  360.7 6.6 %multiply_reduce_fusion.1 = (f32[768]{0:T(1024)}, f32[256]{0:T(256)S(1)}, f32[256,768]{1,0:T(8,128)S(1)}) fusion(f32[256,768]{1,0:T(8,128)S(1)} %copy-done.6, f32[256]{0:T(256)S(1)} %copy-done.62, f32[768]{0:T(1024)S(1)} %mul.678, bf16[768,4096]{1,0:T(8,128)(2,1)} %bitcast.173, bf16[256,2048]{1,0:T(8,128)(2,1)S(1)} %get-tuple-element.126, ...), kind=kOutput, calls=%fused_computation.72 | convolution fusion | flops 1615985664 | bytes 9969664 | tf_op jit(solution)/shard_map/dot_general | solution.py:474
  369.4 2.9 multiply_reduce_fusion
  385.7 3.0 convolution_convert_fusion.2
  388.8 3.1 convolution_convert_fusion.1
  391.9 4.8 convolution_convert_fusion
  396.7 91.3 %scatter_first.1 = (bf16[4,24,2304]{2,1,0:T(8,128)(2,1)}, bf16[4,24,768]{2,1,0:T(8,128)(2,1)}, bf16[4,24,4096]{2,1,0:T(8,128)(2,1)}, bf16[4,64,768]{2,1,0:T(8,12...) custom-call(bf16[4,2,2,2,24,2304]{5,4,3,2,1,0:T(8,128)(2,1)} %bitcast.170, ...), custom_call_target="tpu_custom_call" | custom-call | tf_op jit(solution)/shard_map/scatter_first/pallas_call | solution.py:158
  492.2 2.0 fusion.67.refs_6_
  494.1 12.0 %fusion.5 = bf16[4096,768]{1,0:T(8,128)(2,1)} fusion(bf16[1024,768]{1,0:T(8,128)(2,1)} %bitcast.217, s32[1024]{0:T(1024)S(1)} %bitcast.211), kind=kOutput, calls=%fused_computation.7 | convolution fusion | flops 6449790976 | bytes 7868416 | tf_op jit(solution)/shard_map/dot_general | solution.py:851
  506.3 61.5 %scatter_second.1 = (f32[24,2304]{1,0:T(8,128)}, f32[24,768]{1,0:T(8,128)}, f32[24,4096]{1,0:T(8,128)}, f32[64,768]{1,0:T(8,128)}, f32[512,768]{1,0:T(8,128)}, /*index=5*/f32[8,128]{1,0:T(8,128)}) custom-call(bf16[4,24,2304]{2,1,0:T(8,128)(2,1)} %get-tuple-element.75.refs_0_, bf16[4,24,768]{2,1,0:T(8,128)(2,1)} %get-tuple-element.76.refs_1_, ...), custom_call_target="tpu_custom_call" | custom-call | tf_op jit(solution)/shard_map/scatter_second/pallas_call | solution.py:158
  574.3 1.9 multiply_subtract_fusion.4
  576.3 2.0 multiply_subtract_fusion.3
  578.3 2.2 multiply_subtract_fusion.2
  580.6 3.0 multiply_subtract_fusion.1
  584.9 3.1 multiply_subtract_fusion
  (292 shorter events, 56.9 us)
Async XLA Ops:
  7.2 10.5 %copy-start.15 = (f32[768,512]{1,0:T(8,128)S(1)}, f32[768,512]{1,0:T(8,128)}, u32[]{:S(2)}) copy-start(f32[768,512]{1,0:T(8,128)} %param.38) | copy-start | bytes 4718596
  7.2 188.4 %all-gather.5.cloned.1.call-start = ((), (), s32[]{:S(2)}) async-start(), calls=%async_computation.5 | async-start | bytes 3932160 | tf_op jit(solution)/shard_map/all_gather | solution.py:756
  17.7 53.3 %copy-start.48 = (f32[1001,24]{0,1:T(8,128)S(1)}, f32[1001,24]{0,1:T(8,128)}, u32[]{:S(2)}) copy-start(f32[1001,24]{0,1:T(8,128)} %param.32) | copy-start | bytes 288292
  71.0 11.5 %copy-start.80 = (s32[1,2,4,128]{3,1,2,0:T(2,128)}, s32[1,2,4,128]{3,1,2,0:T(2,128)S(1)}, u32[]{:S(2)}) copy-start(s32[1,2,4,128]{3,1,2,0:T(2,128)S(1)} %copy.103) | copy-start | bytes 12292
  153.4 102.8 %all-gather.7.cloned.1.call-start = ((), (), s32[]{:S(2)}) async-start(), calls=%async_computation.6 | async-start | bytes 9437184 | tf_op jit(solution)/shard_map/all_gather | solution.py:757
  195.6 158.2 %reduce-scatter.6.cloned.1.call-start = ((), (), s32[]{:S(2)}) async-start(), calls=%async_computation.3 | async-start | bytes 1966080 | tf_op jit(solution)/shard_map/reduce_scatter | solution.py:801
  202.8 12.7 %copy-start.69 = (pred[256]{0:T(512)(128)(4,1)}, pred[256]{0:T(512)(128)(4,1)S(1)}, u32[]{:S(2)}) copy-start(pred[256]{0:T(512)(128)(4,1)S(1)} %iota_compare_fusion.15) | copy-start | bytes 772
  224.4 131.4 %copy-start.64 = (f32[256]{0:T(256)}, f32[256]{0:T(256)S(1)}, u32[]{:S(2)}) copy-start(f32[256]{0:T(256)S(1)} %add_rsqrt_fusion) | copy-start | bytes 3076
  300.0 18.6 %copy-start.1 = (bf16[4,256,768]{2,1,0:T(8,128)(2,1)S(1)}, bf16[4,256,768]{2,1,0:T(8,128)(2,1)}, u32[]{:S(2)}) copy-start(bf16[4,256,768]{2,1,0:T(8,128)(2,1)} %top_rows.1) | copy-start | bytes 4718596
  318.5 56.6 %reduce-scatter.8.cloned.1.call-start = ((), (), s32[]{:S(2)}) async-start(), calls=%async_computation.4 | async-start | bytes 9437184 | tf_op jit(solution)/shard_map/reduce_scatter | solution.py:803
  330.9 22.9 %copy-start.8 = (f32[256,768]{1,0:T(8,128)S(1)}, f32[256,768]{1,0:T(8,128)}, u32[]{:S(2)}) copy-start(f32[256,768]{1,0:T(8,128)} %copy-done.7) | copy-start | bytes 2359300
  331.0 175.1 %reduce-scatter.10.cloned.1.call-start = ((), (), s32[]{:S(2)}) async-start(), calls=%async_computation.7 | async-start | bytes 3932160
  355.8 11.5 %copy-start.76 = (f32[256]{0:T(256)}, f32[256]{0:T(256)S(1)}, u32[]{:S(2)}) copy-start(f32[256]{0:T(256)S(1)} %broadcast_multiply_fusion.6) | copy-start | bytes 3076
  396.7 93.3 %copy-start.83 = (s32[32]{0:T(128)S(1)}, s32[32]{0:T(128)}, u32[]{:S(2)}) copy-start(s32[32]{0:T(128)} %copy-done.82) | copy-start | bytes 388
  396.7 97.5 %copy-start.81 = (s32[1,2,4,128]{3,1,2,0:T(2,128)S(1)}, s32[1,2,4,128]{3,1,2,0:T(2,128)}, u32[]{:S(2)}) copy-start(s32[1,2,4,128]{3,1,2,0:T(2,128)} %copy-done.80) | copy-start | bytes 12292
  506.1 65.2 %copy-start.78 = (f32[3,24]{1,0:T(4,128)S(1)}, f32[3,24]{1,0:T(4,128)}, u32[]{:S(2)}) copy-start(f32[3,24]{1,0:T(4,128)} %param.39) | copy-start | bytes 868
  506.1 65.2 %copy-start.84 = (f32[3,24]{1,0:T(4,128)S(1)}, f32[3,24]{1,0:T(4,128)}, u32[]{:S(2)}) copy-start(f32[3,24]{1,0:T(4,128)} %param.47) | copy-start | bytes 868
  506.1 65.2 %copy-start.85 = (f32[3,24]{1,0:T(4,128)S(1)}, f32[3,24]{1,0:T(4,128)}, u32[]{:S(2)}) copy-start(f32[3,24]{1,0:T(4,128)} %param.55) | copy-start | bytes 868
  506.1 65.8 %copy-start.52 = (f32[24,768]{1,0:T(8,128)S(1)}, f32[24,768]{1,0:T(8,128)}, u32[]{:S(2)}) copy-start(f32[24,768]{1,0:T(8,128)} %param.35) | copy-start | bytes 221188
  506.1 65.8 %copy-start.59 = (f32[24,768]{1,0:T(8,128)S(1)}, f32[24,768]{1,0:T(8,128)}, u32[]{:S(2)}) copy-start(f32[24,768]{1,0:T(8,128)} %param.43) | copy-start | bytes 221188
  506.1 65.8 %copy-start.60 = (f32[24,768]{1,0:T(8,128)S(1)}, f32[24,768]{1,0:T(8,128)}, u32[]{:S(2)}) copy-start(f32[24,768]{1,0:T(8,128)} %param.51) | copy-start | bytes 221188
  506.1 67.4 %copy-start.49 = (f32[1001,24]{0,1:T(8,128)S(1)}, f32[1001,24]{0,1:T(8,128)}, u32[]{:S(2)}) copy-start(f32[1001,24]{0,1:T(8,128)} %param.32) | copy-start | bytes 288292
  506.2 67.4 %copy-start.57 = (f32[1001,24]{0,1:T(8,128)S(1)}, f32[1001,24]{0,1:T(8,128)}, u32[]{:S(2)}) copy-start(f32[1001,24]{0,1:T(8,128)} %param.40) | copy-start | bytes 288292
  506.2 67.4 %copy-start.58 = (f32[1001,24]{0,1:T(8,128)S(1)}, f32[1001,24]{0,1:T(8,128)}, u32[]{:S(2)}) copy-start(f32[1001,24]{0,1:T(8,128)} %param.48) | copy-start | bytes 288292
  506.2 68.1 %copy-start.42 = (f32[64,768]{1,0:T(8,128)S(1)}, f32[64,768]{1,0:T(8,128)}, u32[]{:S(2)}) copy-start(f32[64,768]{1,0:T(8,128)} %param.37) | copy-start | bytes 589828
  506.2 68.1 %copy-start.55 = (f32[64,768]{1,0:T(8,128)S(1)}, f32[64,768]{1,0:T(8,128)}, u32[]{:S(2)}) copy-start(f32[64,768]{1,0:T(8,128)} %param.45) | copy-start | bytes 589828
  506.2 68.1 %copy-start.56 = (f32[64,768]{1,0:T(8,128)S(1)}, f32[64,768]{1,0:T(8,128)}, u32[]{:S(2)}) copy-start(f32[64,768]{1,0:T(8,128)} %param.53) | copy-start | bytes 589828
  506.2 70.1 %copy-start.53 = (f32[24,2304]{1,0:T(8,128)S(1)}, f32[24,2304]{1,0:T(8,128)}, u32[]{:S(2)}) copy-start(f32[24,2304]{1,0:T(8,128)} %param.42) | copy-start | bytes 663556
  506.2 70.0 %copy-start.54 = (f32[24,2304]{1,0:T(8,128)S(1)}, f32[24,2304]{1,0:T(8,128)}, u32[]{:S(2)}) copy-start(f32[24,2304]{1,0:T(8,128)} %param.50) | copy-start | bytes 663556
  506.2 72.1 %copy-start.50 = (f32[24,4096]{1,0:T(8,128)S(1)}, f32[24,4096]{1,0:T(8,128)}, u32[]{:S(2)}) copy-start(f32[24,4096]{1,0:T(8,128)} %param.44) | copy-start | bytes 1179652
  506.3 72.1 %copy-start.51 = (f32[24,4096]{1,0:T(8,128)S(1)}, f32[24,4096]{1,0:T(8,128)}, u32[]{:S(2)}) copy-start(f32[24,4096]{1,0:T(8,128)} %param.52) | copy-start | bytes 1179652
  567.8 10.5 %copy-start.30 = (f32[24,4096]{1,0:T(8,128)S(1)}, f32[24,4096]{1,0:T(8,128)}, u32[]{:S(2)}) copy-start(f32[24,4096]{1,0:T(8,128)} %param.36) | copy-start | bytes 1179652
  (64 other events, 205.6 us)
Sparse Core Ops, SparseCore 0:
  153.6 42.0 all-gather.4
  197.2 16.7 all-gather.6
  318.6 35.1 reduce-scatter.5
  356.0 13.4 reduce-scatter.7
  375.2 51.3 reduce-scatter.9

commit v3 on v2

--- a/solution.py
+++ b/solution.py
@@ -109,41 +109,87 @@
         self.held.append(copy)
         return copy
 
-    def finish(self, but=()):
+    def done(self, copy):
+        copy.wait()
+        self.held = [other for other in self.held if other is not copy]
+
+    def finish(self):
         for copy in self.sent:
             copy.wait_send()
         for copy in self.held:
-            if copy not in but:
-                copy.wait()
-
-
-def small_gather(comm, place, src, out):
+            copy.wait()
+
+
+def all_offsets(dims):
+    nz, ny, nx = dims
+    spots = [(k, j, i, core) for k in range(nz) for j in range(ny) for i in range(nx) for core in range(2)]
+    return spots[1:]
+
+
+def small_exchange(comm, place, src, out, own):
+    z, y, x, c = (place.z, place.y, place.x, place.c)
     nz, ny, nx = place.dims
-    z, y, x, c = (place.z, place.y, place.x, place.c)
-    mine = comm.keep(src, out.at[z, y, x, c])
-    comm.held.remove(mine)
-    got = [comm.send(src, out.at[z, y, x, c], place.dev(c=1))]
-    yield
-    for copy in got:
-        copy.wait_recv()
-    mine.wait()
-    got = [comm.send(out.at[z, y, x], out.at[z, y, x], place.dev(x=t)) for t in range(1, nx)]
-    yield
-    for copy in got:
-        copy.wait_recv()
-    got = [comm.send(out.at[z, y], out.at[z, y], place.dev(y=t)) for t in range(1, ny)]
-    yield
-    for copy in got:
-        copy.wait_recv()
-    got = [comm.send(out.at[z], out.at[z], place.dev(z=t)) for t in range(1, nz)]
-    yield
-    for copy in got:
-        copy.wait_recv()
-
-
-def drain(stages):
-    for _ in stages:
-        pass
+    if own:
+        comm.keep(src(z, y, x, c), out.at[z, y, x, c])
+    got = []
+    for off in all_offsets(place.dims):
+        there = (place.zs(nz - off[0]), place.ys(ny - off[1]), place.xs(nx - off[2]), (c + off[3]) % 2)
+        got.append(comm.send(src(*there), out.at[z, y, x, c], place.dev(*off)))
+    return got
+
+
+class PlaneGather:
+    def __init__(self, comm, place):
+        self.comm, self.place = (comm, place)
+        self.firsts, self.seconds, self.mates = ([], [], [])
+
+    def ways(self, axis):
+        _, ny, nx = self.place.dims
+        return range(1, ny if axis == "y" else nx)
+
+    def back(self, axis, t, yy, xx):
+        return (self.place.ys(t), xx) if axis == "y" else (yy, self.place.xs(t))
+
+    def spread(self, block, first, src=None):
+        place, second = (self.place, "y" if first == "x" else "x")
+        dst = block(place.y, place.x)
+        src = dst if src is None else src
+        for t in self.ways(first):
+            copy = self.comm.send(src, dst, place.dev(**{first: t}))
+            self.firsts.append((block, first, second, t, copy))
+        for t in self.ways(second):
+            copy = self.comm.send(src, dst, place.dev(**{second: t}))
+            self.seconds.append((block(*self.back(second, t, place.y, place.x)), copy))
+        self.mates.append(self.comm.send(src, dst, place.dev(c=1)))
+
+    def forward(self):
+        place = self.place
+        for block, first, second, t, copy in self.firsts:
+            copy.wait_recv()
+            yy, xx = self.back(first, t, place.y, place.x)
+            held = block(yy, xx)
+            for u in self.ways(second):
+                copy = self.comm.send(held, held, place.dev(**{second: u}))
+                self.seconds.append((block(*self.back(second, u, yy, xx)), copy))
+            self.mates.append(self.comm.send(held, held, place.dev(c=1)))
+        self.firsts = []
+
+    def settle(self):
+        for held, copy in self.seconds:
+            copy.wait_recv()
+            self.mates.append(self.comm.send(held, held, self.place.dev(c=1)))
+        self.seconds = []
+
+    def forward_some(self, count):
+        rest = self.firsts[count:]
+        self.firsts = self.firsts[:count]
+        self.forward()
+        self.firsts = rest
+
+    def arrive(self):
+        for copy in self.mates:
+            copy.wait_recv()
+        self.mates = []
 
 
 def sems(count):
@@ -169,116 +215,164 @@
 
 
 def small_sends(dims):
-    return sum(dims) - 2
-
-
-def gather_first(dims, layers, table, meta, cid):
+    return dims[0] * dims[1] * dims[2] * 2 - 1
+
+
+def gather_all(dims, layers, first_axes, table, classes, gains, meta, images, cid):
     nz, ny, nx = dims
     n = len(layers)
+    rows, width = table.shape
+    length = meta.shape[1] * 2
+    count_images = nz * ny * nx * images
+    label_rows = -(-count_images // 128)
+    groups = [(k,) for k in range(nz)] if nz <= 4 else [tuple(range(nz))]
 
     def kernel(*refs):
-        ins, rest = (refs[: n + 2], refs[n + 2 :])
-        outs, (ssem, rsem, lsem) = (rest[: n + 2], rest[n + 2 :])
+        ins, rest = (refs[:n], refs[n:])
+        table_in, class_in, gain_in, meta_in, *rest = rest
+        outs, rest = (rest[:n], rest[n:])
+        parts_out, meta_out, small_out, *rest = rest
+        low, rest = (rest[:n], rest[n:])
+        whole, found, total, class_low, gain_row, small_in, ssem, rsem, lsem = rest
         place = Place(dims)
         z, y, x, c = (place.z, place.y, place.x, place.c)
-        greet(place, line_offsets(dims) + plane_offsets(dims))
+        greet(place, all_offsets(dims))
         comm = Comm(ssem, rsem, lsem)
-        small = small_gather(comm, place, ins[n + 1], outs[n + 1])
-        next(small)
-        tab, whole = (ins[n], outs[n])
-        slot = whole.at[y, x, c]
-        near = [
-            (off, comm.send(tab, slot, place.dev(*off))) for off in plane_offsets(dims)
-        ]
+        metas = small_exchange(comm, place, lambda *spot: meta_in, meta_out, False)
+        meta_out[z, y, x, c] = meta_in[...]
         waits = []
+        whole[y, x, c] = table_in[...].astype(BF)
+        tables, blocks = (PlaneGather(comm, place), PlaneGather(comm, place))
+        for first, start in (("x", 0), ("y", rows // 2)):
+            half = pl.ds(start, rows // 2)
+            tables.spread(lambda yy, xx, half=half: whole.at[yy, xx, c, half], first)
         for a in range(n):
-            comm.keep(ins[a], outs[a].at[z])
-            for s in range(1, nz):
-                waits.append(comm.send(ins[a], outs[a].at[z], place.dev(z=s)))
-        comm.keep(tab, slot)
-        waits.append(comm.send(tab, slot, place.dev(c=1)))
-        next(small)
-        next(small)
-        next(small)
-        for off, copy in near:
+            low[a][...] = ins[a][...].astype(BF)
+        along = {}
+        for s in range(1, nz):
+            for a in range(n):
+                along[s, a] = comm.send(low[a], outs[a].at[z, y, x, c], place.dev(z=s))
+        kept = [comm.keep(low[a], outs[a].at[z, y, x, c]) for a in range(n)]
+
+        def spread(group):
+            for a in range(n):
+                for k in group:
+                    if k:
+                        along[k, a].wait_recv()
+                if len(group) > 1:
+                    comm.done(kept[a])
+                    at = pl.ds(0, nz)
+                else:
+                    at = place.zs(group[0])
+                blocks.spread(
+                    lambda yy, xx, a=a, at=at: outs[a].at[at, yy, xx, c],
+                    first_axes[a],
+                    low[a] if group == (0,) else None,
+                )
+
+        for copy in metas:
             copy.wait_recv()
-            block = whole.at[place.ys(off[1]), place.xs(off[2]), c]
-            waits.append(comm.send(block, block, place.dev(c=1)))
-        drain(small)
+
+        class_low[...] = jnp.zeros_like(class_low)
+        class_low[0 : class_in.shape[0], 0 : class_in.shape[1]] = class_in[...]
+        small_in[...] = jnp.zeros_like(small_in)
+        for r in range(label_rows):
+            labels = jnp.zeros((1, 128), jnp.int32)
+            for k in range(nz * ny * nx):
+                labels = labels + meta_out[k // (ny * nx), k // nx % ny, k % nx, 0, 5 + r : 6 + r, :]
+            pick = lax.broadcasted_iota(jnp.int32, (class_low.shape[0], 128), 0) == labels
+            picked = lax.dot_general(
+                jnp.where(pick, 1.0, 0.0).astype(BF),
+                class_low[...].astype(BF),
+                (((0,), (0,)), ((), ())),
+                preferred_element_type=F32,
+            )
+            for i in range(min(128, count_images - 128 * r)):
+                k, core = divmod(128 * r + i, 2)
+                small_in[k // (ny * nx), k // nx % ny, k % nx, core, 0:1, :] = picked[i : i + 1]
+        gain_row[...] = jnp.zeros_like(gain_row)
+        gain_row[0:3, 0 : gain_in.shape[1]] = gain_in[...].astype(BF).astype(F32)
+
+        @pl.loop(0, nz)
+        def _(k):
+            for j in range(ny):
+                for i in range(nx):
+                    for core in range(2):
+                        small_in[k, j, i, core, 1:4, :] = gain_row[0:3]
+
+        waits += small_exchange(comm, place, lambda *spot: small_in.at[spot], small_out, True)
+
+        size = len(layers)
+        steps = [lambda group=group: spread(group) for group in groups]
+        steps.pop(0)()
+        tables.forward()
+        if steps:
+            steps.pop(0)()
+        blocks.forward_some(size)
+        if steps:
+            steps.pop(0)()
+        tables.settle()
+        blocks.forward_some(size)
+        for step in steps:
+            step()
+        tables.arrive()
+
+        for s in range(1, nz + 1):
+            zz = place.zs(s % nz)
+            columns = []
+            for half in range(2):
+                codes = meta_out[zz, y, x, half, pl.ds(c, 1), :].astype(F32)
+                columns.append(jnp.broadcast_to(codes, (128, meta.shape[1])).T)
+            column = jnp.concatenate(columns, axis=0)
+            column = column - (z * ny * nx * 2 * rows).astype(F32)
+            total[...] = jnp.zeros_like(total)
+
+            @pl.loop(0, ny * nx * 2)
+            def _(j):
+                base = (j * rows).astype(F32)
+                lane = lax.broadcasted_iota(jnp.int32, (length, 128), 1).astype(F32) + base
+                picks = [
+                    jnp.where(column == lane + float(128 * q), 1.0, 0.0).astype(BF)
+                    for q in range(-(-rows // 128))
+                ]
+                pick = jnp.concatenate(picks, axis=1)[:, :rows]
+                total[...] += matmul(pick, whole[j // (2 * nx), j // 2 % nx, j % 2])
+
+            found[s % nz] = total[...].astype(BF)
+            if s < nz:
+                waits.append(comm.send(found.at[s], parts_out.at[nz - s], place.dev(z=nz - s)))
+            blocks.forward_some(size)
+        comm.keep(found.at[0], parts_out.at[0])
+        blocks.forward()
+        blocks.settle()
+        blocks.arrive()
         for copy in waits:
             copy.wait_recv()
         comm.finish()
 
-    count = n * (nz - 1) + 2 * ny * nx + small_sends(dims)
-    outs = [shape((nz,) + v.shape, v.dtype) for v in layers]
-    outs += [shape((ny, nx, 2) + table.shape, table.dtype), shape(dims + (2,) + meta.shape, meta.dtype)]
+    count = n * (nz - 1) + (n * len(groups) + 2) * (2 * ny * nx - 1) + nz + 2 * small_sends(dims)
+    small = dims + (2, 8, 128)
+    outs = [shape(dims + (2,) + v.shape, BF) for v in layers]
+    outs += [
+        shape((nz, length, width), BF),
+        shape(dims + (2,) + meta.shape, meta.dtype),
+        shape(small, F32),
+    ]
+    scratch = [pltpu.VMEM(v.shape, BF) for v in layers]
+    scratch += [
+        pltpu.VMEM((ny, nx, 2) + table.shape, BF),
+        pltpu.VMEM((nz, length, width), BF),
+        pltpu.VMEM((length, width), F32),
+        pltpu.VMEM((-(-classes.shape[0] // 128) * 128, 128), F32),
+        pltpu.VMEM((8, 128), F32),
+        pltpu.VMEM(small, F32),
+        sems(count),
+        sems(count),
+        sems(n + 3),
+    ]
     return call(
-        kernel, outs, [ANY] * (n + 2), [ANY] * (n + 2), [sems(count), sems(count), sems(n + 2)],
-        cid, "gather_first", (*layers, table, meta),
-    )
-
-
-def gather_second(dims, lines, first_axes, rows, small, cid):
-    nz, ny, nx = dims
-    n = len(lines)
-    parts = 2 if nz <= 4 else 1
-    step = nz // parts
-
-    def kernel(*refs):
-        ins, rest = (refs[: n + 2], refs[n + 2 :])
-        outs, (ssem, rsem, lsem) = (rest[: n + 2], rest[n + 2 :])
-        place = Place(dims)
-        z, y, x, c = (place.z, place.y, place.x, place.c)
-        greet(place, line_offsets(dims))
-        comm = Comm(ssem, rsem, lsem)
-        gather = small_gather(comm, place, ins[n + 1], outs[n + 1])
-        next(gather)
-        waits = []
-        for s in range(1, nz):
-            waits.append(comm.send(ins[n].at[place.zs(nz - s)], outs[n].at[z], place.dev(z=s)))
-        comm.keep(ins[n].at[z], outs[n].at[z])
-        firsts, seconds = ([], [])
-        for g in range(parts):
-            span = pl.ds(g * step, step)
-            for a in range(n):
-                src, dst = (ins[a].at[span], outs[a].at[span, y, x, c])
-                comm.keep(src, dst)
-                waits.append(comm.send(src, dst, place.dev(c=1)))
-                first = first_axes[a]
-                second = "y" if first == "x" else "x"
-                sizes = {"x": nx, "y": ny}
-                for t in range(1, sizes[first]):
-                    firsts.append((a, span, first, second, sizes[second], t, comm.send(src, dst, place.dev(**{first: t}))))
-                for t in range(1, sizes[second]):
-                    yy, xx = (place.ys(t), x) if second == "y" else (y, place.xs(t))
-                    seconds.append((a, span, yy, xx, comm.send(src, dst, place.dev(**{second: t}))))
-        next(gather)
-        next(gather)
-        next(gather)
-        for a, span, first, second, size, t, copy in firsts:
-            copy.wait_recv()
-            yy, xx = (place.ys(t), x) if first == "y" else (y, place.xs(t))
-            block = outs[a].at[span, yy, xx, c]
-            for u in range(1, size):
-                y2, x2 = (place.ys(u), xx) if second == "y" else (yy, place.xs(u))
-                seconds.append((a, span, y2, x2, comm.send(block, block, place.dev(**{second: u}))))
-            waits.append(comm.send(block, block, place.dev(c=1)))
-        drain(gather)
-        for a, span, yy, xx, copy in seconds:
-            copy.wait_recv()
-            block = outs[a].at[span, yy, xx, c]
-            waits.append(comm.send(block, block, place.dev(c=1)))
-        for copy in waits:
-            copy.wait_recv()
-        comm.finish()
-
-    count = n * parts * (2 * ny * nx - 1) + nz + small_sends(dims)
-    outs = [shape(dims + (2,) + v.shape[1:], v.dtype) for v in lines]
-    outs += [shape(rows.shape, rows.dtype), shape(dims + (2,) + small.shape, small.dtype)]
-    return call(
-        kernel, outs, [ANY] * (n + 2), [ANY] * (n + 2),
-        [sems(count), sems(count), sems(n * parts + 2)],
-        cid, "gather_second", (*lines, rows, small),
+        kernel, outs, [VMEM] * (n + 4), [ANY] * (n + 1) + [VMEM] * 2, scratch,
+        cid, "gather_all", (*layers, table, classes, gains, meta), 60 * 2**20,
     )
 
 
@@ -301,6 +395,40 @@
     )
 
 
+def head_gather(dims, block, head, cid):
+    nz, ny, nx = dims
+    rows = head.shape[0]
+
+    def kernel(src, head_in, out, whole, low, ssem, rsem, lsem):
+        place = Place(dims)
+        z, y, x, c = (place.z, place.y, place.x, place.c)
+        greet(place, line_offsets(dims))
+        comm = Comm(ssem, rsem, lsem)
+        low[...] = head_in[...].astype(BF)
+        comm.keep(low, whole.at[c, y, x])
+        gather = PlaneGather(comm, place)
+        for first, start in (("x", 0), ("y", rows // 2)):
+            half = pl.ds(start, rows // 2)
+            gather.spread(lambda yy, xx, half=half: whole.at[c, yy, xx, half], first, low.at[half])
+        waits = [comm.send(src, out.at[z], place.dev(z=s)) for s in range(1, nz)]
+        comm.keep(src, out.at[z])
+        gather.forward()
+        gather.settle()
+        gather.arrive()
+        for copy in waits:
+            copy.wait_recv()
+        comm.finish()
+
+    count = nz + 2 * (2 * ny * nx - 1)
+    return call(
+        kernel,
+        [shape((nz,) + block.shape, BF), shape((2, ny, nx) + head.shape, BF)],
+        [ANY, VMEM], [ANY, ANY],
+        [pltpu.VMEM(head.shape, BF), sems(count), sems(count), sems(2)],
+        cid, "head_gather", (block, head), 48 * 2**20,
+    )
+
+
 def add_blocks(out, terms):
     lead = out.shape[:-2]
 
@@ -312,6 +440,9 @@
                 visit(index + (i,))
 
         else:
+            if len(terms) == 2 and out.dtype == BF:
+                out[index] = terms[0][index] + terms[1][index]
+                return
             total = terms[0][index].astype(F32)
             for term in terms[1:]:
                 total = total + term[index].astype(F32)
@@ -320,135 +451,153 @@
     visit(())
 
 
-def scatter_first(dims, grads, first_axes, rows, small, cid):
+def scatter_all(dims, grads, first_axes, rows, codes, head, small, same, partial, device_codes, cid):
     nz, ny, nx = dims
     n = len(grads)
+    length, width = rows.shape
+    block = (device_codes, width)
+    parts = 2 if nz <= 4 else 1
+    step = nz // parts
+    items = [(a, g) for g in range(parts) for a in range(n)]
 
     def kernel(*refs):
-        ins, rest = (refs[: n + 2], refs[n + 2 :])
-        outs, rest = (rest[: n + 2], rest[n + 2 :])
-        halves, ones, twos, (ssem, rsem, lsem) = (
-            rest[:n], rest[n : 2 * n], rest[2 * n : 3 * n], rest[3 * n :]
+        ins, rest = (refs[:n], refs[n:])
+        rows_in, codes_in, head_in, small_in, same_in, partial_in, *rest = rest
+        outs, rest = (rest[:n], rest[n:])
+        table_out, small_out, sums, *rest = rest
+        halves, ones, twos, threes, rest = (
+            rest[:n], rest[n : 2 * n], rest[2 * n : 3 * n], rest[3 * n : 4 * n], rest[4 * n :]
         )
-        place = Place(dims)
-        z, y, x, c = (place.z, place.y, place.x, place.c)
-        greet(place, line_offsets(dims))
-        comm = Comm(ssem, rsem, lsem)
-        gather = small_gather(comm, place, ins[n + 1], outs[n + 1])
-        pair = []
-        for a in range(n):
-            pair.append(comm.send(ins[a].at[:, :, :, 1 - c], halves[a], place.dev(c=1)))
-        next(gather)
-        waits = [comm.send(ins[n], outs[n].at[z], place.dev(z=s)) for s in range(1, nz)]
-        comm.keep(ins[n], outs[n].at[z])
-        got_one = []
-        for a in range(n):
-            pair[a].wait_recv()
-            add_blocks(halves[a], [halves[a], ins[a].at[:, :, :, c]])
-            if first_axes[a] == "y":
-                got_one.append([
-                    comm.send(halves[a].at[:, place.ys(ny - t)], ones[a].at[t - 1], place.dev(y=t))
-                    for t in range(1, ny)
-                ])
-            else:
-                got_one.append([
-                    comm.send(halves[a].at[:, :, place.xs(nx - t)], ones[a].at[t - 1], place.dev(x=t))
-                    for t in range(1, nx)
-                ])
-        next(gather)
-        next(gather)
-        next(gather)
-        got_two = []
-        for a in range(n):
-            for copy in got_one[a]:
-                copy.wait_recv()
-            if first_axes[a] == "y":
-                mine = halves[a].at[:, y]
-                add_blocks(mine, [mine] + [ones[a].at[t] for t in range(ny - 1)])
-                got_two.append([
-                    comm.send(halves[a].at[:, y, place.xs(nx - t)], twos[a].at[t - 1], place.dev(x=t))
-                    for t in range(1, nx)
-                ])
-            else:
-                mine = halves[a].at[:, :, x]
-                add_blocks(mine, [mine] + [ones[a].at[t] for t in range(nx - 1)])
-                got_two.append([
-                    comm.send(halves[a].at[:, place.ys(ny - t), x], twos[a].at[t - 1], place.dev(y=t))
-                    for t in range(1, ny)
-                ])
-        drain(gather)
-        for a in range(n):
-            for copy in got_two[a]:
-                copy.wait_recv()
-            terms = [twos[a].at[t] for t in range(twos[a].shape[0])]
-            add_blocks(outs[a], [halves[a].at[:, y, x]] + terms)
-        for copy in waits:
-            copy.wait_recv()
-        comm.finish()
-
-    count = n * (ny + nx - 1) + nz + small_sends(dims)
-    scratch = [pltpu.VMEM((nz, ny, nx) + g.shape[4:], g.dtype) for g in grads]
-    for g, axis in zip(grads, first_axes):
-        near, far = (ny, nx) if axis == "y" else (nx, ny)
-        scratch.append(pltpu.VMEM((near - 1, nz, far) + g.shape[4:], g.dtype))
-    for g, axis in zip(grads, first_axes):
-        scratch.append(pltpu.VMEM(((nx if axis == "y" else ny) - 1, nz) + g.shape[4:], g.dtype))
-    outs = [shape((nz,) + g.shape[4:], g.dtype) for g in grads]
-    outs += [shape((nz,) + rows.shape, rows.dtype), shape(dims + (2,) + small.shape, small.dtype)]
-    return call(
-        kernel, outs, [VMEM] * n + [ANY] * 2, [VMEM] * n + [ANY] * 2,
-        scratch + [sems(count), sems(count), sems(2)],
-        cid, "scatter_first", (*grads, rows, small), 60 * 2**20,
-    )
-
-
-def scatter_second(dims, lines, table, head, partial, cid):
-    nz, ny, nx = dims
-    n = len(lines)
-    block = table.shape[3:]
-
-    def kernel(*refs):
-        ins, rest = (refs[: n + 3], refs[n + 3 :])
-        outs, rest = (rest[: n + 2], rest[n + 2 :])
-        got, (half, near, mine, every, ssem, rsem, lsem) = (rest[:n], rest[n:])
+        lined, given, own, half, near, tops, mixed, mine, every, ssem, rsem, lsem = rest
         place = Place(dims)
         z, y, x, c = (place.z, place.y, place.x, place.c)
         offsets = plane_offsets(dims)
-        greet(place, line_offsets(dims) + offsets)
+        greet(place, all_offsets(dims))
         comm = Comm(ssem, rsem, lsem)
-        pair = comm.send(ins[n].at[:, :, 1 - c], half, place.dev(c=1))
-        lines_in = [
-            [
-                comm.send(ins[a].at[place.zs(nz - s)], got[a].at[s - 1], place.dev(z=s))
-                for s in range(1, nz)
-            ]
-            for a in range(n)
-        ]
-        pair.wait_recv()
-        add_blocks(half, [half, ins[n].at[:, :, c]])
+        pair, got_one, got_two = ({}, {}, {})
+        waits = small_exchange(comm, place, lambda *spot: small_in.at[spot], small_out, True)
+        for a, g in items:
+            span = pl.ds(g * step, step)
+            pair[a, g] = comm.send(ins[a].at[span, :, :, 1 - c], halves[a].at[span], place.dev(c=1))
+        lines = [comm.send(rows_in, lined.at[s], place.dev(z=s)) for s in range(1, nz)]
+        lined[0] = rows_in[...]
+
+        def first_step(a, g):
+            span = pl.ds(g * step, step)
+            pair[a, g].wait_recv()
+            add_blocks(halves[a].at[span], [halves[a].at[span], ins[a].at[span, :, :, c]])
+            if first_axes[a] == "y":
+                got_one[a, g] = [
+                    comm.send(halves[a].at[span, place.ys(ny - t)], ones[a].at[t - 1, span], place.dev(y=t))
+                    for t in range(1, ny)
+                ]
+            else:
+                got_one[a, g] = [
+                    comm.send(halves[a].at[span, :, place.xs(nx - t)], ones[a].at[t - 1, span], place.dev(x=t))
+                    for t in range(1, nx)
+                ]
+
+        def second_step(a, g):
+            span = pl.ds(g * step, step)
+            for copy in got_one[a, g]:
+                copy.wait_recv()
+            if first_axes[a] == "y":
+                held = halves[a].at[span, y]
+                add_blocks(held, [held] + [ones[a].at[t, span] for t in range(ny - 1)])
+                got_two[a, g] = [
+                    comm.send(halves[a].at[span, y, place.xs(nx - t)], twos[a].at[t - 1, span], place.dev(x=t))
+                    for t in range(1, nx)
+                ]
+            else:
+                held = halves[a].at[span, :, x]
+                add_blocks(held, [held] + [ones[a].at[t, span] for t in range(nx - 1)])
+                got_two[a, g] = [
+                    comm.send(halves[a].at[span, place.ys(ny - t), x], twos[a].at[t - 1, span], place.dev(y=t))
+                    for t in range(1, ny)
+                ]
+
+        for a, g in items:
+            first_step(a, g)
+        for a, g in items[: len(items) // 2]:
+            second_step(a, g)
+
+        for copy in lines:
+            copy.wait_recv()
+        held_codes = codes_in[...]
+        flat = jnp.concatenate([held_codes[k : k + 1] for k in range(nz * length // 128)], axis=1)
+
+        def product(into, core):
+            @pl.loop(0, ny * nx)
+            def _(j):
+                code = lax.broadcasted_iota(jnp.int32, (device_codes, nz * length), 0)
+                pick = code + (j * 2 + core) * device_codes == flat
+                pick = jnp.where(pick, 1.0, 0.0).astype(BF)
+                value = matmul(pick, lined[...].reshape(nz * length, width))
+                into[j // nx, j % nx] = value.astype(BF)
+
+        product(given, 1 - c)
+        table_pair = comm.send(given, half, place.dev(c=1))
+        product(own, c)
+        for a, g in items[len(items) // 2 :]:
+            second_step(a, g)
+        table_pair.wait_recv()
+        add_blocks(half, [half, own])
         arriving = [
             comm.send(half.at[place.ys(ny - off[1]), place.xs(nx - off[2])], near.at[k], place.dev(*off))
             for k, off in enumerate(offsets)
         ]
-        share = ins[n + 1][...].astype(F32)
-        square = jnp.sum(share * share)
+
+        third = {}
         for a in range(n):
-            for copy in lines_in[a]:
+            for g in range(parts):
+                span = pl.ds(g * step, step)
+                for copy in got_two[a, g]:
+                    copy.wait_recv()
+                held = halves[a].at[span, y, x]
+                add_blocks(held, [held] + [twos[a].at[t, span] for t in range(twos[a].shape[0])])
+            third[a] = [
+                comm.send(halves[a].at[place.zs(nz - s), y, x], threes[a].at[s - 1], place.dev(z=s))
+                for s in range(1, nz)
+            ]
+        for copy in waits:
+            copy.wait_recv()
+        comm.done(comm.held[0])
+        mixed[...] = jnp.zeros_like(mixed)
+
+        @pl.loop(0, nz)
+        def _(k):
+            for j in range(ny):
+                for i in range(nx):
+                    for core in range(2):
+                        at = ((k * ny + j) * nx + i) * 2 + core
+                        tops[pl.ds(at, 1), :] = small_out[k, j, i, core, 0:1, :]
+                        mixed[...] += small_out[k, j, i, core]
+
+        summed = jnp.dot(
+            same_in[...], tops[...], precision=lax.Precision.HIGHEST, preferred_element_type=F32
+        )
+        row = lax.broadcasted_iota(jnp.int32, mixed.shape, 0)
+        gained = jnp.where((row >= 1) & (row < 4), mixed[...], 0.0)
+        square = jnp.sum(summed * tops[...]) + jnp.sum(gained * gained)
+        share = head_in[...].astype(F32)
+        square = square + jnp.sum(share * share)
+        for a in range(n):
+            for copy in third[a]:
                 copy.wait_recv()
-            add_blocks(outs[a], [ins[a].at[z]] + [got[a].at[s] for s in range(nz - 1)])
+            add_blocks(outs[a], [halves[a].at[z, y, x]] + [threes[a].at[s] for s in range(nz - 1)])
             square = square + jnp.sum(outs[a][...] * outs[a][...])
         for copy in arriving:
             copy.wait_recv()
-        add_blocks(outs[n], [half.at[y, x]] + [near.at[k] for k in range(len(offsets))])
-        square = square + jnp.sum(outs[n][...] * outs[n][...])
-        held = ins[n + 2][...]
-        first = (lax.broadcasted_iota(jnp.int32, held.shape, 0) == 0) & (
-            lax.broadcasted_iota(jnp.int32, held.shape, 1) == 0
+        add_blocks(table_out, [half.at[y, x]] + [near.at[k] for k in range(len(offsets))])
+        square = square + jnp.sum(table_out[...] * table_out[...])
+        first = (lax.broadcasted_iota(jnp.int32, mine.shape, 0) == 0) & (
+            lax.broadcasted_iota(jnp.int32, mine.shape, 1) == 0
         )
-        mine[...] = held + jnp.where(first, square, 0.0)
-        drain(small_gather(comm, place, mine, every))
-        outs[n + 1][...] = jnp.zeros_like(held)
-        sums = outs[n + 1]
+        mine[...] = partial_in[...] + jnp.where(first, square, 0.0)
+        for copy in small_exchange(comm, place, lambda *spot: mine, every, False):
+            copy.wait_recv()
+        every[z, y, x, c] = mine[...]
+        sums[...] = jnp.zeros_like(sums)
 
         @pl.loop(0, nz)
         def _(k):
@@ -458,15 +607,32 @@
 
         comm.finish()
 
-    count = n * (nz - 1) + ny * nx + small_sends(dims)
-    scratch = [pltpu.VMEM((nz - 1,) + v.shape[1:], v.dtype) for v in lines]
-    scratch += [pltpu.VMEM((ny, nx) + block, BF), pltpu.VMEM((ny * nx - 1,) + block, BF)]
-    scratch += [pltpu.VMEM(partial.shape, F32), pltpu.VMEM(dims + (2,) + partial.shape, F32)]
-    outs = [shape(v.shape[1:], F32) for v in lines] + [shape(block, F32), shape(partial.shape, F32)]
+    count = n * (parts * (ny + nx - 1) + nz - 1) + nz + ny * nx + 2 * small_sends(dims)
+    trail = [g.shape[4:] for g in grads]
+    near_far = [(ny, nx) if axis == "y" else (nx, ny) for axis in first_axes]
+    scratch = [pltpu.VMEM((nz, ny, nx) + t, BF) for t in trail]
+    scratch += [pltpu.VMEM((u - 1, nz, v) + t, BF) for t, (u, v) in zip(trail, near_far)]
+    scratch += [pltpu.VMEM((v - 1, nz) + t, BF) for t, (u, v) in zip(trail, near_far)]
+    scratch += [pltpu.VMEM((nz - 1,) + t, BF) for t in trail]
+    scratch += [
+        pltpu.VMEM((nz, length, width), BF),
+        pltpu.VMEM((ny, nx) + block, BF),
+        pltpu.VMEM((ny, nx) + block, BF),
+        pltpu.VMEM((ny, nx) + block, BF),
+        pltpu.VMEM((ny * nx - 1,) + block, BF),
+        pltpu.VMEM((same.shape[0], 128), F32),
+        pltpu.VMEM((8, 128), F32),
+        pltpu.VMEM(partial.shape, F32),
+        pltpu.VMEM(dims + (2,) + partial.shape, F32),
+        sems(count),
+        sems(count),
+        sems(2),
+    ]
+    outs = [shape(t, F32) for t in trail]
+    outs += [shape(block, F32), shape(small.shape, F32), shape(partial.shape, F32)]
     return call(
-        kernel, outs, [VMEM] * (n + 3), [VMEM] * (n + 2),
-        scratch + [sems(count), sems(count), sems(1)],
-        cid, "scatter_second", (*lines, table, head, partial), 60 * 2**20,
+        kernel, outs, [VMEM] * (n + 6), [VMEM] * (n + 3), scratch,
+        cid, "scatter_all", (*grads, rows, codes, head, small, same, partial), 62 * 2**20,
     )
 
 
@@ -722,11 +888,15 @@
     plane_groups = [[k * plane + i for i in range(plane)] for k in range(nz)]
     line_groups = [[k * plane + i for k in range(nz)] for i in range(plane)]
 
-    layers = [v.astype(BF) for v in (attend_in, attend_mix, expand_in, shrink_out)]
-    tail = jnp.concatenate([labels, heights])
-    meta = jnp.concatenate([targets, loss_mask, pad_rows(tail, 4)], axis=0)
-    *lines, table, metas = gather_first(dims, layers, code_table.astype(BF), meta, 0)
-    table = table.reshape(line_codes, width)
+    layers = (attend_in, attend_mix, expand_in, shrink_out)
+    tail = pad_rows(jnp.concatenate([labels, heights]), 1)
+    label_rows = -(-chips * images // 128)
+    spread = lax.dynamic_update_slice(jnp.zeros((label_rows * 128,), jnp.int32), labels, (chip * images,))
+    spread = jnp.pad(spread.reshape(label_rows, 128), ((0, 3 - label_rows), (0, 0)))
+    meta = jnp.concatenate([targets, loss_mask, tail, spread], axis=0)
+    *weights, row_parts, metas, smalls = gather_all(
+        dims, layers, FIRST_AXES, code_table, class_table, norm_gains, meta, images, 0
+    )
 
     own_tokens = lax.dynamic_slice_in_dim(metas, core, 1, axis=4)[:, :, :, :, 0]
     own_masks = lax.dynamic_slice_in_dim(metas, 2 + core, 1, axis=4)[:, :, :, :, 0]
@@ -742,26 +912,14 @@
     all_labels = metas[:, :, :, 0, 4, :images].reshape(-1)
     before = jnp.concatenate(
         [jnp.full((nz, 1), -1, jnp.int32), line_targets[:, :-1] - z * line_codes], axis=1
-    ).reshape(-1)
-    code_pick = (before[:, None] == jnp.arange(line_codes)[None, :]).astype(BF)
-    rows = matmul(code_pick, table).astype(BF).reshape(nz, length, width)
-    class_pick = all_labels[:, None] == jnp.arange(class_table.shape[0])[None, :]
-    class_part = matmul(class_pick.astype(BF), class_table.astype(BF))
-    gains_low = norm_gains.astype(BF).astype(F32)
-    small = jnp.concatenate([pad_rows(class_part, 6), pad_rows(gains_low, 2)], axis=0)
-
-    *weights, row_parts, smalls = gather_second(dims, lines, FIRST_AXES, rows, small, 1)
+    )
     qkv_w, mix_w, expand_w, shrink_w = (v.reshape(-1, v.shape[-1]) for v in weights)
-    head_low, smalls = lax.optimization_barrier((head_weight.astype(BF), smalls))
-    head_near = lax.all_gather(head_low, "dp", axis_index_groups=plane_groups)
-    head_near = lax.all_gather(head_near, "seq")
-    smalls = smalls.reshape(chips * 2, -1)
-    class_rows = smalls[:, : 6 * 128].reshape(chips * 2, chips * images, -1)
-    class_row = lax.dynamic_slice_in_dim(class_rows, chip * images + core, 1, axis=1).reshape(1, -1)
-    gain = smalls[:, 6 * 128 : 6 * 128 + 3 * gain_columns].reshape(chips * 2, 3, gain_columns)
-    gain = gain.transpose(1, 0, 2).reshape(3, -1)
+
+    smalls = smalls.reshape(chips * 2, 8, 128)[:, :, :gain_columns]
+    class_row = smalls[:, 0].reshape(1, -1)
+    gain = smalls[:, 1:4].transpose(1, 0, 2).reshape(3, -1)
     start = jnp.sum(row_parts.astype(F32), axis=0)
-    start = jnp.where((places == 0)[:, None], class_row, start)
+    start = jnp.concatenate([class_row, start[:-1]], axis=0)
     height = lax.dynamic_slice_in_dim(line_heights, z, 1, axis=0).reshape(())
 
     cosine, sine = rope_tables(places, HD)
@@ -783,7 +941,9 @@
     normed_top, norm_top, inverse_top = norm_forward(final, gain[2])
     normed_top = normed_top.astype(BF)
 
-    tops = line_gather(dims, normed_top, 2, "top_rows").reshape(nz * length, width)
+    tops, head_near = head_gather(dims, normed_top, head_weight, 2)
+    tops = tops.reshape(nz * length, width)
+    head_near = head_near.reshape(2, plane, width, -1)
     marks = (line_targets - z * line_codes).reshape(-1, 1)
     logits, stats = head_forward(tops, head_near, marks)
     stats = line_gather(dims, stats, 3, "row_stats")
@@ -837,24 +997,27 @@
     grads_in = []
     for grad, shard in zip((grad_qkv, grad_mix, grad_expand, grad_shrink), layers):
         grads_in.append(grad.astype(BF).reshape(dims + (2,) + block_form(*shard.shape)))
-    small = jnp.concatenate(
-        [
-            pad_rows(grad_start[0], width // 128),
-            pad_rows(jnp.concatenate([gain_one, gain_two, gain_top]), 3 * width // 128),
-        ],
-        axis=0,
-    )
-    *line_grads, row_grads, smalls = scatter_first(
-        dims, grads_in, FIRST_AXES, grad_start.astype(BF), small, 4
-    )
-    row_grads = row_grads.reshape(nz * length, width)
-    table_grad = lax.dot_general(
-        code_pick, row_grads, (((0,), (0,)), ((), ())), preferred_element_type=F32
-    )
-    table_grad = table_grad.astype(BF).reshape(ny, nx, 2, device_codes, width)
-    smalls = smalls.reshape(chips * 2, 4, -1)
-    device = chip * 2 + core
-    small_mine = lax.dynamic_slice_in_dim(smalls, device * gain_columns, gain_columns, axis=2)
+    small = jnp.stack([grad_start[0], gain_one, gain_two, gain_top])
+    small = small.reshape(4, chips * 2, gain_columns).transpose(1, 0, 2)
+    small = jnp.pad(small, ((0, 0), (0, 4), (0, 128 - gain_columns))).reshape(dims + (2, 8, 128))
+    behind = (z + nz - jnp.arange(nz)) % nz
+    same = (all_labels[:, None] == all_labels[None, :]).astype(F32)
+    partial = pad_rows(jnp.stack([jnp.zeros(()), loss_local, count_local]), 8)
+    *layer_shares, code_share, smalls, sums = scatter_all(
+        dims,
+        grads_in,
+        FIRST_AXES,
+        grad_start.astype(BF),
+        before[behind].reshape(-1, 128),
+        grad_head,
+        small,
+        same,
+        partial,
+        device_codes,
+        4,
+    )
+    small_mine = smalls.reshape(chips * 2, 8, 128)[:, :4, :gain_columns]
+    class_pick = all_labels[:, None] == jnp.arange(class_table.shape[0])[None, :]
     class_share = jnp.dot(
         class_pick.astype(F32).T,
         small_mine[:, 0],
@@ -862,11 +1025,6 @@
         preferred_element_type=F32,
     )
     gain_share = jnp.sum(small_mine[:, 1:], axis=0)
-    square_local = jnp.sum(class_share * class_share) + jnp.sum(gain_share * gain_share)
-    partial = pad_rows(jnp.stack([square_local, loss_local, count_local]), 8)
-    *layer_shares, code_share, sums = scatter_second(
-        dims, line_grads, table_grad, grad_head, partial, 5
-    )
     layer_shares = [g.reshape(v.shape) for g, v in zip(layer_shares, layers)]
     shares = (class_share, code_share, *layer_shares, grad_head.astype(F32), gain_share)
     total_square, loss_sum, loss_count = (sums[0, 0], sums[0, 1], sums[0, 2])

time: 602 us -> 501 us (0.83)
  Pallas kernels: 374 us -> 328 us
  waiting for transfers between devices: 60.9 us -> 32.2 us
  matrix products: 69.5 us -> 48.2 us
  other arithmetic: 42.7 us -> 34.6 us
    pallas_call x6 -> x4, Pallas kernels: 317 us -> 271 us  [call(): pl.pallas_call(kernel, out_shape=outs, in_specs=in_specs, out_specs=out_s...]
    all_gather x2 -> x0, waiting for transfers between devices: 39.1 us -> none  [the longest x1 39.1 us: on_device(): head_near = lax.all_gather(head_low, 'dp', axis_index_groups=plane_groups)]
    unnamed x6 -> x4, waiting for transfers between devices: 0.09 us -> 14.6 us
    dot_general x1 -> x0, matrix products: 12 us -> none  [on_device(): lax.dot_general(code_pick, row_grads, (((0,), (0,)), ((), ())), preferred...]
    convert_element_type x7 -> x1, other arithmetic: 10.5 us -> 0.68 us  [on_device(): same = (all_labels[:, None] == all_labels[None, :]).astype(F32)]
    dot_general x14 -> x12, matrix products: 44.4 us -> 35.9 us  [matmul(): return jnp.dot(left, right, preferred_element_type=F32)]
    reduce_scatter x1, waiting for transfers between devices: 21.7 us -> 15.3 us  [on_device(): grad_top = lax.psum_scatter(grad_tops, 'dp', axis_index_groups=line_groups)]
    unnamed x188 -> x103, local copies, waits for them, and re-layouts: 15.8 us -> 14.9 us
  transfers between devices with their start and end apart: 5 -> 3, of which waited for: 2 -> 3; matrix products, arithmetic and copies ran while one was open for 14% -> 10% of each run, Pallas kernels for 22% -> 3%
where the time goes in v3:
time: 501 us; the launch traced here: 494 us
  Pallas kernels  328 us (65%)
  matrix products  48.2 us (10%)
  other arithmetic  34.6 us (7%)
  local copies, waits for them, and re-layouts  32.3 us (6%)
  waiting for transfers between devices  32.2 us (6%)
  between operations  18 us (4%)
    pallas_call x4, Pallas kernels, call(): pl.pallas_call(kernel, out_shape=outs, in_specs=in_specs, out_specs=out_s...  271 us
    dot_general x12, matrix products, matmul(): return jnp.dot(left, right, preferred_element_type=F32)  35.9 us
    pallas_call x1, Pallas kernels, head_forward(): pl.pallas_call(kernel, grid=(blocks,), out_shape=[shape((blocks, rows, co...  26.9 us
    pallas_call x1, Pallas kernels, head_backward(): pl.pallas_call(kernel, grid=(blocks,), out_shape=[shape(logits.shape, BF)...  18.4 us
    reduce_scatter x1, waiting for transfers between devices, on_device(): grad_top = lax.psum_scatter(grad_tops, 'dp', axis_index_groups=line_groups)  15.3 us
    sub x7, other arithmetic, adam_update(): return (master - rate * (stride + decay * master), moment, second)  15.1 us
    unnamed x103, local copies, waits for them, and re-layouts  14.9 us
    unnamed x4, waiting for transfers between devices  14.6 us
  transfers between devices with their start and end apart: 3, of which 3 were waited for; matrix products, arithmetic and copies ran while one was open for 10% of the time, Pallas kernels for 3%

profile of v3, /device:TPU:0, one launch (start us, length us, event | category | flops | bytes accessed | tf_op | source)
XLA Modules:
  0.0 494.2 jit_solution(4257295839735169535)
XLA Ops:
  8.1 1.9 copy.79.refs_5_
  12.0 107.4 %gather_all.1 = (bf16[4,2,2,2,24,2304]{5,4,3,2,1,0:T(8,128)(2,1)}, bf16[4,2,2,2,24,768]{5,4,3,2,1,0:T(8,128)(2,1)}, bf16[4,2,2,2,24,4096]{5,4,3,2,1,0:T(8,128)(2...) custom-call(f32[24,2304]{1,0:T(8,128)} %refs_0_.1, ...), custom_call_target="tpu_custom_call" | custom-call | tf_op jit(solution)/shard_map/gather_all/pallas_call | solution.py:204
  127.3 5.9 %copy.82 = bf16[2304,768]{1,0:T(8,128)(2,1)} copy(bf16[2304,768]{0,1:T(8,128)(2,1)} %bitcast.175) | data formatting | bytes 7077888 | tf_op jit(solution)/shard_map/dot_general | solution.py:640
  133.2 3.2 fusion.30
  138.3 2.8 fusion.90
  141.1 2.7 convolution_convert_fusion.6
  148.2 3.1 copy-done.46
  153.4 34.6 %head_gather.1 = (bf16[4,256,768]{2,1,0:T(8,128)(2,1)S(1)}, bf16[2,2,2,768,512]{4,3,2,1,0:T(8,128)(2,1)}) custom-call(bf16[256,768]{1,0:T(8,128)(2,1)S(1)} %multiply_convert_fusion.4.src, f32[768,512]{1,0:T(8,128)S(1)} %copy-done), custom_call_target="tpu_custom_call" | custom-call | tf_op jit(solution)/shard_map/head_gather/pallas_call | solution.py:204
  188.0 26.9 %head_forward.1 = (f32[8,1024,512]{2,1,0:T(8,128)}, f32[8,1024]{1,0:T(8,128)S(1)}) custom-call(bf16[1024,768]{1,0:T(8,128)(2,1)S(1)} %bitcast.154, bf16[2,4,768,512]{3,2,1,0:T(8,128)(2,1)} %bitcast.200, s32[1024,1]{1,0:T(8,128)S(1)} %copy.84.mark_ref), custom_call_target="tpu_custom_call" | custom-call | flops 6442450944 | bytes 23068672 | tf_op jit(solution)/shard_map/head_forward/pallas_call | solution.py:674
  215.5 11.3 %row_stats.1 = f32[4,8,1024]{2,1,0:T(8,128)} custom-call(f32[8,1024]{1,0:T(8,128)} %copy-done.1), custom_call_target="tpu_custom_call" | custom-call | tf_op jit(solution)/shard_map/row_stats/pallas_call | solution.py:204
  228.0 18.4 %head_backward.1 = (bf16[8,1024,512]{2,1,0:T(8,128)(2,1)}, bf16[1024,768]{1,0:T(8,128)(2,1)}) custom-call(f32[8,1024,512]{2,1,0:T(8,128)} %get-tuple-element.56.l_ref, bf16[2,4,768,512]{3,2,1,0:T(8,128)(2,1)} %bitcast.201, s32[1024,1]{1,0:T(8,128)S(1)} %copy.84.mark_ref, f32[8,1024]{1,0:T(8,128)S(1)} %select_maximum_fusion.stat_ref), custom_call_target="tpu_custom_call" | custom-call | flops 6442450944 | bytes 31457280 | tf_op jit(solution)/shard_map/head_backward/pallas_call | solution.py:723
  247.9 12.4 %head_weights.1 = bf16[2,4,768,512]{3,2,1,0:T(8,128)(2,1)} custom-call(bf16[1024,768]{1,0:T(8,128)(2,1)S(1)} %bitcast.155, bf16[8,1024,512]{2,1,0:T(8,128)(2,1)} %get-tuple-element.59.g_ref), custom_call_target="tpu_custom_call" | custom-call | flops 6442450944 | bytes 14680064 | tf_op jit(solution)/shard_map/head_weights/pallas_call | solution.py:759
  263.7 2.0 fusion.57.refs_9_
  266.4 15.3 %reduce-scatter.6.cloned.1.call-done = bf16[1,256,768]{2,1,0:T(8,128)(2,1)} async-done(((bf16[4,256,768]{2,1,0:T(8,128)(2,1)}), bf16[1,256,768]{2,1,0:T(8,128)(2,1)}) %reduce-scatter.6.cloned.1.call-update) | async-done | bytes 393232 | tf_op jit(solution)/shard_map/reduce_scatter | solution.py:961
  283.2 5.0 %multiply_convert_fusion.2 = (bf16[256,2048]{1,0:T(8,128)(2,1)S(1)}, bf16[256,2048]{1,0:T(8,128)(2,1)S(1)}) fusion(f32[256,4096]{1,0:T(8,128)} %copy-done.4, bf16[2048,768]{1,0:T(8,128)(2,1)} %bitcast.202, f32[256]{0:T(256)S(1)} %broadcast_multiply_fusion.6, f32[256,768]{1,0:T(8,128)} %copy-done.9, f32[768]{0:T(1024)S(1)} %mul.675, ...), kind=kOutput, calls=%fused_computation.15 | convolution fusion | flops 813498368 | bytes 10621952 | tf_op jit(solution)/shard_map/dot_general | solution.py:640
  288.3 6.8 %multiply_reduce_fusion.1 = (f32[768]{0:T(1024)S(1)}, f32[256]{0:T(256)S(1)}, f32[256,768]{1,0:T(8,128)}) fusion(f32[256,768]{1,0:T(8,128)S(1)} %copy-done.7, f32[256]{0:T(256)S(1)} %add_rsqrt_fusion.1, f32[768]{0:T(1024)S(1)} %mul.667, bf16[768,4096]{1,0:T(8,128)(2,1)} %bitcast.166, bf16[256,2048]{1,0:T(8,128)(2,1)S(1)} %get-tuple-element.106, ...), kind=kOutput, calls=%fused_computation.68 | convolution fusion | flops 1615985664 | bytes 9969664 | tf_op jit(solution)/shard_map/dot_general | solution.py:640
  295.1 2.3 reduce-scatter.8.cloned.1.call-done
  297.5 2.1 multiply_add_fusion.3
  301.7 1.9 copy.87
  303.8 3.0 multiply_reduce_fusion
  316.5 2.6 convolution_convert_fusion.3
  319.1 4.5 convolution_convert_fusion.1
  323.6 3.1 convolution_convert_fusion.2
  326.7 4.6 convolution_convert_fusion
  331.3 14.6 %reduce-scatter.10.cloned.1.call-done = bf16[1,768,512]{2,1,0:T(8,128)(2,1)} async-done(((bf16[4,768,512]{2,1,0:T(8,128)(2,1)}), bf16[1,768,512]{2,1,0:T(8,128)(2,1)}) %reduce-scatter.10.cloned.1.call-update) | async-done | bytes 786448
  345.9 117.3 %scatter_all.1 = (f32[24,2304]{1,0:T(8,128)}, f32[24,768]{1,0:T(8,128)}, f32[24,4096]{1,0:T(8,128)}, f32[64,768]{1,0:T(8,128)}, f32[512,768]{1,0:T(8,128)}, /*in...) custom-call(bf16[4,2,2,2,24,2304]{5,4,3,2,1,0:T(8,128)(2,1)} %bitcast.163, bf16[4,2,2,2,24,768]{5,4,3,2,1,0:T(8,128)(2,1)} %bitcast.170, ...), custom_call_target="tpu_custom_call" | custom-call | tf_op jit(solution)/shard_map/scatter_all/pallas_call | solution.py:204
  470.9 2.1 multiply_subtract_fusion.5
  473.0 2.1 multiply_subtract_fusion.4
  475.1 2.2 multiply_subtract_fusion.3
  477.3 2.4 multiply_subtract_fusion.2
  479.8 3.0 multiply_subtract_fusion.1
  483.4 3.0 multiply_subtract_fusion
  (189 shorter events, 45.7 us)
Async XLA Ops:
  7.2 274.4 %reduce-scatter.6.cloned.1.call-start = ((), (), s32[]{:S(2)}) async-start(), calls=%async_computation.3 | async-start | bytes 1966080 | tf_op jit(solution)/shard_map/reduce_scatter | solution.py:961
  141.1 3.7 slice-start
  141.1 4.5 slice-start.1
  144.4 3.8 copy-start.6
  147.5 4.9 copy-start.4
  147.5 3.8 copy-start.46
  148.2 4.2 copy-start.13
  188.0 26.9 %copy-start.2 = (bf16[4,256,768]{2,1,0:T(8,128)(2,1)}, bf16[4,256,768]{2,1,0:T(8,128)(2,1)S(1)}, u32[]{:S(2)}) copy-start(bf16[4,256,768]{2,1,0:T(8,128)(2,1)S(1)} %get-tuple-element.54) | copy-start | bytes 4718596
  246.4 51.0 %reduce-scatter.8.cloned.1.call-start = ((), (), s32[]{:S(2)}) async-start(), calls=%async_computation.4 | async-start | bytes 9437184 | tf_op jit(solution)/shard_map/reduce_scatter | solution.py:963
  260.3 85.6 %reduce-scatter.10.cloned.1.call-start = ((), (), s32[]{:S(2)}) async-start(), calls=%async_computation.5 | async-start | bytes 3932160
  283.2 5.0 %copy-start.7 = (f32[256,768]{1,0:T(8,128)S(1)}, f32[256,768]{1,0:T(8,128)}, u32[]{:S(2)}) copy-start(f32[256,768]{1,0:T(8,128)} %copy-done.6) | copy-start | bytes 2359300
  288.2 6.8 %copy-start.33 = (bf16[256,2048]{1,0:T(8,128)(2,1)}, bf16[256,2048]{1,0:T(8,128)(2,1)S(1)}, u32[]{:S(2)}) copy-start(bf16[256,2048]{1,0:T(8,128)(2,1)S(1)} %get-tuple-element.105) | copy-start | bytes 3145732
  288.3 6.8 %copy-start.35 = (bf16[256,2048]{1,0:T(8,128)(2,1)}, bf16[256,2048]{1,0:T(8,128)(2,1)S(1)}, u32[]{:S(2)}) copy-start(bf16[256,2048]{1,0:T(8,128)(2,1)S(1)} %get-tuple-element.106) | copy-start | bytes 3145732
  303.8 3.2 copy-start.22
  319.1 4.5 copy-start.10
  319.1 4.5 copy-start.14
  323.6 3.1 copy-start.8
  323.6 3.1 copy-start.34
  345.9 122.7 %copy-start.43 = (f32[3,24]{1,0:T(4,128)S(1)}, f32[3,24]{1,0:T(4,128)}, u32[]{:S(2)}) copy-start(f32[3,24]{1,0:T(4,128)} %refs_6_.1) | copy-start | bytes 868
  345.9 122.7 %copy-start.44 = (f32[3,24]{1,0:T(4,128)S(1)}, f32[3,24]{1,0:T(4,128)}, u32[]{:S(2)}) copy-start(f32[3,24]{1,0:T(4,128)} %param.47) | copy-start | bytes 868
  345.9 122.7 %copy-start.45 = (f32[3,24]{1,0:T(4,128)S(1)}, f32[3,24]{1,0:T(4,128)}, u32[]{:S(2)}) copy-start(f32[3,24]{1,0:T(4,128)} %param.55) | copy-start | bytes 868
  345.9 123.3 %copy-start.40 = (f32[24,768]{1,0:T(8,128)S(1)}, f32[24,768]{1,0:T(8,128)}, u32[]{:S(2)}) copy-start(f32[24,768]{1,0:T(8,128)} %refs_1_.1) | copy-start | bytes 221188
  345.9 123.3 %copy-start.42 = (f32[24,768]{1,0:T(8,128)S(1)}, f32[24,768]{1,0:T(8,128)}, u32[]{:S(2)}) copy-start(f32[24,768]{1,0:T(8,128)} %param.43) | copy-start | bytes 221188
  345.9 125.0 %copy-start.41 = (f32[1001,24]{0,1:T(8,128)S(1)}, f32[1001,24]{0,1:T(8,128)}, u32[]{:S(2)}) copy-start(f32[1001,24]{0,1:T(8,128)} %param.32) | copy-start | bytes 288292
  345.9 127.1 %copy-start.38 = (f32[64,768]{1,0:T(8,128)S(1)}, f32[64,768]{1,0:T(8,128)}, u32[]{:S(2)}) copy-start(f32[64,768]{1,0:T(8,128)} %refs_3_.1) | copy-start | bytes 589828
  463.2 11.9 %copy-start.37 = (f32[24,2304]{1,0:T(8,128)S(1)}, f32[24,2304]{1,0:T(8,128)}, u32[]{:S(2)}) copy-start(f32[24,2304]{1,0:T(8,128)} %refs_0_.1) | copy-start | bytes 663556
  469.2 8.2 %copy-start.25 = (f32[24,4096]{1,0:T(8,128)S(1)}, f32[24,4096]{1,0:T(8,128)}, u32[]{:S(2)}) copy-start(f32[24,4096]{1,0:T(8,128)} %refs_2_.1) | copy-start | bytes 1179652
  470.9 8.9 %copy-start.28 = (f32[512,768]{1,0:T(8,128)S(1)}, f32[512,768]{1,0:T(8,128)}, u32[]{:S(2)}) copy-start(f32[512,768]{1,0:T(8,128)} %get-tuple-element.62) | copy-start | bytes 4718596
  473.0 6.8 %copy-start.27 = (f32[512,768]{1,0:T(8,128)S(1)}, f32[512,768]{1,0:T(8,128)}, u32[]{:S(2)}) copy-start(f32[512,768]{1,0:T(8,128)} %param.49) | copy-start | bytes 4718596
  475.1 4.7 copy-start.15
  475.1 4.7 copy-start.26
  479.8 3.6 copy-start.24
  (20 other events, 40.1 us)
Sparse Core Ops, SparseCore 0:
  246.5 35.0 reduce-scatter.5
  283.9 13.4 reduce-scatter.7
  300.7 45.1 reduce-scatter.9

commit v4 on v3

--- a/solution.py
+++ b/solution.py
@@ -376,59 +376,6 @@
     )
 
 
-def line_gather(dims, block, cid, name):
-    nz = dims[0]
-
-    def kernel(src, out, ssem, rsem, lsem):
-        place = Place(dims)
-        greet(place, [(s, 0, 0, 0) for s in range(1, nz)])
-        comm = Comm(ssem, rsem, lsem)
-        waits = [comm.send(src, out.at[place.z], place.dev(z=s)) for s in range(1, nz)]
-        comm.keep(src, out.at[place.z])
-        for copy in waits:
-            copy.wait_recv()
-        comm.finish()
-
-    return call(
-        kernel, shape((nz,) + block.shape, block.dtype), [ANY], ANY,
-        [sems(nz), sems(nz), sems(1)], cid, name, (block,),
-    )
-
-
-def head_gather(dims, block, head, cid):
-    nz, ny, nx = dims
-    rows = head.shape[0]
-
-    def kernel(src, head_in, out, whole, low, ssem, rsem, lsem):
-        place = Place(dims)
-        z, y, x, c = (place.z, place.y, place.x, place.c)
-        greet(place, line_offsets(dims))
-        comm = Comm(ssem, rsem, lsem)
-        low[...] = head_in[...].astype(BF)
-        comm.keep(low, whole.at[c, y, x])
-        gather = PlaneGather(comm, place)
-        for first, start in (("x", 0), ("y", rows // 2)):
-            half = pl.ds(start, rows // 2)
-            gather.spread(lambda yy, xx, half=half: whole.at[c, yy, xx, half], first, low.at[half])
-        waits = [comm.send(src, out.at[z], place.dev(z=s)) for s in range(1, nz)]
-        comm.keep(src, out.at[z])
-        gather.forward()
-        gather.settle()
-        gather.arrive()
-        for copy in waits:
-            copy.wait_recv()
-        comm.finish()
-
-    count = nz + 2 * (2 * ny * nx - 1)
-    return call(
-        kernel,
-        [shape((nz,) + block.shape, BF), shape((2, ny, nx) + head.shape, BF)],
-        [ANY, VMEM], [ANY, ANY],
-        [pltpu.VMEM(head.shape, BF), sems(count), sems(count), sems(2)],
-        cid, "head_gather", (block, head), 48 * 2**20,
-    )
-
-
 def add_blocks(out, terms):
     lead = out.shape[:-2]
 
@@ -636,144 +583,190 @@
     )
 
 
+def head_all(dims, rows, head, marks, counted, cid):
+    nz, ny, nx = dims
+    length, width = rows.shape
+    columns = head.shape[1]
+    lanes = min(columns, 128)
+    groups = columns // lanes
+    plane = ny * nx
+    blocks = 2 * plane
+    keep = columns >= 128
+
+    def kernel(*refs):
+        rows_in, head_in, marks_in, counted_in, top_out, head_out, loss_out, *rest = refs
+        whole, lined, turned, peaks, totals, picks, exps, grads, *rest = rest
+        columned, partial, back, coming, mine, every, given, half, ssem, rsem, lsem = rest
+        place = Place(dims)
+        z, y, x, c = (place.z, place.y, place.x, place.c)
+        greet(place, line_offsets(dims))
+        comm = Comm(ssem, rsem, lsem)
+        whole[c, y, x] = head_in[...].astype(BF)
+        lined[0] = rows_in[...]
+        arriving = [comm.send(lined.at[0], lined.at[s], place.dev(z=s)) for s in range(1, nz)]
+        gather = PlaneGather(comm, place)
+        for first, start in (("x", 0), ("y", width // 2)):
+            part = pl.ds(start, width // 2)
+            gather.spread(lambda yy, xx, part=part: whole.at[c, yy, xx, part], first)
+        turned[:, 0:length] = lined[0].T
+        gather.forward()
+        gather.settle()
+        gather.arrive()
+
+        def block(k):
+            return whole[k // plane, k // nx % ny, k % nx]
+
+        def split(value):
+            return [value[:, lanes * q : lanes * (q + 1)] for q in range(groups)]
+
+        def hits(s, k):
+            base = (k % plane * 2 + k // plane) * columns
+            lane = lax.broadcasted_iota(jnp.int32, (length, lanes), 1) + base
+            return [lane + lanes * q == marks_in[s] for q in range(groups)]
+
+        def logits_of(s, k):
+            return matmul(lined[s], block(k))
+
+        def forward(s):
+            at = pl.ds(s * length, length)
+            peaks[...] = jnp.full_like(peaks, -jnp.inf)
+            totals[...] = jnp.zeros_like(totals)
+            picks[...] = jnp.zeros_like(picks)
+
+            @pl.loop(0, blocks)
+            def _(k):
+                logits = logits_of(s, k)
+                if keep:
+                    exps[k, at] = logits
+                high, found = (peaks[...], picks[...])
+                for piece, hit in zip(split(logits), hits(s, k)):
+                    high = jnp.maximum(high, piece)
+                    found = found + jnp.where(hit, piece, 0.0)
+                peaks[...] = high
+                picks[...] = found
+
+            peak = jnp.max(peaks[...], axis=1, keepdims=True)
+            peaks[...] = jnp.broadcast_to(peak, (length, lanes))
+
+            @pl.loop(0, blocks)
+            def _(k):
+                logits = exps[k, at] if keep else logits_of(s, k)
+                total = totals[...]
+                for q, piece in enumerate(split(logits)):
+                    power = jnp.exp(piece - peaks[...])
+                    if keep:
+                        exps[k, at, lanes * q : lanes * (q + 1)] = power
+                    total = total + power
+                totals[...] = total
+
+            if not keep:
+                exps[s] = peaks[...]
+            lane = lax.broadcasted_iota(jnp.int32, (length, 128), 1)
+            total = jnp.sum(totals[...], axis=1, keepdims=True)
+            found = jnp.sum(picks[...], axis=1, keepdims=True)
+            table = jnp.where(lane == 0, peak, jnp.where(lane == 1, total, found))
+            mine[place.zs(s)] = table.T[:8]
+
+        forward(0)
+        for s in range(1, nz):
+            arriving[s - 1].wait_recv()
+            turned[:, s * length : (s + 1) * length] = lined[s].T
+            forward(s)
+        stats = [comm.send(mine, every.at[s], place.dev(z=s)) for s in range(1, nz)]
+        every[0] = mine[...]
+        for copy in stats:
+            copy.wait_recv()
+
+        def backward(s):
+            at = pl.ds(s * length, length)
+            held = [every[q, place.zs(s)] for q in range(nz)]
+            peak = held[0][0:1]
+            for other in held[1:]:
+                peak = jnp.maximum(peak, other[0:1])
+            total = sum(other[1:2] * jnp.exp(other[0:1] - peak) for other in held)
+            weight = counted_in[s : s + 1]
+            if s == 0:
+                found = sum(other[2:3] for other in held)
+                loss = (peak + jnp.log(total) - found) * weight
+                loss_out[...] = jnp.concatenate([loss, jnp.zeros((7, length), F32)], axis=0)
+            scale = weight / total * jnp.exp(held[0][0:1] - peak)
+            tall = jnp.concatenate([scale, weight, jnp.zeros((126, length), F32)], axis=0).T
+            columned[0] = jnp.broadcast_to(tall[:, 0:1], (length, lanes))
+            columned[1] = jnp.broadcast_to(tall[:, 1:2], (length, lanes))
+            partial[...] = jnp.zeros_like(partial)
+
+            @pl.loop(0, blocks)
+            def _(k):
+                if keep:
+                    powers = split(exps[k, at])
+                else:
+                    powers = [jnp.exp(piece - exps[s]) for piece in split(logits_of(s, k))]
+                pieces = []
+                for power, hit in zip(powers, hits(s, k)):
+                    grad = power * columned[0] - jnp.where(hit, columned[1], 0.0)
+                    pieces.append(grad.astype(BF))
+                grad = jnp.concatenate(pieces, axis=1) if groups > 1 else pieces[0]
+                grads[k, at] = grad
+                partial[...] += lax.dot_general(
+                    grad, block(k), (((1,), (1,)), ((), ())), preferred_element_type=F32
+                )
+
+        coming_in = []
+        for s in range(1, nz):
+            backward(s)
+            back[s - 1] = partial[...].astype(BF)
+            coming_in.append(comm.send(back.at[s - 1], coming.at[s - 1], place.dev(z=nz - s)))
+        backward(0)
+
+        def weights(into, core):
+            @pl.loop(0, plane)
+            def _(j):
+                into[j // nx, j % nx] = matmul(turned[...], grads[core * plane + j]).astype(BF)
+
+        weights(given, 1 - c)
+        pair = comm.send(given, half, place.dev(c=1))
+        weights(head_out, c)
+        pair.wait_recv()
+        add_blocks(head_out, [head_out, half])
+        for copy in coming_in:
+            copy.wait_recv()
+        total = partial[...]
+        for s in range(nz - 1):
+            total = total + coming[s].astype(F32)
+        top_out[...] = total
+        comm.finish()
+
+    count = 3 * (nz - 1) + 2 * (2 * plane - 1) + 1
+    scratch = [
+        pltpu.VMEM((2, ny, nx) + head.shape, BF),
+        pltpu.VMEM((nz, length, width), BF),
+        pltpu.VMEM((width, nz * length), BF),
+        pltpu.VMEM((length, lanes), F32),
+        pltpu.VMEM((length, lanes), F32),
+        pltpu.VMEM((length, lanes), F32),
+        pltpu.VMEM((blocks, nz * length, columns) if keep else (nz, length, lanes), F32),
+        pltpu.VMEM((blocks, nz * length, columns), BF),
+        pltpu.VMEM((2, length, lanes), F32),
+        pltpu.VMEM((length, width), F32),
+        pltpu.VMEM((nz - 1, length, width), BF),
+        pltpu.VMEM((nz - 1, length, width), BF),
+        pltpu.VMEM((nz, 8, length), F32),
+        pltpu.VMEM((nz, nz, 8, length), F32),
+        pltpu.VMEM((ny, nx) + head.shape, BF),
+        pltpu.VMEM((ny, nx) + head.shape, BF),
+        sems(count),
+        sems(count),
+        sems(1),
+    ]
+    return call(
+        kernel,
+        [shape((length, width), F32), shape((ny, nx) + head.shape, BF), shape((8, length), F32)],
+        [VMEM] * 4, [VMEM] * 3, scratch, cid, "head_all", (rows, head, marks, counted), 62 * 2**20,
+    )
+
+
 def matmul(left, right):
     return jnp.dot(left, right, preferred_element_type=F32)
-
-
-def head_forward(tops, weights, marks):
-    cores, plane, width, columns = weights.shape
-    rows = tops.shape[0]
-    blocks = cores * plane
-
-    def kernel(x_ref, w_ref, mark_ref, logit_ref, stat_ref, peak, total, picked):
-        k = pl.program_id(0)
-
-        @pl.when(k == 0)
-        def _():
-            peak[...] = jnp.full_like(peak, -jnp.inf)
-            total[...] = jnp.zeros_like(total)
-            picked[...] = jnp.zeros_like(picked)
-
-        logits = matmul(x_ref[...], w_ref[...])
-        logit_ref[...] = logits
-        lanes = lax.broadcasted_iota(jnp.int32, logits.shape, 1) + k * columns
-        chosen = jnp.where(lanes == mark_ref[...], logits, 0.0)
-        picked[...] += jnp.sum(chosen, axis=1, keepdims=True)
-        old = peak[...]
-        new = jnp.maximum(old, jnp.max(logits, axis=1, keepdims=True))
-        exponent = jnp.sum(jnp.exp(logits - new), axis=1, keepdims=True)
-        total[...] = total[...] * jnp.exp(old - new) + exponent
-        peak[...] = new
-
-        @pl.when(k == blocks - 1)
-        def _():
-            lane = lax.broadcasted_iota(jnp.int32, (rows, 128), 1)
-            table = jnp.where(lane == 0, peak[...], jnp.where(lane == 1, total[...], picked[...]))
-            stat_ref[...] = table.T[:8]
-
-    return pl.pallas_call(
-        kernel,
-        grid=(blocks,),
-        out_shape=[shape((blocks, rows, columns), F32), shape((8, rows), F32)],
-        in_specs=[
-            pl.BlockSpec((rows, width), lambda k: (0, 0)),
-            pl.BlockSpec((None, None, width, columns), lambda k: (k % 2, k // 2, 0, 0)),
-            pl.BlockSpec((rows, 1), lambda k: (0, 0)),
-        ],
-        out_specs=[
-            pl.BlockSpec((None, rows, columns), lambda k: (k, 0, 0)),
-            pl.BlockSpec((8, rows), lambda k: (0, 0)),
-        ],
-        scratch_shapes=[pltpu.VMEM((rows, 1), F32)] * 3,
-        compiler_params=pltpu.CompilerParams(vmem_limit_bytes=48 * 2**20),
-        cost_estimate=pl.CostEstimate(
-            flops=2 * rows * width * columns * blocks,
-            bytes_accessed=blocks * columns * (2 * width + 4 * rows),
-            transcendentals=rows * columns * blocks,
-        ),
-        name="head_forward",
-    )(tops, weights, marks)
-
-
-def head_backward(logits, weights, marks, stats):
-    blocks, rows, columns = logits.shape
-    width = weights.shape[2]
-
-    def kernel(l_ref, w_ref, mark_ref, stat_ref, grad_ref, top_ref, column, total):
-        k = pl.program_id(0)
-
-        @pl.when(k == 0)
-        def _():
-            column[...] = jnp.concatenate([stat_ref[...]] * 16, axis=0).T
-            total[...] = jnp.zeros_like(total)
-
-        held = column[...]
-        soft = jnp.exp(l_ref[...] - held[:, 0:1]) * held[:, 1:2]
-        lanes = lax.broadcasted_iota(jnp.int32, soft.shape, 1) + k * columns
-        grad = (soft - jnp.where(lanes == mark_ref[...], held[:, 2:3], 0.0)).astype(BF)
-        grad_ref[...] = grad
-        total[...] += lax.dot_general(
-            grad, w_ref[...], (((1,), (1,)), ((), ())), preferred_element_type=F32
-        )
-
-        @pl.when(k == blocks - 1)
-        def _():
-            top_ref[...] = total[...].astype(BF)
-
-    return pl.pallas_call(
-        kernel,
-        grid=(blocks,),
-        out_shape=[shape(logits.shape, BF), shape((rows, width), BF)],
-        in_specs=[
-            pl.BlockSpec((None, rows, columns), lambda k: (k, 0, 0)),
-            pl.BlockSpec((None, None, width, columns), lambda k: (k % 2, k // 2, 0, 0)),
-            pl.BlockSpec((rows, 1), lambda k: (0, 0)),
-            pl.BlockSpec((8, rows), lambda k: (0, 0)),
-        ],
-        out_specs=[
-            pl.BlockSpec((None, rows, columns), lambda k: (k, 0, 0)),
-            pl.BlockSpec((rows, width), lambda k: (0, 0)),
-        ],
-        scratch_shapes=[pltpu.VMEM((rows, 128), F32), pltpu.VMEM((rows, width), F32)],
-        compiler_params=pltpu.CompilerParams(vmem_limit_bytes=48 * 2**20),
-        cost_estimate=pl.CostEstimate(
-            flops=2 * rows * width * columns * blocks,
-            bytes_accessed=blocks * columns * (2 * width + 6 * rows),
-            transcendentals=rows * columns * blocks,
-        ),
-        name="head_backward",
-    )(logits, weights, marks, stats)
-
-
-def head_weights(tops, grads):
-    blocks, rows, columns = grads.shape
-    width = tops.shape[1]
-
-    def kernel(x_ref, g_ref, out_ref, turned):
-        @pl.when(pl.program_id(0) == 0)
-        def _():
-            turned[...] = x_ref[...].T
-
-        out_ref[...] = matmul(turned[...], g_ref[...]).astype(BF)
-
-    return pl.pallas_call(
-        kernel,
-        grid=(blocks,),
-        out_shape=shape((2, blocks // 2, width, columns), BF),
-        in_specs=[
-            pl.BlockSpec((rows, width), lambda k: (0, 0)),
-            pl.BlockSpec((None, rows, columns), lambda k: (k, 0, 0)),
-        ],
-        out_specs=pl.BlockSpec((None, None, width, columns), lambda k: (k % 2, k // 2, 0, 0)),
-        scratch_shapes=[pltpu.VMEM((width, rows), BF)],
-        compiler_params=pltpu.CompilerParams(vmem_limit_bytes=48 * 2**20),
-        cost_estimate=pl.CostEstimate(
-            flops=2 * rows * width * columns * blocks,
-            bytes_accessed=blocks * columns * 2 * (width + rows),
-            transcendentals=0,
-        ),
-        name="head_weights",
-    )(tops, grads)
 
 
 def norm_forward(values, gain):
@@ -886,7 +879,6 @@
     chip, core = (lax.axis_index("dp"), lax.axis_index("seq"))
     z, y, x = (chip // plane, (chip // nx) % ny, chip % nx)
     plane_groups = [[k * plane + i for i in range(plane)] for k in range(nz)]
-    line_groups = [[k * plane + i for k in range(nz)] for i in range(plane)]
 
     layers = (attend_in, attend_mix, expand_in, shrink_out)
     tail = pad_rows(jnp.concatenate([labels, heights]), 1)
@@ -941,29 +933,19 @@
     normed_top, norm_top, inverse_top = norm_forward(final, gain[2])
     normed_top = normed_top.astype(BF)
 
-    tops, head_near = head_gather(dims, normed_top, head_weight, 2)
-    tops = tops.reshape(nz * length, width)
-    head_near = head_near.reshape(2, plane, width, -1)
-    marks = (line_targets - z * line_codes).reshape(-1, 1)
-    logits, stats = head_forward(tops, head_near, marks)
-    stats = line_gather(dims, stats, 3, "row_stats")
-    peaks = jnp.max(stats[:, 0], axis=0)
-    totals = jnp.sum(stats[:, 1] * jnp.exp(stats[:, 0] - peaks[None, :]), axis=0)
-    log_total = peaks + jnp.log(totals)
-    counted = line_counted.reshape(-1)
-    losses = (log_total - jnp.sum(stats[:, 2], axis=0)) * counted
-    loss_local = jnp.sum(lax.dynamic_slice_in_dim(losses.reshape(nz, -1), z, 1, axis=0))
+    behind = (z + nz - jnp.arange(nz)) % nz
+    marks = (line_targets - z * line_codes)[behind]
+    lanes = min(head_weight.shape[1], 128)
+    marks = jnp.broadcast_to(marks[:, :, None], (nz, length, lanes))
+    grad_top, grad_head, losses = head_all(
+        dims, normed_top, head_weight, marks, line_counted[behind], 2
+    )
+    loss_local = jnp.sum(losses[0])
     count_local = jnp.sum(lax.dynamic_slice_in_dim(line_counted, z, 1, axis=0))
-    scales = jnp.stack([peaks, counted / totals, counted])
-    scales = jnp.pad(scales, ((0, 5), (0, 0)))
-    grad_logits, grad_tops = head_backward(logits, head_near, marks, scales)
-    grad_tops = grad_tops.reshape(nz, length, width)
-    grad_top = lax.psum_scatter(grad_tops, "dp", axis_index_groups=line_groups)
-    grad_head = head_weights(tops, grad_logits)
-    grad_head = lax.psum_scatter(grad_head, "seq", scatter_dimension=0)
+    grad_head = grad_head.reshape((plane,) + head_weight.shape)
     grad_head = lax.psum_scatter(grad_head, "dp", axis_index_groups=plane_groups)
 
-    grad_final, gain_top = norm_backward(grad_top.astype(F32), norm_top, inverse_top, gain[2])
+    grad_final, gain_top = norm_backward(grad_top, norm_top, inverse_top, gain[2])
     back_down = grad_final.astype(BF)
     grad_shrink = matmul(hidden.T, back_down)
     grad_hidden = matmul(back_down, shrink_w.T)
@@ -1000,7 +982,6 @@
     small = jnp.stack([grad_start[0], gain_one, gain_two, gain_top])
     small = small.reshape(4, chips * 2, gain_columns).transpose(1, 0, 2)
     small = jnp.pad(small, ((0, 0), (0, 4), (0, 128 - gain_columns))).reshape(dims + (2, 8, 128))
-    behind = (z + nz - jnp.arange(nz)) % nz
     same = (all_labels[:, None] == all_labels[None, :]).astype(F32)
     partial = pad_rows(jnp.stack([jnp.zeros(()), loss_local, count_local]), 8)
     *layer_shares, code_share, smalls, sums = scatter_all(

time: 501 us -> 457 us (0.912)
  waiting for transfers between devices: 32.2 us -> 0.02 us
  matrix products: 48.2 us -> 41.3 us
    pallas_call x3 -> x0, Pallas kernels: 57.6 us -> none  [the longest x1 26.9 us: head_forward(): pl.pallas_call(kernel, grid=(blocks,), out_shape=[shape((blocks, rows, co...]
    pallas_call x4 -> x3, Pallas kernels: 271 us -> 323 us  [call(): pl.pallas_call(kernel, out_shape=outs, in_specs=in_specs, out_specs=out_s...]
    reduce_scatter x2 -> x0, waiting for transfers between devices: 17.6 us -> none  [the longest x1 15.3 us: on_device(): grad_top = lax.psum_scatter(grad_tops, 'dp', axis_index_groups=line_groups)]
    unnamed x4 -> x2, waiting for transfers between devices: 14.6 us -> 0.02 us
    dot_general x12, matrix products: 35.9 us -> 28.7 us  [matmul(): return jnp.dot(left, right, preferred_element_type=F32)]
    unnamed x103 -> x152, local copies, waits for them, and re-layouts: 14.9 us -> 14.9 us
  transfers between devices with their start and end apart: 3 -> 1, of which waited for: 3 -> 0; matrix products, arithmetic and copies ran while one was open for 10% -> 9% of each run, Pallas kernels for 3% -> 0%
where the time goes in v4:
time: 457 us; the launch traced here: 451 us
  Pallas kernels  323 us (71%)
  matrix products  41.3 us (9%)
  local copies, waits for them, and re-layouts  35.3 us (8%)
  other arithmetic  33.1 us (7%)
  between operations  18.6 us (4%)
    pallas_call x3, Pallas kernels, call(): pl.pallas_call(kernel, out_shape=outs, in_specs=in_specs, out_specs=out_s...  323 us
    dot_general x12, matrix products, matmul(): return jnp.dot(left, right, preferred_element_type=F32)  28.7 us
    unnamed x152, local copies, waits for them, and re-layouts  14.9 us
    sub x7, other arithmetic, adam_update(): return (master - rate * (stride + decay * master), moment, second)  14.6 us
  transfers between devices with their start and end apart: 1, of which 0 were waited for; matrix products, arithmetic and copies ran while one was open for 9% of the time, Pallas kernels for 0%

profile of v4, /device:TPU:0, one launch (start us, length us, event | category | flops | bytes accessed | tf_op | source)
XLA Modules:
  0.0 451.3 jit_solution(13075140292034070791)
XLA Ops:
  8.1 1.9 copy.75.refs_5_
  10.7 1.3 pad_add_fusion.refs_7_
  12.0 107.5 %gather_all.1 = (bf16[4,2,2,2,24,2304]{5,4,3,2,1,0:T(8,128)(2,1)}, bf16[4,2,2,2,24,768]{5,4,3,2,1,0:T(8,128)(2,1)}, bf16[4,2,2,2,24,4096]{5,4,3,2,1,0:T(8,128)(2...) custom-call(f32[24,2304]{1,0:T(8,128)} %refs_0_.1, ...), custom_call_target="tpu_custom_call" | custom-call | tf_op jit(solution)/shard_map/gather_all/pallas_call | solution.py:204
  127.0 1.7 convert_reduce_fusion
  128.9 5.9 %copy.78 = bf16[2304,768]{1,0:T(8,128)(2,1)} copy(bf16[2304,768]{0,1:T(8,128)(2,1)} %bitcast.137) | data formatting | bytes 7077888 | tf_op jit(solution)/shard_map/dot_general | solution.py:769
  134.8 3.2 fusion.25
  139.9 2.8 fusion.74
  142.8 2.7 convolution_convert_fusion.6
  147.2 1.9 fusion.61
  149.7 1.5 copy-done
  151.2 1.7 copy-done.68
  156.7 99.2 %head_all.1 = (f32[256,768]{1,0:T(8,128)}, bf16[2,2,768,512]{3,2,1,0:T(8,128)(2,1)}, f32[8,256]{1,0:T(8,128)}) custom-call(bf16[256,768]{1,0:T(8,128)(2,1)} %multiply_convert_fusion.4.refs_0_, f32[768,512]{1,0:T(8,128)} %refs_1_.3, s32[4,256,128]{2,1,0:T(8,128)} %broadcast_in_dim.15.refs_2_, f32[4,256]{1,0:T(4,128)} %gather_fusion.1), custom_call_target="tpu_custom_call" | custom-call | tf_op jit(solution)/shard_map/head_all/pallas_call | solution.py:204
  257.1 1.7 multiply_reduce_fusion.1
  259.0 4.5 %multiply_convert_fusion.2 = (bf16[256,2048]{1,0:T(8,128)(2,1)S(1)}, bf16[256,2048]{1,0:T(8,128)(2,1)S(1)}) fusion(f32[256,4096]{1,0:T(8,128)} %copy-done, bf16[2048,768]{1,0:T(8,128)(2,1)S(1)} %bitcast.159, f32[256,768]{1,0:T(8,128)S(1)} %subtract_multiply_fusion), kind=kOutput, calls=%fused_computation.17 | convolution fusion | flops 812318720 | bytes 10223616 | tf_op jit(solution)/shard_map/dot_general | solution.py:769
  263.7 2.0 multiply_reduce_fusion.2
  271.6 3.3 multiply_reduce_fusion
  279.4 1.7 copy-done.13
  285.6 1.3 slice_reduce_fusion.3
  287.0 2.0 fusion.48.refs_9_
  289.6 1.5 convolution_convert_fusion.3
  291.1 4.5 %convolution_convert_fusion.1 = bf16[768,2304]{1,0:T(8,128)(2,1)} fusion(bf16[256,2304]{0,1:T(8,128)(2,1)} %bitcast.136, f32[768]{0:T(1024)S(1)} %copy-done.45, f32[256]{0:T(256)S(1)} %copy-done.58, f32[255,768]{1,0:T(8,128)S(1)} %bitcast.121, f32[1,768]{1,0:T(1,128)S(1)} %copy-done.49), kind=kOutput, calls=%fused_computation.5 | convolution fusion | flops 908525568 | bytes 5509120 | tf_op jit(solution)/shard_map/dot_general | solution.py:769
  295.6 3.0 convolution_convert_fusion.2
  298.6 4.6 %convolution_convert_fusion = bf16[768,4096]{1,0:T(8,128)(2,1)} fusion(bf16[256,2048]{1,0:T(8,128)(2,1)S(1)} %copy-done.30, bf16[256,2048]{1,0:T(8,128)(2,1)S(1)} %copy-done.28, f32[256,768]{1,0:T(8,128)S(1)} %get-tuple-element.134, f32[768]{0:T(1024)S(1)} %copy-done.36, f32[256]{0:T(256)S(1)} %copy-done.54), kind=kOutput, calls=%fused_computation.4 | convolution fusion | flops 1618542592 | bytes 9179136 | tf_op jit(solution)/shard_map/dot_general | solution.py:769
  303.4 116.3 %scatter_all.1 = (f32[24,2304]{1,0:T(8,128)}, f32[24,768]{1,0:T(8,128)}, f32[24,4096]{1,0:T(8,128)}, f32[64,768]{1,0:T(8,128)}, f32[512,768]{1,0:T(8,128)}, /*in...) custom-call(bf16[4,2,2,2,24,2304]{5,4,3,2,1,0:T(8,128)(2,1)} %bitcast.124, bf16[4,2,2,2,24,768]{5,4,3,2,1,0:T(8,128)(2,1)} %bitcast.132, ...), custom_call_target="tpu_custom_call" | custom-call | tf_op jit(solution)/shard_map/scatter_all/pallas_call | solution.py:204
  421.6 1.4 fusion.72
  425.7 1.7 multiply_subtract_fusion.6
  427.4 2.1 multiply_subtract_fusion.5
  429.5 2.0 multiply_subtract_fusion.4
  431.5 2.0 multiply_subtract_fusion.3
  433.6 2.2 multiply_subtract_fusion.2
  435.8 3.0 multiply_subtract_fusion.1
  440.1 3.1 multiply_subtract_fusion
  (227 shorter events, 37.8 us)
Async XLA Ops:
  7.2 296.0 %reduce-scatter.4.cloned.1.call-start = ((), (), s32[]{:S(2)}) async-start(), calls=%async_computation.1 | async-start | bytes 3932160
  124.6 10.2 %copy-start.40 = (f32[4,256]{1,0:T(4,128)}, f32[4,256]{1,0:T(4,128)S(1)}, u32[]{:S(2)}) copy-start(f32[4,256]{1,0:T(4,128)S(1)} %fusion.47) | copy-start | bytes 12292
  126.5 19.0 %copy-start.48 = (f32[1,768]{1,0:T(1,128)}, f32[1,768]{1,0:T(1,128)S(1)}, u32[]{:S(2)}) copy-start(f32[1,768]{1,0:T(1,128)S(1)} %reshape_squeeze.3) | copy-start | bytes 9220
  126.7 27.3 %copy-start.51 = (f32[768]{0:T(1024)}, f32[768]{0:T(1024)S(1)}, u32[]{:S(2)}) copy-start(f32[768]{0:T(1024)S(1)} %mul.666) | copy-start | bytes 9220
  126.8 19.4 %copy-start.35 = (f32[768]{0:T(1024)}, f32[768]{0:T(1024)S(1)}, u32[]{:S(2)}) copy-start(f32[768]{0:T(1024)S(1)} %mul.658) | copy-start | bytes 9220
  126.9 8.0 %copy-start.44 = (f32[768]{0:T(1024)}, f32[768]{0:T(1024)S(1)}, u32[]{:S(2)}) copy-start(f32[768]{0:T(1024)S(1)} %mul.637) | copy-start | bytes 9220
  128.9 6.0 %copy-start.57 = (f32[256]{0:T(256)}, f32[256]{0:T(256)S(1)}, u32[]{:S(2)}) copy-start(f32[256]{0:T(256)S(1)} %add_rsqrt_fusion.2) | copy-start | bytes 3076
  258.8 4.9 %slice-start.2 = ((s8[6291456]{0:T(1024)(128)(4,1)}), s8[4194304]{0:T(1024)(128)(4,1)S(1)}, s32[]{:S(2)}) async-start(s8[6291456]{0:T(1024)(128)(4,1)} %bitcast.129), calls=%async_computation.4 | async-start | bytes 8388608
  259.0 6.7 %copy-start.4 = (f32[256,768]{1,0:T(8,128)}, f32[256,768]{1,0:T(8,128)S(1)}, u32[]{:S(2)}) copy-start(f32[256,768]{1,0:T(8,128)S(1)} %subtract_multiply_fusion) | copy-start | bytes 2359300
  259.0 4.6 %slice-start.3 = ((s8[6291456]{0:T(1024)(128)(4,1)}), s8[2097152]{0:T(1024)(128)(4,1)S(1)}, s32[]{:S(2)}) async-start(s8[6291456]{0:T(1024)(128)(4,1)} %bitcast.129), calls=%async_computation.5 | async-start | bytes 4194304
  259.0 4.6 %copy-start.36 = (f32[768]{0:T(1024)S(1)}, f32[768]{0:T(1024)}, u32[]{:S(2)}) copy-start(f32[768]{0:T(1024)} %copy-done.35) | copy-start | bytes 9220
  259.0 4.6 %copy-start.54 = (f32[256]{0:T(256)S(1)}, f32[256]{0:T(256)}, u32[]{:S(2)}) copy-start(f32[256]{0:T(256)} %copy-done.53) | copy-start | bytes 3076
  267.1 4.5 copy-start.60
  282.3 6.6 %copy-start.65 = (s32[32]{0:T(128)S(1)}, s32[32]{0:T(128)}, u32[]{:S(2)}) copy-start(s32[32]{0:T(128)} %eq.35) | copy-start | bytes 388
  291.1 4.5 %copy-start.3 = (bf16[256,2048]{1,0:T(8,128)(2,1)S(1)}, bf16[256,2048]{1,0:T(8,128)(2,1)}, u32[]{:S(2)}) copy-start(bf16[256,2048]{1,0:T(8,128)(2,1)} %copy-done.2) | copy-start | bytes 3145732
  291.1 4.5 %copy-start.5 = (f32[256,768]{1,0:T(8,128)S(1)}, f32[256,768]{1,0:T(8,128)}, u32[]{:S(2)}) copy-start(f32[256,768]{1,0:T(8,128)} %copy-done.4) | copy-start | bytes 2359300
  303.2 121.8 %copy-start.63 = (f32[3,24]{1,0:T(4,128)S(1)}, f32[3,24]{1,0:T(4,128)}, u32[]{:S(2)}) copy-start(f32[3,24]{1,0:T(4,128)} %refs_6_.1) | copy-start | bytes 868
  303.2 121.8 %copy-start.66 = (f32[3,24]{1,0:T(4,128)S(1)}, f32[3,24]{1,0:T(4,128)}, u32[]{:S(2)}) copy-start(f32[3,24]{1,0:T(4,128)} %param.47) | copy-start | bytes 868
  303.2 121.8 %copy-start.67 = (f32[3,24]{1,0:T(4,128)S(1)}, f32[3,24]{1,0:T(4,128)}, u32[]{:S(2)}) copy-start(f32[3,24]{1,0:T(4,128)} %param.55) | copy-start | bytes 868
  303.2 122.5 %copy-start.41 = (f32[24,768]{1,0:T(8,128)S(1)}, f32[24,768]{1,0:T(8,128)}, u32[]{:S(2)}) copy-start(f32[24,768]{1,0:T(8,128)} %refs_1_.2) | copy-start | bytes 221188
  303.3 124.2 %copy-start.50 = (f32[1001,24]{0,1:T(8,128)S(1)}, f32[1001,24]{0,1:T(8,128)}, u32[]{:S(2)}) copy-start(f32[1001,24]{0,1:T(8,128)} %param.32) | copy-start | bytes 288292
  303.3 126.3 %copy-start.32 = (f32[64,768]{1,0:T(8,128)S(1)}, f32[64,768]{1,0:T(8,128)}, u32[]{:S(2)}) copy-start(f32[64,768]{1,0:T(8,128)} %refs_3_.1) | copy-start | bytes 589828
  303.3 126.2 %copy-start.46 = (f32[64,768]{1,0:T(8,128)S(1)}, f32[64,768]{1,0:T(8,128)}, u32[]{:S(2)}) copy-start(f32[64,768]{1,0:T(8,128)} %param.45) | copy-start | bytes 589828
  303.3 126.2 %copy-start.47 = (f32[64,768]{1,0:T(8,128)S(1)}, f32[64,768]{1,0:T(8,128)}, u32[]{:S(2)}) copy-start(f32[64,768]{1,0:T(8,128)} %param.53) | copy-start | bytes 589828
  303.3 128.2 %copy-start.42 = (f32[24,2304]{1,0:T(8,128)S(1)}, f32[24,2304]{1,0:T(8,128)}, u32[]{:S(2)}) copy-start(f32[24,2304]{1,0:T(8,128)} %param.42) | copy-start | bytes 663556
  303.3 128.2 %copy-start.43 = (f32[24,2304]{1,0:T(8,128)S(1)}, f32[24,2304]{1,0:T(8,128)}, u32[]{:S(2)}) copy-start(f32[24,2304]{1,0:T(8,128)} %param.50) | copy-start | bytes 663556
  303.3 130.2 %copy-start.38 = (f32[24,4096]{1,0:T(8,128)S(1)}, f32[24,4096]{1,0:T(8,128)}, u32[]{:S(2)}) copy-start(f32[24,4096]{1,0:T(8,128)} %param.44) | copy-start | bytes 1179652
  303.3 130.2 %copy-start.39 = (f32[24,4096]{1,0:T(8,128)S(1)}, f32[24,4096]{1,0:T(8,128)}, u32[]{:S(2)}) copy-start(f32[24,4096]{1,0:T(8,128)} %param.52) | copy-start | bytes 1179652
  419.7 11.8 %copy-start.31 = (f32[24,2304]{1,0:T(8,128)S(1)}, f32[24,2304]{1,0:T(8,128)}, u32[]{:S(2)}) copy-start(f32[24,2304]{1,0:T(8,128)} %refs_0_.1) | copy-start | bytes 663556
  425.7 7.9 %copy-start.19 = (f32[24,4096]{1,0:T(8,128)S(1)}, f32[24,4096]{1,0:T(8,128)}, u32[]{:S(2)}) copy-start(f32[24,4096]{1,0:T(8,128)} %refs_2_.1) | copy-start | bytes 1179652
  427.4 8.3 %copy-start.22 = (f32[512,768]{1,0:T(8,128)S(1)}, f32[512,768]{1,0:T(8,128)}, u32[]{:S(2)}) copy-start(f32[512,768]{1,0:T(8,128)} %get-tuple-element.56) | copy-start | bytes 4718596
  429.5 6.2 %copy-start.21 = (f32[512,768]{1,0:T(8,128)S(1)}, f32[512,768]{1,0:T(8,128)}, u32[]{:S(2)}) copy-start(f32[512,768]{1,0:T(8,128)} %param.49) | copy-start | bytes 4718596
  (43 other events, 103.6 us)
Sparse Core Ops, SparseCore 0:
  256.1 42.1 reduce-scatter.3
